TPU v7x, 512 devices: a whole 4x4x16 slice. The times are simulated.
512 devices in a mesh: pt: 128 (over z, x, core), cen: 4 (over y).
Axes of the slice: x: 4, y: 4, z: 16, core: 2. Of those that a mesh axis runs over, the one named last changes fastest.
Arguments:
- points: bfloat16 [196608, 1024], P('pt'), may hold values from -8 to 8
- lengths: int32 [768], P('pt'), may hold values from 1 to 256, 147456 in all
- candidates: int32 [768, 16], P('pt'), may hold values from 0 to 255, as said below
- centroids: bfloat16 [256, 256, 1024], P('pt', 'cen'), may hold values from -6 to 6
Outputs:
- updated: bfloat16 [256, 256, 1024], P('pt', 'cen')
- masses: float32 [256, 256], P('pt', 'cen')
- log_partition: float32 [196608], P('pt')
Inputs may be any that keep to these rules, and one draw needn't show every extreme that they name: `candidates`: the 16 ids of a point block are different, and each names a centroid block held by a device of pt at most 4 positions away on either side, counted circularly, from the device of pt that holds the point block; block b is held by index b // 2 of pt.
All inputs are finite; a program needn't handle non-finite values. No bound on the sum of `lengths` on one device may be relied on, other than what follows from the above.
Results may differ from a plain program's by a relative error of at most 0.005.
Values may be sent and summed in bfloat16 or wider, within the bound.
No kernel may reach another device: no remote copies, remote signals or barrier semaphores. Data moves between devices by JAX's collectives and lax.ppermute only.
A program may use at most 64 MiB of HBM per device.

v0:
```python
import math

import jax
import jax.numpy as jnp
from jax import lax
from jax.sharding import PartitionSpec as P

D = 1024
REACH = 4


sharpness_factor = 1.5
prior_mass = 1.0


def passed_along(value, axis, steps):
    count = lax.axis_size(axis)
    pairs = [(source, (source + steps) % count) for source in range(count)]
    return lax.ppermute(value, axis, pairs)


def shortened(value):

    def short(part):
        return part.astype(jnp.bfloat16) if part.dtype == jnp.float32 else part

    return jax.tree.map(short, value)


def pair_sum(first_pair, second_pair):
    return (first_pair[0] + second_pair[0], first_pair[1] + second_pair[1])


def local(points, lengths, candidates, centroids):
    pt_count = lax.axis_size("pt")
    pt_index = lax.axis_index("pt")
    local_blocks, centre_rows, feature_vectors = centroids.shape
    blocks_here = lengths.shape[0]
    block_len = points.shape[0] // blocks_here
    span_count = min(2 * REACH + 1, pt_count)
    pieces = []
    for window_slot in range(span_count):
        offset = window_slot - REACH
        if offset == 0:
            pieces.append(centroids)
        else:
            pieces.append(passed_along(centroids, "pt", -offset))
    window = jnp.concatenate(pieces, 0)
    squares = jnp.sum(jnp.square(window.astype(jnp.float32)), -1)
    owner_dev = candidates // local_blocks
    position = (owner_dev - pt_index + REACH) % pt_count * local_blocks + candidates % local_blocks
    sharpness = sharpness_factor * math.sqrt(D)
    point_blocks = points.reshape(blocks_here, block_len, feature_vectors)

    def score_block(inputs):
        sample_rows, slots_of = inputs
        gathered = window[slots_of].reshape(-1, feature_vectors)
        products = lax.dot_general(
            sample_rows, gathered, (((1,), (1,)), ((), ())), preferred_element_type=jnp.float32
        )
        return (2.0 * products - squares[slots_of].reshape(1, -1)) * sharpness

    logits = lax.map(score_block, (point_blocks, position))
    local_max = jnp.max(logits, -1)
    row_max = lax.pmax(local_max, "cen")
    row_sum = lax.psum(jnp.sum(jnp.exp(logits - row_max[..., None]), -1), "cen")
    log_partition = (row_max + jnp.log(row_sum)).reshape(-1)
    live_mask = (jnp.arange(block_len, dtype=jnp.int32)[None, :] < lengths[:, None]).astype(
        jnp.float32
    )
    weights = (
        jnp.exp(logits - row_max[..., None]) / row_sum[..., None] * live_mask[..., None]
    ).astype(jnp.bfloat16)

    def gather_stats(running, inputs):
        moments, masses = running
        sample_rows, slots_of, block_weights = inputs
        reshaped_input = block_weights.reshape(block_len, -1, centre_rows)
        weighted_features = jnp.einsum(
            "ixn,io->xno", reshaped_input, sample_rows, preferred_element_type=jnp.float32
        )
        moments = moments.at[slots_of].add(weighted_features)
        masses = masses.at[slots_of].add(jnp.sum(reshaped_input.astype(jnp.float32), 0))
        return ((moments, masses), None)

    initial = (
        jnp.zeros((span_count * local_blocks, centre_rows, feature_vectors), jnp.float32),
        jnp.zeros((span_count * local_blocks, centre_rows), jnp.float32),
    )
    (moments, masses), unused = lax.scan(gather_stats, initial, (point_blocks, position, weights))
    outgoing = [
        (
            moments[k * local_blocks : (k + 1) * local_blocks],
            masses[k * local_blocks : (k + 1) * local_blocks],
        )
        for k in range(span_count)
    ]
    home_pair = outgoing[REACH]
    for window_slot in range(span_count):
        offset = window_slot - REACH
        if offset != 0:
            arrived = passed_along(shortened(outgoing[window_slot]), "pt", offset)
            home_pair = pair_sum(home_pair, arrived)
    home_moments, home_masses = home_pair
    updated = (
        (home_moments + prior_mass * centroids.astype(jnp.float32))
        / (home_masses + prior_mass)[..., None]
    ).astype(jnp.bfloat16)
    return (updated, home_masses, log_partition)


def solution(mesh):
    return jax.shard_map(
        local,
        mesh=mesh,
        in_specs=(P("pt", None), P("pt"), P("pt", None), P("pt", "cen", None)),
        out_specs=(P("pt", "cen", None), P("pt", "cen"), P("pt")),
        check_vma=False,
    )
```

profile of v0, /device:TPU:1, one launch (start us, length us, event | category | flops | bytes accessed | tf_op | source)
XLA Modules:
  0.0 291.6 jit_solution(2045138497681839117)
XLA Ops:
  0.6 5.5 %collective-permute-start = (bf16[2,64,1024]{2,1,0:T(8,128)(2,1)}, bf16[2,64,1024]{2,1,0:T(8,128)(2,1)S(1)}, u32[]{:S(2)}, u32[]{:S(2)}) collective-permute-start(bf16[2,64,1024]{2,1,0:T(8,128)(2,1)} %param.11), channel_id=1, source_target_pairs={{0,16},{4,20},{8,24},{12,28},{16,32},{20,36},{24,40},{28,44},{32,4... | collective-permute-start | bytes 786440 | tf_op jit(solution)/shard_map/ppermute | solution.py:19
  6.1 4.3 %collective-permute-start.1 = (bf16[2,64,1024]{2,1,0:T(8,128)(2,1)}, bf16[2,64,1024]{2,1,0:T(8,128)(2,1)S(1)}, u32[]{:S(2)}, u32[]{:S(2)}) collective-permute-start(bf16[2,64,1024]{2,1,0:T(8,128)(2,1)} %param.11), channel_id=1, source_target_pairs={{0,12},{4,16},{8,20},{12,24},{16,28},{20,32},{24,36},{28,40},{32,4... | collective-permute-start | bytes 786440 | tf_op jit(solution)/shard_map/ppermute | solution.py:19
  22.0 5.2 %collective-permute-start.5 = (bf16[2,64,1024]{2,1,0:T(8,128)(2,1)}, bf16[2,64,1024]{2,1,0:T(8,128)(2,1)S(1)}, u32[]{:S(2)}, u32[]{:S(2)}) collective-permute-start(bf16[2,64,1024]{2,1,0:T(8,128)(2,1)} %param.11), channel_id=1, source_target_pairs={{0,504},{4,508},{8,0},{12,4},{16,8},{20,12},{24,16},{28,20},{32,24... | collective-permute-start | bytes 786440 | tf_op jit(solution)/shard_map/ppermute | solution.py:19
  28.4 5.4 %collective-permute-start.6 = (bf16[2,64,1024]{2,1,0:T(8,128)(2,1)}, bf16[2,64,1024]{2,1,0:T(8,128)(2,1)S(1)}, u32[]{:S(2)}, u32[]{:S(2)}) collective-permute-start(bf16[2,64,1024]{2,1,0:T(8,128)(2,1)} %param.11), channel_id=1, source_target_pairs={{0,500},{4,504},{8,508},{12,0},{16,4},{20,8},{24,12},{28,16},{32,2... | collective-permute-start | bytes 786440 | tf_op jit(solution)/shard_map/ppermute | solution.py:19
  33.8 6.7 %collective-permute-start.7 = (bf16[2,64,1024]{2,1,0:T(8,128)(2,1)}, bf16[2,64,1024]{2,1,0:T(8,128)(2,1)S(1)}, u32[]{:S(2)}, u32[]{:S(2)}) collective-permute-start(bf16[2,64,1024]{2,1,0:T(8,128)(2,1)} %param.11), channel_id=1, source_target_pairs={{0,496},{4,500},{8,504},{12,508},{16,0},{20,4},{24,8},{28,12},{32,... | collective-permute-start | bytes 786440 | tf_op jit(solution)/shard_map/ppermute | solution.py:19
  46.1 37.1 %while.22 = (s32[]{:T(128)}, f32[6,256,1024]{2,1,0:T(8,128)}, bf16[6,256,1024]{2,1,0:T(8,128)(2,1)}, s32[6,16]{1,0:T(8,128)S(1)}, bf16[18,64,1024]{2,1,0:T(8,128)(2,1)S(1)}, /*index=5*/f32[18,64]{1,0:T(8,128)S(1)}, s32[]{:T(128)}) while((s32[]{:T(128)}, f32[6,256,1024]{2,1,0:T(8,128)}, bf16[6,256,1024]{2,1,0:T(8,128)(2,1)}, ...), condition=%wide.region_2.3_spmd, body=%wide.region_1.2_spmd.sunk | while | flops 537658432 | bytes 7890321 | solution.py:63
  83.3 6.5 %copy.7 = f32[6,256,1024]{1,2,0:T(8,128)} copy(f32[6,256,1024]{2,1,0:T(8,128)} %get-tuple-element.68) | data formatting | bytes 12582912 | tf_op jit(solution)/shard_map/while | solution.py:63
  92.9 8.8 %pmax.7 = f32[6,256]{1,0:T(8,128)S(1)} all-reduce(f32[6,256]{1,0:T(8,128)S(1)} %reduce_max.9), channel_id=1, replica_groups=mesh['pt'=128,'cen'=4] {'cen'}, use_global_device_ids=true, to_apply=%region_4.5 | all-reduce | flops 1536 | bytes 12288 | tf_op jit(solution)/shard_map/pmax | solution.py:65
  105.4 6.1 %psum.7 = f32[6,256]{1,0:T(8,128)S(1)} all-reduce(f32[6,256]{1,0:T(8,128)S(1)} %fusion.15), channel_id=1, replica_groups=mesh['pt'=128,'cen'=4] {'cen'}, use_global_device_ids=true, to_apply=%region_6.7 | all-reduce | flops 1536 | bytes 12288 | tf_op jit(solution)/shard_map/psum | solution.py:66
  118.1 86.7 %while.23 = (s32[]{:T(128)}, f32[18,64,1024]{2,1,0:T(8,128)}, f32[18,64]{1,0:T(8,128)S(1)}, s32[6,16]{1,0:T(8,128)S(1)}, bf16[6,256,1024]{1,2,0:T(8,128)(2,1)S(1)}, /*index=5*/bf16[6,256,1024]{2,1,0:T(8,128)(2,1)}, s32[]{:T(128)}) while((s32[]{:T(128)}, f32[18,64,1024]{2,1,0:T(8,128)}, f32[18,64]{1,0:T(8,128)S(1)}, s32[6,16]{1,0:T(8,128)S(1)}, ...), condition=%wide.region_11.12_spmd, body=%wide.region_7.11_spmd.sunk | while | flops 538443840 | bytes 18899796 | solution.py:90
  122.2 9.7 %scatter_fusion = f32[18,64,1024]{2,1,0:T(8,128)} fusion(f32[18,64,1024]{2,1,0:T(8,128)} %get-tuple-element.222, s32[16]{0:T(128)S(1)} %fusion.41, f32[16,64,1024]{2,1,0:T(8,128)} %fusion.42), kind=kCustom, calls=%fused_computation.2.clone.1 | custom fusion | flops 1048576 | bytes 12582976 | tf_op jit(solution)/shard_map/while/body/eval_jaxpr/scatter-add | solution.py:82
  136.6 9.7 %scatter_fusion = f32[18,64,1024]{2,1,0:T(8,128)} fusion(f32[18,64,1024]{2,1,0:T(8,128)} %get-tuple-element.222, s32[16]{0:T(128)S(1)} %fusion.41, f32[16,64,1024]{2,1,0:T(8,128)} %fusion.42), kind=kCustom, calls=%fused_computation.2.clone.1 | custom fusion | flops 1048576 | bytes 12582976 | tf_op jit(solution)/shard_map/while/body/eval_jaxpr/scatter-add | solution.py:82
  151.0 9.7 %scatter_fusion = f32[18,64,1024]{2,1,0:T(8,128)} fusion(f32[18,64,1024]{2,1,0:T(8,128)} %get-tuple-element.222, s32[16]{0:T(128)S(1)} %fusion.41, f32[16,64,1024]{2,1,0:T(8,128)} %fusion.42), kind=kCustom, calls=%fused_computation.2.clone.1 | custom fusion | flops 1048576 | bytes 12582976 | tf_op jit(solution)/shard_map/while/body/eval_jaxpr/scatter-add | solution.py:82
  165.5 9.6 %scatter_fusion = f32[18,64,1024]{2,1,0:T(8,128)} fusion(f32[18,64,1024]{2,1,0:T(8,128)} %get-tuple-element.222, s32[16]{0:T(128)S(1)} %fusion.41, f32[16,64,1024]{2,1,0:T(8,128)} %fusion.42), kind=kCustom, calls=%fused_computation.2.clone.1 | custom fusion | flops 1048576 | bytes 12582976 | tf_op jit(solution)/shard_map/while/body/eval_jaxpr/scatter-add | solution.py:82
  179.9 9.8 %scatter_fusion = f32[18,64,1024]{2,1,0:T(8,128)} fusion(f32[18,64,1024]{2,1,0:T(8,128)} %get-tuple-element.222, s32[16]{0:T(128)S(1)} %fusion.41, f32[16,64,1024]{2,1,0:T(8,128)} %fusion.42), kind=kCustom, calls=%fused_computation.2.clone.1 | custom fusion | flops 1048576 | bytes 12582976 | tf_op jit(solution)/shard_map/while/body/eval_jaxpr/scatter-add | solution.py:82
  194.4 9.7 %scatter_fusion = f32[18,64,1024]{2,1,0:T(8,128)} fusion(f32[18,64,1024]{2,1,0:T(8,128)} %get-tuple-element.222, s32[16]{0:T(128)S(1)} %fusion.41, f32[16,64,1024]{2,1,0:T(8,128)} %fusion.42), kind=kCustom, calls=%fused_computation.2.clone.1 | custom fusion | flops 1048576 | bytes 12582976 | tf_op jit(solution)/shard_map/while/body/eval_jaxpr/scatter-add | solution.py:82
  207.8 5.4 %collective-permute-start.10 = (bf16[2,64,1024]{2,1,0:T(8,128)(2,1)S(1)}, bf16[2,64,1024]{2,1,0:T(8,128)(2,1)S(1)}, u32[]{:S(2)}, u32[]{:S(2)}) collective-permute-start(bf16[2,64,1024]{2,1,0:T(8,128)(2,1)S(1)} %get-tuple-element.105), channel_id=1, source_target_pairs={{0,504},{4,508},{8,0},{12,4},{16,8},{20,12},{24,16},{28,20},{32,24... | collective-permute-start | bytes 786440 | tf_op jit(solution)/shard_map/ppermute | solution.py:19
  213.3 8.3 %collective-permute-start.11 = (bf16[2,64,1024]{2,1,0:T(8,128)(2,1)S(1)}, bf16[2,64,1024]{2,1,0:T(8,128)(2,1)S(1)}, u32[]{:S(2)}, u32[]{:S(2)}) collective-permute-start(bf16[2,64,1024]{2,1,0:T(8,128)(2,1)S(1)} %get-tuple-element.104), channel_id=1, source_target_pairs={{0,508},{4,0},{8,4},{12,8},{16,12},{20,16},{24,20},{28,24},{32,28}... | collective-permute-start | bytes 786440 | tf_op jit(solution)/shard_map/ppermute | solution.py:19
  223.5 4.8 %collective-permute-start.16 = (bf16[2,64]{1,0:T(2,128)(2,1)S(1)}, bf16[2,64]{1,0:T(2,128)(2,1)S(1)}, u32[]{:S(2)}, u32[]{:S(2)}) collective-permute-start(bf16[2,64]{1,0:T(2,128)(2,1)S(1)} %get-tuple-element.107), channel_id=1, source_target_pairs={{0,496},{4,500},{8,504},{12,508},{16,0},{20,4},{24,8},{28,12},{32,... | collective-permute-start | bytes 776 | tf_op jit(solution)/shard_map/ppermute | solution.py:19
  230.5 7.5 %collective-permute-start.18 = (bf16[2,64]{1,0:T(2,128)(2,1)S(1)}, bf16[2,64]{1,0:T(2,128)(2,1)S(1)}, u32[]{:S(2)}, u32[]{:S(2)}) collective-permute-start(bf16[2,64]{1,0:T(2,128)(2,1)S(1)} %get-tuple-element.113), channel_id=1, source_target_pairs={{0,504},{4,508},{8,0},{12,4},{16,8},{20,12},{24,16},{28,20},{32,24... | collective-permute-start | bytes 776 | tf_op jit(solution)/shard_map/ppermute | solution.py:19
  245.6 4.5 %collective-permute-start.22 = (bf16[2,64]{1,0:T(2,128)(2,1)S(1)}, bf16[2,64]{1,0:T(2,128)(2,1)S(1)}, u32[]{:S(2)}, u32[]{:S(2)}) collective-permute-start(bf16[2,64]{1,0:T(2,128)(2,1)S(1)} %get-tuple-element.109), channel_id=1, source_target_pairs={{0,12},{4,16},{8,20},{12,24},{16,28},{20,32},{24,36},{28,40},{32,4... | collective-permute-start | bytes 776 | tf_op jit(solution)/shard_map/ppermute | solution.py:19
  265.0 6.7 %collective-permute-start.8 = (bf16[2,64,1024]{2,1,0:T(8,128)(2,1)S(1)}, bf16[2,64,1024]{2,1,0:T(8,128)(2,1)S(1)}, u32[]{:S(2)}, u32[]{:S(2)}) collective-permute-start(bf16[2,64,1024]{2,1,0:T(8,128)(2,1)S(1)} %get-tuple-element.99), channel_id=1, source_target_pairs={{0,496},{4,500},{8,504},{12,508},{16,0},{20,4},{24,8},{28,12},{32,... | collective-permute-start | bytes 786440 | tf_op jit(solution)/shard_map/ppermute | solution.py:19
  271.7 4.0 %collective-permute-start.9 = (bf16[2,64,1024]{2,1,0:T(8,128)(2,1)S(1)}, bf16[2,64,1024]{2,1,0:T(8,128)(2,1)S(1)}, u32[]{:S(2)}, u32[]{:S(2)}) collective-permute-start(bf16[2,64,1024]{2,1,0:T(8,128)(2,1)S(1)} %get-tuple-element.106), channel_id=1, source_target_pairs={{0,500},{4,504},{8,508},{12,0},{16,4},{20,8},{24,12},{28,16},{32,2... | collective-permute-start | bytes 786440 | tf_op jit(solution)/shard_map/ppermute | solution.py:19
  281.2 5.5 %collective-permute-done.8 = bf16[2,64,1024]{2,1,0:T(8,128)(2,1)S(1)} collective-permute-done((bf16[2,64,1024]{2,1,0:T(8,128)(2,1)S(1)}, bf16[2,64,1024]{2,1,0:T(8,128)(2,1)S(1)}, u32[]{:S(2)}, u32[]{:S(2)}) %collective-permute-start.8) | collective-permute-done | bytes 262176 | tf_op jit(solution)/shard_map/ppermute | solution.py:19
  (131 shorter events, 136.8 us)
Async XLA Ops:
  0.6 20.7 %collective-permute-start = (bf16[2,64,1024]{2,1,0:T(8,128)(2,1)}, bf16[2,64,1024]{2,1,0:T(8,128)(2,1)S(1)}, u32[]{:S(2)}, u32[]{:S(2)}) collective-permute-start(bf16[2,64,1024]{2,1,0:T(8,128)(2,1)} %param.11), channel_id=1, source_target_pairs={{0,16},{4,20},{8,24},{12,28},{16,32},{20,36},{24,40},{28,44},{32,4... | collective-permute-start | bytes 786440 | tf_op jit(solution)/shard_map/ppermute | solution.py:19
  6.1 22.2 %collective-permute-start.1 = (bf16[2,64,1024]{2,1,0:T(8,128)(2,1)}, bf16[2,64,1024]{2,1,0:T(8,128)(2,1)S(1)}, u32[]{:S(2)}, u32[]{:S(2)}) collective-permute-start(bf16[2,64,1024]{2,1,0:T(8,128)(2,1)} %param.11), channel_id=1, source_target_pairs={{0,12},{4,16},{8,20},{12,24},{16,28},{20,32},{24,36},{28,40},{32,4... | collective-permute-start | bytes 786440 | tf_op jit(solution)/shard_map/ppermute | solution.py:19
  10.5 23.4 %collective-permute-start.2 = (bf16[2,64,1024]{2,1,0:T(8,128)(2,1)}, bf16[2,64,1024]{2,1,0:T(8,128)(2,1)S(1)}, u32[]{:S(2)}, u32[]{:S(2)}) collective-permute-start(bf16[2,64,1024]{2,1,0:T(8,128)(2,1)} %param.11), channel_id=1, source_target_pairs={{0,8},{4,12},{8,16},{12,20},{16,24},{20,28},{24,32},{28,36},{32,40... | collective-permute-start | bytes 786440 | tf_op jit(solution)/shard_map/ppermute | solution.py:19
  13.6 26.9 %collective-permute-start.3 = (bf16[2,64,1024]{2,1,0:T(8,128)(2,1)}, bf16[2,64,1024]{2,1,0:T(8,128)(2,1)S(1)}, u32[]{:S(2)}, u32[]{:S(2)}) collective-permute-start(bf16[2,64,1024]{2,1,0:T(8,128)(2,1)} %param.11), channel_id=1, source_target_pairs={{0,4},{4,8},{8,12},{12,16},{16,20},{20,24},{24,28},{28,32},{32,36}... | collective-permute-start | bytes 786440 | tf_op jit(solution)/shard_map/ppermute | solution.py:19
  15.5 26.0 %collective-permute-start.4 = (bf16[2,64,1024]{2,1,0:T(8,128)(2,1)}, bf16[2,64,1024]{2,1,0:T(8,128)(2,1)S(1)}, u32[]{:S(2)}, u32[]{:S(2)}) collective-permute-start(bf16[2,64,1024]{2,1,0:T(8,128)(2,1)} %param.11), channel_id=1, source_target_pairs={{0,508},{4,0},{8,4},{12,8},{16,12},{20,16},{24,20},{28,24},{32,28}... | collective-permute-start | bytes 786440 | tf_op jit(solution)/shard_map/ppermute | solution.py:19
  22.0 19.5 %collective-permute-start.5 = (bf16[2,64,1024]{2,1,0:T(8,128)(2,1)}, bf16[2,64,1024]{2,1,0:T(8,128)(2,1)S(1)}, u32[]{:S(2)}, u32[]{:S(2)}) collective-permute-start(bf16[2,64,1024]{2,1,0:T(8,128)(2,1)} %param.11), channel_id=1, source_target_pairs={{0,504},{4,508},{8,0},{12,4},{16,8},{20,12},{24,16},{28,20},{32,24... | collective-permute-start | bytes 786440 | tf_op jit(solution)/shard_map/ppermute | solution.py:19
  28.4 13.2 %collective-permute-start.6 = (bf16[2,64,1024]{2,1,0:T(8,128)(2,1)}, bf16[2,64,1024]{2,1,0:T(8,128)(2,1)S(1)}, u32[]{:S(2)}, u32[]{:S(2)}) collective-permute-start(bf16[2,64,1024]{2,1,0:T(8,128)(2,1)} %param.11), channel_id=1, source_target_pairs={{0,500},{4,504},{8,508},{12,0},{16,4},{20,8},{24,12},{28,16},{32,2... | collective-permute-start | bytes 786440 | tf_op jit(solution)/shard_map/ppermute | solution.py:19
  33.8 11.7 %collective-permute-start.7 = (bf16[2,64,1024]{2,1,0:T(8,128)(2,1)}, bf16[2,64,1024]{2,1,0:T(8,128)(2,1)S(1)}, u32[]{:S(2)}, u32[]{:S(2)}) collective-permute-start(bf16[2,64,1024]{2,1,0:T(8,128)(2,1)} %param.11), channel_id=1, source_target_pairs={{0,496},{4,500},{8,504},{12,508},{16,0},{20,4},{24,8},{28,12},{32,... | collective-permute-start | bytes 786440 | tf_op jit(solution)/shard_map/ppermute | solution.py:19
  207.8 53.2 %collective-permute-start.10 = (bf16[2,64,1024]{2,1,0:T(8,128)(2,1)S(1)}, bf16[2,64,1024]{2,1,0:T(8,128)(2,1)S(1)}, u32[]{:S(2)}, u32[]{:S(2)}) collective-permute-start(bf16[2,64,1024]{2,1,0:T(8,128)(2,1)S(1)} %get-tuple-element.105), channel_id=1, source_target_pairs={{0,504},{4,508},{8,0},{12,4},{16,8},{20,12},{24,16},{28,20},{32,24... | collective-permute-start | bytes 786440 | tf_op jit(solution)/shard_map/ppermute | solution.py:19
  213.3 51.7 %collective-permute-start.11 = (bf16[2,64,1024]{2,1,0:T(8,128)(2,1)S(1)}, bf16[2,64,1024]{2,1,0:T(8,128)(2,1)S(1)}, u32[]{:S(2)}, u32[]{:S(2)}) collective-permute-start(bf16[2,64,1024]{2,1,0:T(8,128)(2,1)S(1)} %get-tuple-element.104), channel_id=1, source_target_pairs={{0,508},{4,0},{8,4},{12,8},{16,12},{20,16},{24,20},{28,24},{32,28}... | collective-permute-start | bytes 786440 | tf_op jit(solution)/shard_map/ppermute | solution.py:19
  221.6 50.1 %collective-permute-start.12 = (bf16[2,64,1024]{2,1,0:T(8,128)(2,1)S(1)}, bf16[2,64,1024]{2,1,0:T(8,128)(2,1)S(1)}, u32[]{:S(2)}, u32[]{:S(2)}) collective-permute-start(bf16[2,64,1024]{2,1,0:T(8,128)(2,1)S(1)} %get-tuple-element.103), channel_id=1, source_target_pairs={{0,4},{4,8},{8,12},{12,16},{16,20},{20,24},{24,28},{28,32},{32,36}... | collective-permute-start | bytes 786440 | tf_op jit(solution)/shard_map/ppermute | solution.py:19
  223.5 7.0 %collective-permute-start.16 = (bf16[2,64]{1,0:T(2,128)(2,1)S(1)}, bf16[2,64]{1,0:T(2,128)(2,1)S(1)}, u32[]{:S(2)}, u32[]{:S(2)}) collective-permute-start(bf16[2,64]{1,0:T(2,128)(2,1)S(1)} %get-tuple-element.107), channel_id=1, source_target_pairs={{0,496},{4,500},{8,504},{12,508},{16,0},{20,4},{24,8},{28,12},{32,... | collective-permute-start | bytes 776 | tf_op jit(solution)/shard_map/ppermute | solution.py:19
  228.3 9.7 %collective-permute-start.17 = (bf16[2,64]{1,0:T(2,128)(2,1)S(1)}, bf16[2,64]{1,0:T(2,128)(2,1)S(1)}, u32[]{:S(2)}, u32[]{:S(2)}) collective-permute-start(bf16[2,64]{1,0:T(2,128)(2,1)S(1)} %get-tuple-element.114), channel_id=1, source_target_pairs={{0,500},{4,504},{8,508},{12,0},{16,4},{20,8},{24,12},{28,16},{32,2... | collective-permute-start | bytes 776 | tf_op jit(solution)/shard_map/ppermute | solution.py:19
  230.5 10.2 %collective-permute-start.18 = (bf16[2,64]{1,0:T(2,128)(2,1)S(1)}, bf16[2,64]{1,0:T(2,128)(2,1)S(1)}, u32[]{:S(2)}, u32[]{:S(2)}) collective-permute-start(bf16[2,64]{1,0:T(2,128)(2,1)S(1)} %get-tuple-element.113), channel_id=1, source_target_pairs={{0,504},{4,508},{8,0},{12,4},{16,8},{20,12},{24,16},{28,20},{32,24... | collective-permute-start | bytes 776 | tf_op jit(solution)/shard_map/ppermute | solution.py:19
  238.0 5.6 %collective-permute-start.19 = (bf16[2,64]{1,0:T(2,128)(2,1)S(1)}, bf16[2,64]{1,0:T(2,128)(2,1)S(1)}, u32[]{:S(2)}, u32[]{:S(2)}) collective-permute-start(bf16[2,64]{1,0:T(2,128)(2,1)S(1)} %get-tuple-element.112), channel_id=1, source_target_pairs={{0,508},{4,0},{8,4},{12,8},{16,12},{20,16},{24,20},{28,24},{32,28}... | collective-permute-start | bytes 776 | tf_op jit(solution)/shard_map/ppermute | solution.py:19
  240.7 4.8 %collective-permute-start.20 = (bf16[2,64]{1,0:T(2,128)(2,1)S(1)}, bf16[2,64]{1,0:T(2,128)(2,1)S(1)}, u32[]{:S(2)}, u32[]{:S(2)}) collective-permute-start(bf16[2,64]{1,0:T(2,128)(2,1)S(1)} %get-tuple-element.111), channel_id=1, source_target_pairs={{0,4},{4,8},{8,12},{12,16},{16,20},{20,24},{24,28},{28,32},{32,36}... | collective-permute-start | bytes 776 | tf_op jit(solution)/shard_map/ppermute | solution.py:19
  243.6 7.6 %collective-permute-start.21 = (bf16[2,64]{1,0:T(2,128)(2,1)S(1)}, bf16[2,64]{1,0:T(2,128)(2,1)S(1)}, u32[]{:S(2)}, u32[]{:S(2)}) collective-permute-start(bf16[2,64]{1,0:T(2,128)(2,1)S(1)} %get-tuple-element.110), channel_id=1, source_target_pairs={{0,8},{4,12},{8,16},{12,20},{16,24},{20,28},{24,32},{28,36},{32,40... | collective-permute-start | bytes 776 | tf_op jit(solution)/shard_map/ppermute | solution.py:19
  245.6 8.6 %collective-permute-start.22 = (bf16[2,64]{1,0:T(2,128)(2,1)S(1)}, bf16[2,64]{1,0:T(2,128)(2,1)S(1)}, u32[]{:S(2)}, u32[]{:S(2)}) collective-permute-start(bf16[2,64]{1,0:T(2,128)(2,1)S(1)} %get-tuple-element.109), channel_id=1, source_target_pairs={{0,12},{4,16},{8,20},{12,24},{16,28},{20,32},{24,36},{28,40},{32,4... | collective-permute-start | bytes 776 | tf_op jit(solution)/shard_map/ppermute | solution.py:19
  251.2 7.9 %collective-permute-start.23 = (bf16[2,64]{1,0:T(2,128)(2,1)S(1)}, bf16[2,64]{1,0:T(2,128)(2,1)S(1)}, u32[]{:S(2)}, u32[]{:S(2)}) collective-permute-start(bf16[2,64]{1,0:T(2,128)(2,1)S(1)} %get-tuple-element.108), channel_id=1, source_target_pairs={{0,16},{4,20},{8,24},{12,28},{16,32},{20,36},{24,40},{28,44},{32,4... | collective-permute-start | bytes 776 | tf_op jit(solution)/shard_map/ppermute | solution.py:19
  254.1 22.7 %collective-permute-start.13 = (bf16[2,64,1024]{2,1,0:T(8,128)(2,1)S(1)}, bf16[2,64,1024]{2,1,0:T(8,128)(2,1)S(1)}, u32[]{:S(2)}, u32[]{:S(2)}) collective-permute-start(bf16[2,64,1024]{2,1,0:T(8,128)(2,1)S(1)} %get-tuple-element.102), channel_id=1, source_target_pairs={{0,8},{4,12},{8,16},{12,20},{16,24},{20,28},{24,32},{28,36},{32,40... | collective-permute-start | bytes 786440 | tf_op jit(solution)/shard_map/ppermute | solution.py:19
  259.1 18.9 %collective-permute-start.14 = (bf16[2,64,1024]{2,1,0:T(8,128)(2,1)S(1)}, bf16[2,64,1024]{2,1,0:T(8,128)(2,1)}, u32[]{:S(2)}, u32[]{:S(2)}) collective-permute-start(bf16[2,64,1024]{2,1,0:T(8,128)(2,1)S(1)} %get-tuple-element.101), channel_id=1, source_target_pairs={{0,12},{4,16},{8,20},{12,24},{16,28},{20,32},{24,36},{28,40},{32,4... | collective-permute-start | bytes 786440 | tf_op jit(solution)/shard_map/ppermute | solution.py:19
  261.1 20.2 %collective-permute-start.15 = (bf16[2,64,1024]{2,1,0:T(8,128)(2,1)S(1)}, bf16[2,64,1024]{2,1,0:T(8,128)(2,1)S(1)}, u32[]{:S(2)}, u32[]{:S(2)}) collective-permute-start(bf16[2,64,1024]{2,1,0:T(8,128)(2,1)S(1)} %get-tuple-element.100), channel_id=1, source_target_pairs={{0,16},{4,20},{8,24},{12,28},{16,32},{20,36},{24,40},{28,44},{32,4... | collective-permute-start | bytes 786440 | tf_op jit(solution)/shard_map/ppermute | solution.py:19
  265.0 21.8 %collective-permute-start.8 = (bf16[2,64,1024]{2,1,0:T(8,128)(2,1)S(1)}, bf16[2,64,1024]{2,1,0:T(8,128)(2,1)S(1)}, u32[]{:S(2)}, u32[]{:S(2)}) collective-permute-start(bf16[2,64,1024]{2,1,0:T(8,128)(2,1)S(1)} %get-tuple-element.99), channel_id=1, source_target_pairs={{0,496},{4,500},{8,504},{12,508},{16,0},{20,4},{24,8},{28,12},{32,... | collective-permute-start | bytes 786440 | tf_op jit(solution)/shard_map/ppermute | solution.py:19
  271.7 17.6 %collective-permute-start.9 = (bf16[2,64,1024]{2,1,0:T(8,128)(2,1)S(1)}, bf16[2,64,1024]{2,1,0:T(8,128)(2,1)S(1)}, u32[]{:S(2)}, u32[]{:S(2)}) collective-permute-start(bf16[2,64,1024]{2,1,0:T(8,128)(2,1)S(1)} %get-tuple-element.106), channel_id=1, source_target_pairs={{0,500},{4,504},{8,508},{12,0},{16,4},{20,8},{24,12},{28,16},{32,2... | collective-permute-start | bytes 786440 | tf_op jit(solution)/shard_map/ppermute | solution.py:19
  (2 other events, 82.5 us)
where the time goes:
time: 295 us; the launch traced here: 292 us
  starting transfers between devices  97.9 us (33%)
  other arithmetic  81.6 us (28%)
  matrix products  43.7 us (15%)
  local copies, waits for them, and re-layouts  29.3 us (10%)
  waiting for transfers between devices  22.8 us (8%)
  blocking collectives  14.9 us (5%)
    ppermute x24, starting transfers between devices, passed_along(): return lax.ppermute(value, axis, pairs)  97.9 us
    scatter-add x6, other arithmetic, gather_stats(): moments = moments.at[slots_of].add(weighted_features)  58.2 us
    ppermute x24, waiting for transfers between devices, passed_along(): return lax.ppermute(value, axis, pairs)  22.8 us
    dot_general x6, matrix products, gather_stats(): jnp.einsum('ixn,io->xno', reshaped_input, sample_rows, preferred_element_...  22.7 us
    dot_general x6, matrix products, score_block(): lax.dot_general(sample_rows, gathered, (((1,), (1,)), ((), ())), preferre...  21 us
    gather x6, local copies, waits for them, and re-layouts, score_block(): gathered = window[slots_of].reshape(-1, feature_vectors)  12.2 us
    pmax x1, blocking collectives, local(): row_max = lax.pmax(local_max, 'cen')  8.84 us
    while x1, local copies, waits for them, and re-layouts, local(): logits = lax.map(score_block, (point_blocks, position))  6.52 us
  transfers between devices with their start and end apart: 24, of which 9 were waited for; matrix products, arithmetic and copies ran while one was open for 2% of the time, Pallas kernels for 0%

commit v1 on v0

v1 whole, which is shorter than its diff:
```python
import math

import jax
import jax.numpy as jnp
from jax import lax
from jax.experimental import pallas as pl
from jax.experimental.pallas import tpu as pltpu
from jax.sharding import Mesh
from jax.sharding import PartitionSpec as P

D = 1024
CORES = 2
BLOCK = 256
LANES = 128
CHUNK = 512
FAR = -1e30

sharpness_factor = 1.5
prior_mass = 1.0
SHARP = sharpness_factor * math.sqrt(D)


def log_weights(mask_ref, points, rows_ref, square_ref, first_block, centre_rows):
    products = lax.dot_general(
        rows_ref[...], points, (((1,), (1,)), ((), ())), preferred_element_type=jnp.float32
    )
    count = rows_ref.shape[0] // centre_rows
    columns = []
    for part in range(points.shape[0] // BLOCK):
        pieces = []
        for b in range(count):
            rows = slice(b * centre_rows, (b + 1) * centre_rows)
            bias = square_ref[rows, :] + mask_ref[first_block + part, b]
            bias = jnp.concatenate([bias] * (BLOCK // LANES), 1)
            pieces.append(
                products[rows, part * BLOCK : (part + 1) * BLOCK] * (2.0 * SHARP) + bias
            )
        columns.append(jnp.concatenate(pieces, 0))
    return jnp.concatenate(columns, 1)


def fill_rows(shards, rows_ref, square_ref):
    size = shards[0].shape[0]
    for n, shard in enumerate(shards):
        value = shard[...]
        rows_ref[n * size : (n + 1) * size, :] = value
        wide = value.astype(jnp.float32)
        squares = jnp.sum(wide * wide, 1, keepdims=True) * (-SHARP)
        square_ref[n * size : (n + 1) * size, :] = jnp.broadcast_to(squares, (size, LANES))


def score_kernel(centre_rows, half, shard_count, has_earlier, *refs):
    mask_ref, core_ref = refs[:2]
    shards = refs[2 : 2 + shard_count]
    own_ref, other_ref = refs[2 + shard_count : 4 + shard_count]
    rest = refs[4 + shard_count :]
    if has_earlier:
        early_max, early_sum, power_ref, max_ref, lse_ref, rows_ref, square_ref = rest
    else:
        power_ref, max_ref, sum_ref, rows_ref, square_ref = rest
    step = pl.program_id(0)

    @pl.when(step == 0)
    def _():
        fill_rows(shards, rows_ref, square_ref)

    def chunk(points):
        logits = log_weights(
            mask_ref, points, rows_ref, square_ref, step * (CHUNK // BLOCK), centre_rows
        )
        top = jnp.max(logits, 0, keepdims=True)
        power = jnp.exp(logits - top)
        total = jnp.sum(power, 0, keepdims=True)
        power_ref[...] = power.astype(jnp.bfloat16)
        for n in range(CHUNK // LANES):
            group = step * (CHUNK // LANES) + n
            lanes = slice(n * LANES, (n + 1) * LANES)
            max_here, sum_here = top[:, lanes], total[:, lanes]
            max_ref[pl.ds(group, 1), :] = max_here
            if has_earlier:
                max_before = early_max[pl.ds(group, 1), :]
                sum_before = early_sum[pl.ds(group, 1), :]
                both = jnp.maximum(max_here, max_before)
                summed = sum_here * jnp.exp(max_here - both) + sum_before * jnp.exp(
                    max_before - both
                )
                groups = half // LANES
                place = jnp.where(
                    core_ref[0] == 0, group, lax.rem(group + groups, 2 * groups)
                )
                lse_ref[pl.ds(place, 1), :] = both + jnp.log(summed)
            else:
                sum_ref[pl.ds(group, 1), :] = sum_here

    steps = half // CHUNK

    @pl.when(step < steps)
    def _():
        chunk(own_ref[...])

    @pl.when(step >= steps)
    def _():
        chunk(other_ref[...])


def whole(shape):
    return pl.BlockSpec(shape, lambda i: (0,) * len(shape))


def score(shards, mask, core, own, other, centre_rows, earlier=None):
    size = shards[0].shape[0]
    half = own.shape[0]
    steps = half // CHUNK
    rows = size * len(shards)
    groups = 2 * half // LANES
    stat = jax.ShapeDtypeStruct((groups, LANES), jnp.float32)
    smem = pl.BlockSpec(memory_space=pltpu.SMEM)
    in_specs = [smem, smem]
    in_specs += [whole((size, D))] * len(shards)
    in_specs += [
        pl.BlockSpec((CHUNK, D), lambda i: (jnp.minimum(i, steps - 1), 0)),
        pl.BlockSpec((CHUNK, D), lambda i: (jnp.maximum(i - steps, 0), 0)),
    ]
    args = [mask, core, *shards, own, other]
    if earlier is not None:
        in_specs += [whole((groups, LANES))] * 2
        args += list(earlier)

    def kernel(*refs):
        score_kernel(centre_rows, half, len(shards), earlier is not None, *refs)

    return pl.pallas_call(
        kernel,
        grid=(2 * steps,),
        in_specs=in_specs,
        out_specs=[pl.BlockSpec((rows, CHUNK), lambda i: (0, i))]
        + [whole((groups, LANES))] * 2,
        out_shape=[jax.ShapeDtypeStruct((rows, 2 * half), jnp.bfloat16), stat, stat],
        scratch_shapes=[
            pltpu.VMEM((rows, D), jnp.bfloat16),
            pltpu.VMEM((rows, LANES), jnp.float32),
        ],
        compiler_params=pltpu.CompilerParams(vmem_limit_bytes=40 << 20),
        cost_estimate=pl.CostEstimate(
            flops=2 * rows * 2 * half * D,
            bytes_accessed=2 * half * D * 2 + rows * half * 4,
            transcendentals=rows * 2 * half,
        ),
    )(*args)


def moments_kernel(first, dests, size, half, keep, *refs):
    core_ref, all_ref, max_ref, live_ref, power_ref, own_ref, other_ref = refs[:7]
    outs = refs[7 : 7 + dests + (2 if keep else 0) + (1 if first else 0)]
    scale_ref, total_ref, mass_ref = refs[-3:]
    step = pl.program_id(0)
    steps = half // CHUNK
    groups = half // LANES

    @pl.when(step == 0)
    def _():
        parts = all_ref[...]
        top = jnp.max(parts, 0)
        lse = top + jnp.log(jnp.sum(jnp.exp(parts - top[None]), 0))
        here = jnp.where(core_ref[0] == 0, lse[:groups], lse[groups:])
        there = jnp.where(core_ref[0] == 0, lse[groups:], lse[:groups])
        ordered = jnp.concatenate([here, there], 0)
        scale_ref[...] = jnp.exp(max_ref[...] - ordered) * live_ref[...]
        if first:
            outs[-1][...] = here
        total_ref[...] = jnp.zeros_like(total_ref)
        mass_ref[...] = jnp.zeros_like(mass_ref)

    def chunk(points):
        pieces = []
        mass = mass_ref[...]
        for n in range(CHUNK // LANES):
            scale = scale_ref[pl.ds(step * (CHUNK // LANES) + n, 1), :]
            power = power_ref[:, n * LANES : (n + 1) * LANES].astype(jnp.float32)
            weights = (power * scale).astype(jnp.bfloat16)
            mass += weights.astype(jnp.float32)
            pieces.append(weights)
        mass_ref[...] = mass
        total_ref[...] += jnp.dot(
            jnp.concatenate(pieces, 1), points, preferred_element_type=jnp.float32
        )

    @pl.when(step < steps)
    def _():
        chunk(own_ref[...])

    @pl.when(step >= steps)
    def _():
        chunk(other_ref[...])

    @pl.when(step == 2 * steps - 1)
    def _():
        for n in range(dests + (1 if keep else 0)):
            rows = slice(n * size, (n + 1) * size)
            mass = jnp.sum(jnp.transpose(mass_ref[rows, :]), 0, keepdims=True)
            mass = jnp.broadcast_to(mass, (8, size))
            if n < dests:
                out = outs[n]
                for j in range(D // LANES):
                    out[j * size : (j + 1) * size, :] = total_ref[
                        rows, j * LANES : (j + 1) * LANES
                    ].astype(jnp.bfloat16)
                coarse = mass.astype(jnp.bfloat16).astype(jnp.float32)
                out[D // LANES * size :, :] = jnp.concatenate(
                    [coarse, mass - coarse], 0
                ).astype(jnp.bfloat16)
            else:
                outs[dests][...] = total_ref[rows, :]
                outs[dests + 1][...] = mass


def message_rows(size):
    return D // LANES * size + 16


def moments(core, everyone, top, live, power, own, other, size, dests, keep, first):
    half = own.shape[0]
    steps = half // CHUNK
    rows = power.shape[0]
    groups = 2 * half // LANES
    smem = pl.BlockSpec(memory_space=pltpu.SMEM)
    message = (message_rows(size), LANES)
    out_shape = [jax.ShapeDtypeStruct(message, jnp.bfloat16)] * dests
    if keep:
        out_shape += [
            jax.ShapeDtypeStruct((size, D), jnp.float32),
            jax.ShapeDtypeStruct((8, size), jnp.float32),
        ]
    if first:
        out_shape += [jax.ShapeDtypeStruct((half // LANES, LANES), jnp.float32)]

    def kernel(*refs):
        moments_kernel(first, dests, size, half, keep, *refs)

    return pl.pallas_call(
        kernel,
        grid=(2 * steps,),
        in_specs=[
            smem,
            whole(everyone.shape),
            whole((groups, LANES)),
            whole((groups, LANES)),
            pl.BlockSpec((rows, CHUNK), lambda i: (0, i)),
            pl.BlockSpec((CHUNK, D), lambda i: (jnp.minimum(i, steps - 1), 0)),
            pl.BlockSpec((CHUNK, D), lambda i: (jnp.maximum(i - steps, 0), 0)),
        ],
        out_specs=[whole(s.shape) for s in out_shape],
        out_shape=out_shape,
        scratch_shapes=[
            pltpu.VMEM((groups, LANES), jnp.float32),
            pltpu.VMEM((rows, D), jnp.float32),
            pltpu.VMEM((rows, LANES), jnp.float32),
        ],
        compiler_params=pltpu.CompilerParams(vmem_limit_bytes=40 << 20),
        cost_estimate=pl.CostEstimate(
            flops=2 * rows * 2 * half * D,
            bytes_accessed=2 * half * D * 2 + rows * half * 4,
            transcendentals=0,
        ),
    )(core, everyone, top, live, power, own, other)


def finish_kernel(size, *refs):
    home_ref, home_mass_ref, centre_ref = refs[:3]
    arrived = refs[3:-2]
    updated_ref, mass_out_ref = refs[-2:]
    tail = D // LANES * size
    mass = home_mass_ref[...]
    for message in arrived:
        sent = message[tail:, :].astype(jnp.float32)
        mass += sent[:8] + sent[8:]
    mass_out_ref[...] = mass
    inverse = 1.0 / (mass[:1] + prior_mass)
    inverse = jnp.transpose(jnp.broadcast_to(inverse, (LANES, size)))
    for j in range(D // LANES):
        lanes = slice(j * LANES, (j + 1) * LANES)
        total = home_ref[:, lanes] + prior_mass * centre_ref[:, lanes].astype(jnp.float32)
        for message in arrived:
            total += message[j * size : (j + 1) * size, :].astype(jnp.float32)
        updated_ref[:, lanes] = (total * inverse).astype(jnp.bfloat16)


def finish(home, home_mass, centre, arrived):
    size = centre.shape[0]
    return pl.pallas_call(
        lambda *refs: finish_kernel(size, *refs),
        out_shape=[
            jax.ShapeDtypeStruct((size, D), jnp.bfloat16),
            jax.ShapeDtypeStruct((8, size), jnp.float32),
        ],
        compiler_params=pltpu.CompilerParams(vmem_limit_bytes=40 << 20),
    )(home, home_mass, centre, *arrived)


def local(points, lengths, candidates, centroids):
    chips = lax.axis_size("chip")
    cen_count = lax.axis_size("cen")
    chip = lax.axis_index("chip")
    core = lax.axis_index("core")
    local_blocks, centre_rows, _ = centroids.shape
    size = local_blocks * centre_rows
    half = points.shape[0]

    def moved(value, steps):
        return lax.ppermute(value, "chip", [(c, (c + steps) % chips) for c in range(chips)])

    centre = centroids.reshape(size, D)
    near = [moved(centre, 1), moved(centre, -1)]
    far = [moved(centre, 2), moved(centre, -2)]
    swap = [(0, 1), (1, 0)]
    other = lax.ppermute(points, "core", swap)
    facts = jnp.concatenate([candidates, lengths[:, None]], 1)
    facts = jnp.concatenate([facts, lax.ppermute(facts, "core", swap)], 0)
    candidates, lengths = facts[:, :-1], facts[:, -1]

    owners = (chip + jnp.array([-1, 1, 0, -2, 2], jnp.int32)) % chips
    blocks = (
        (owners * CORES + core)[:, None] * local_blocks
        + jnp.arange(local_blocks, dtype=jnp.int32)[None, :]
    ).reshape(-1)
    chosen = jnp.any(candidates[:, None, :] == blocks[None, :, None], -1)
    mask = jnp.where(chosen, 0.0, FAR).astype(jnp.float32)
    places = jnp.arange(2 * half, dtype=jnp.int32).reshape(-1, BLOCK) % BLOCK
    live = (places < lengths[:, None]).astype(jnp.float32).reshape(-1, LANES)
    core_here = core.astype(jnp.int32).reshape(1)

    split = 3 * local_blocks
    near_power, near_max, near_sum = score(
        [*near, centre], mask[:, :split], core_here, points, other, centre_rows
    )
    far_power, far_max, lse_here = score(
        far, mask[:, split:], core_here, points, other, centre_rows, (near_max, near_sum)
    )
    count = CORES * cen_count
    everyone = lax.all_to_all(
        jnp.broadcast_to(lse_here, (count, *lse_here.shape)), ("core", "cen"), 0, 0
    )
    far_before, far_after, lse = moments(
        core_here, everyone, far_max, live, far_power, points, other, size, 2, False, True
    )
    arrived = [moved(far_before, -2), moved(far_after, 2)]
    near_before, near_after, home, home_mass = moments(
        core_here, everyone, near_max, live, near_power, points, other, size, 2, True, False
    )
    arrived += [moved(near_before, -1), moved(near_after, 1)]
    updated, masses = finish(home, home_mass, centre, arrived)
    return (
        updated.reshape(centroids.shape),
        masses[0].reshape(local_blocks, centre_rows),
        lse.reshape(-1),
    )


def solution(mesh):
    pt, cen = mesh.axis_names
    split = Mesh(
        mesh.devices.reshape(mesh.shape[pt] // CORES, CORES, mesh.shape[cen]),
        ("chip", "core", "cen"),
    )
    whole_pt = ("chip", "core")
    return jax.shard_map(
        local,
        mesh=split,
        in_specs=(P(whole_pt, None), P(whole_pt), P(whole_pt, None), P(whole_pt, "cen", None)),
        out_specs=(P(whole_pt, "cen", None), P(whole_pt, "cen"), P(whole_pt)),
        check_vma=False,
    )
```

time: 295 us -> 102 us (0.35)
  other arithmetic: 81.6 us -> 2.69 us
  starting transfers between devices: 97.9 us -> 47.3 us
  matrix products: 43.7 us -> 0 us
  Pallas kernels: 0 us -> 20.6 us
  blocking collectives: 14.9 us -> 0 us
  local copies, waits for them, and re-layouts: 29.3 us -> 15.1 us
  waiting for transfers between devices: 22.8 us -> 14.9 us
    scatter-add x12 -> x0, other arithmetic: 62 us -> none  [the longest x6 58.2 us: gather_stats(): moments = moments.at[slots_of].add(weighted_features)]
    ppermute x24 -> x10, starting transfers between devices: 97.9 us -> 42.4 us  [the longest x8 31.4 us: moved(): lax.ppermute(value, 'chip', [(c, (c + steps) % chips) for c in range(chip...]
    dot_general x12 -> x0, matrix products: 43.7 us -> none  [the longest x6 22.7 us: gather_stats(): jnp.einsum('ixn,io->xno', reshaped_input, sample_rows, preferred_element_...]
    pallas_call x0 -> x5, Pallas kernels: none -> 20.6 us  [the longest x2 11.6 us: score(): pl.pallas_call(kernel, grid=(2 * steps,), in_specs=in_specs, out_specs=[p...]
    gather x12 -> x0, local copies, waits for them, and re-layouts: 15.6 us -> none  [the longest x6 12.2 us: score_block(): gathered = window[slots_of].reshape(-1, feature_vectors)]
    ppermute x24 -> x10, waiting for transfers between devices: 22.8 us -> 9.95 us  [the longest x8 9.94 us: moved(): lax.ppermute(value, 'chip', [(c, (c + steps) % chips) for c in range(chip...]
    unnamed x12 -> x24, local copies, waits for them, and re-layouts: 2.77 us -> 12.3 us
    pmax x1 -> x0, blocking collectives: 8.84 us -> none  [local(): row_max = lax.pmax(local_max, 'cen')]
  transfers between devices with their start and end apart: 24 -> 11, of which waited for: 9 -> 3; matrix products, arithmetic and copies ran while one was open for 2% -> 4% of each run, Pallas kernels for 0% -> 11%
where the time goes in v1:
time: 102 us; the launch traced here: 101 us
  starting transfers between devices  47.3 us (46%)
  Pallas kernels  20.6 us (20%)
  local copies, waits for them, and re-layouts  15.1 us (15%)
  waiting for transfers between devices  14.9 us (15%)
  other arithmetic  2.69 us (3%)
    ppermute x8, starting transfers between devices, moved(): lax.ppermute(value, 'chip', [(c, (c + steps) % chips) for c in range(chip...  31.4 us
    unnamed x24, local copies, waits for them, and re-layouts  12.3 us
    pallas_call x2, Pallas kernels, score(): pl.pallas_call(kernel, grid=(2 * steps,), in_specs=in_specs, out_specs=[p...  11.6 us
    ppermute x8, waiting for transfers between devices, moved(): lax.ppermute(value, 'chip', [(c, (c + steps) % chips) for c in range(chip...  9.94 us
    ppermute x1, starting transfers between devices, local(): other = lax.ppermute(points, 'core', swap)  8.79 us
    pallas_call x2, Pallas kernels, moments(): pl.pallas_call(kernel, grid=(2 * steps,), in_specs=[smem, whole(everyone....  8.09 us
    all_to_all x1, starting transfers between devices, local(): lax.all_to_all(jnp.broadcast_to(lse_here, (count, *lse_here.shape)), ('co...  4.94 us
    all_to_all x1, waiting for transfers between devices, local(): lax.all_to_all(jnp.broadcast_to(lse_here, (count, *lse_here.shape)), ('co...  4.92 us
  transfers between devices with their start and end apart: 11, of which 3 were waited for; matrix products, arithmetic and copies ran while one was open for 4% of the time, Pallas kernels for 11%

profile of v1, /device:TPU:1, one launch (start us, length us, event | category | flops | bytes accessed | tf_op | source)
XLA Modules:
  0.0 101.5 jit_solution(2099667249953046651)
XLA Ops:
  0.6 8.8 %collective-permute-start.3 = (bf16[1536,1024]{1,0:T(8,128)(2,1)}, bf16[1536,1024]{1,0:T(8,128)(2,1)S(1)}, u32[]{:S(2)}, u32[]{:S(2)}) collective-permute-start(bf16[1536,1024]{1,0:T(8,128)(2,1)} %refs_5_.5), channel_id=1, source_target_pairs={{0,4},{4,0},{1,5},{5,1},{2,6},{6,2},{3,7},{7,3},{8,12},{12,8},{9,1... | collective-permute-start | bytes 9437192 | tf_op jit(solution)/shard_map/ppermute | solution.py:316
  9.4 1.9 %collective-permute-start.4 = (bf16[128,1024]{1,0:T(8,128)(2,1)}, bf16[128,1024]{1,0:T(8,128)(2,1)}, u32[]{:S(2)}, u32[]{:S(2)}) collective-permute-start(bf16[128,1024]{1,0:T(8,128)(2,1)} %bitcast.8), channel_id=1, source_target_pairs={{0,8},{8,16},{16,24},{24,32},{32,40},{40,48},{48,56},{56,64},{64,7... | collective-permute-start | bytes 786440 | tf_op jit(solution)/shard_map/ppermute | solution.py:310
  11.4 7.9 %collective-permute-start.5 = (bf16[128,1024]{1,0:T(8,128)(2,1)}, bf16[128,1024]{1,0:T(8,128)(2,1)}, u32[]{:S(2)}, u32[]{:S(2)}) collective-permute-start(bf16[128,1024]{1,0:T(8,128)(2,1)} %bitcast.9), channel_id=1, source_target_pairs={{0,504},{8,0},{16,8},{24,16},{32,24},{40,32},{48,40},{56,48},{64,5... | collective-permute-start | bytes 786440 | tf_op jit(solution)/shard_map/ppermute | solution.py:310
  19.3 1.9 %collective-permute-start.1 = (bf16[128,1024]{1,0:T(8,128)(2,1)}, bf16[128,1024]{1,0:T(8,128)(2,1)S(1)}, u32[]{:S(2)}, u32[]{:S(2)}) collective-permute-start(bf16[128,1024]{1,0:T(8,128)(2,1)} %bitcast.10), channel_id=1, source_target_pairs={{0,16},{8,24},{16,32},{24,40},{32,48},{40,56},{48,64},{56,72},{64,... | collective-permute-start | bytes 786440 | tf_op jit(solution)/shard_map/ppermute | solution.py:310
  22.7 2.2 %collective-permute-start = (s32[6,17]{1,0:T(8,128)S(1)}, s32[6,17]{1,0:T(8,128)S(1)}, u32[]{:S(2)}, u32[]{:S(2)}) collective-permute-start(s32[6,17]{1,0:T(8,128)S(1)} %pad_add_fusion.1), channel_id=1, source_target_pairs={{0,4},{4,0},{1,5},{5,1},{2,6},{6,2},{3,7},{7,3},{8,12},{12,8},{9,1... | collective-permute-start | bytes 1232 | tf_op jit(solution)/shard_map/ppermute | solution.py:318
  25.9 7.3 %collective-permute-start.2 = (bf16[128,1024]{1,0:T(8,128)(2,1)}, bf16[128,1024]{1,0:T(8,128)(2,1)}, u32[]{:S(2)}, u32[]{:S(2)}) collective-permute-start(bf16[128,1024]{1,0:T(8,128)(2,1)} %bitcast.11), channel_id=1, source_target_pairs={{0,496},{8,504},{16,0},{24,8},{32,16},{40,24},{48,32},{56,40},{64,... | collective-permute-start | bytes 786440 | tf_op jit(solution)/shard_map/ppermute | solution.py:310
  34.8 1.6 %copy-done.2 = bf16[1536,1024]{1,0:T(8,128)(2,1)} copy-done((bf16[1536,1024]{1,0:T(8,128)(2,1)}, bf16[1536,1024]{1,0:T(8,128)(2,1)S(1)}, u32[]{:S(2)}) %copy-start.2) | copy-done | bytes 3145752
  36.5 1.9 %copy-done = bf16[1536,1024]{1,0:T(8,128)(2,1)S(1)} copy-done((bf16[1536,1024]{1,0:T(8,128)(2,1)S(1)}, bf16[1536,1024]{1,0:T(8,128)(2,1)}, u32[]{:S(2)}) %copy-start) | copy-done | bytes 3145752
  38.4 1.9 %copy-done.3 = bf16[1536,1024]{1,0:T(8,128)(2,1)S(1)} copy-done((bf16[1536,1024]{1,0:T(8,128)(2,1)S(1)}, bf16[1536,1024]{1,0:T(8,128)(2,1)}, u32[]{:S(2)}) %copy-start.3) | copy-done | bytes 3145752
  41.2 6.5 %shard_map.76 = (bf16[384,3072]{1,0:T(8,128)(2,1)S(1)}, f32[24,128]{1,0:T(8,128)S(1)}, f32[24,128]{1,0:T(8,128)S(1)}) custom-call(f32[12,6]{1,0:T(8,128)S(1)} %bitcast.14, s32[1]{0:T(128)} %bitcast.refs_1_.refs_0_, bf16[128,1024]{1,0:T(8,128)(2,1)} %collective-permute-done.4.refs_2_, bf16[128,1024]{1,0:T(8,128)(2,1)} %collective-permute-done.5.refs_3_, ...), custom_call_target="tpu_custom_call" | custom-call | flops 2415919104 | bytes 8650752 | tf_op jit(solution)/shard_map/pallas_call | solution.py:132
  47.7 1.5 %copy-done.10 = bf16[384,3072]{1,0:T(8,128)(2,1)} copy-done((bf16[384,3072]{1,0:T(8,128)(2,1)}, bf16[384,3072]{1,0:T(8,128)(2,1)S(1)}, u32[]{:S(2)}) %copy-start.10) | copy-done | bytes 2359320
  49.2 5.1 %shard_map.77 = (bf16[256,3072]{1,0:T(8,128)(2,1)S(1)}, f32[24,128]{1,0:T(8,128)S(1)}, f32[24,128]{1,0:T(8,128)S(1)}) custom-call(f32[12,4]{1,0:T(8,128)S(1)} %slice.21.refs_0_, s32[1]{0:T(128)} %bitcast.refs_1_.refs_0_, bf16[128,1024]{1,0:T(8,128)(2,1)S(1)} %collective-permute-done.1.refs_2_, bf16[128,1024]{1,0:T(8,128)(2,1)} %collective-permute-done.2.refs_3_, ...), custom_call_target="tpu_custom_call" | custom-call | flops 1610612736 | bytes 7864320 | tf_op jit(solution)/shard_map/pallas_call | solution.py:132
  56.1 4.9 %all-to-all-start = ((f32[8,24,128]{2,1,0:T(8,128)}), f32[8,24,128]{2,1,0:T(8,128)S(1)}, u32[]{:S(2)}, u32[]{:S(2)}) async-start(f32[8,24,128]{2,1,0:T(8,128)} %broadcast_in_dim.20), calls=%async_computation | async-start | bytes 196608 | tf_op jit(solution)/shard_map/all_to_all | solution.py:340
  61.2 4.9 %all-to-all-done.refs_1_ = f32[8,24,128]{2,1,0:T(8,128)S(1)} async-done(((f32[8,24,128]{2,1,0:T(8,128)}), f32[8,24,128]{2,1,0:T(8,128)S(1)}, u32[]{:S(2)}, u32[]{:S(2)}) %all-to-all-start) | async-done | bytes 98336 | tf_op jit(solution)/shard_map/all_to_all | solution.py:340
  66.1 1.9 %copy-done.5 = bf16[1536,1024]{1,0:T(8,128)(2,1)S(1)} copy-done((bf16[1536,1024]{1,0:T(8,128)(2,1)S(1)}, bf16[1536,1024]{1,0:T(8,128)(2,1)}, u32[]{:S(2)}) %copy-start.5) | copy-done | bytes 3145752
  68.0 1.4 %copy-done.7 = bf16[256,3072]{1,0:T(8,128)(2,1)S(1)} copy-done((bf16[256,3072]{1,0:T(8,128)(2,1)S(1)}, bf16[256,3072]{1,0:T(8,128)(2,1)}, u32[]{:S(2)}) %copy-start.7) | copy-done | bytes 1572888
  69.4 3.8 %shard_map.79 = (bf16[1040,128]{1,0:T(8,128)(2,1)S(1)}, bf16[1040,128]{1,0:T(8,128)(2,1)S(1)}, f32[12,128]{1,0:T(8,128)}) custom-call(s32[1]{0:T(128)} %bitcast.refs_1_.refs_0_, f32[8,24,128]{2,1,0:T(8,128)S(1)} %all-to-all-done.refs_1_, f32[24,128]{1,0:T(8,128)S(1)} %get-tuple-element.24.refs_2_, f32[24,128]{1,0:T(8,128)S(1)} %fusion.2.refs_3_, ...), custom_call_target="tpu_custom_call" | custom-call | flops 1610612736 | bytes 7864320 | tf_op jit(solution)/shard_map/pallas_call | solution.py:240
  73.2 1.9 %collective-permute-start.6 = (bf16[1040,128]{1,0:T(8,128)(2,1)S(1)}, bf16[1040,128]{1,0:T(8,128)(2,1)S(1)}, u32[]{:S(2)}, u32[]{:S(2)}) collective-permute-start(bf16[1040,128]{1,0:T(8,128)(2,1)S(1)} %get-tuple-element.26), channel_id=1, source_target_pairs={{0,496},{8,504},{16,0},{24,8},{32,16},{40,24},{48,32},{56,40},{64,... | collective-permute-start | bytes 798728 | tf_op jit(solution)/shard_map/ppermute | solution.py:310
  75.2 4.9 %collective-permute-start.7 = (bf16[1040,128]{1,0:T(8,128)(2,1)S(1)}, bf16[1040,128]{1,0:T(8,128)(2,1)S(1)}, u32[]{:S(2)}, u32[]{:S(2)}) collective-permute-start(bf16[1040,128]{1,0:T(8,128)(2,1)S(1)} %get-tuple-element.27), channel_id=1, source_target_pairs={{0,16},{8,24},{16,32},{24,40},{32,48},{40,56},{48,64},{56,72},{64,... | collective-permute-start | bytes 798728 | tf_op jit(solution)/shard_map/ppermute | solution.py:310
  80.0 4.3 %shard_map.78 = (bf16[1040,128]{1,0:T(8,128)(2,1)S(1)}, bf16[1040,128]{1,0:T(8,128)(2,1)S(1)}, f32[128,1024]{1,0:T(8,128)S(1)}, f32[8,128]{1,0:T(8,128)S(1)}) custom-call(s32[1]{0:T(128)} %bitcast.refs_1_.refs_0_, f32[8,24,128]{2,1,0:T(8,128)S(1)} %all-to-all-done.refs_1_, f32[24,128]{1,0:T(8,128)S(1)} %get-tuple-element.18.refs_6_.refs_2_, ...), custom_call_target="tpu_custom_call" | custom-call | flops 2415919104 | bytes 8650752 | tf_op jit(solution)/shard_map/pallas_call | solution.py:240
  84.3 3.6 %collective-permute-start.8 = (bf16[1040,128]{1,0:T(8,128)(2,1)S(1)}, bf16[1040,128]{1,0:T(8,128)(2,1)S(1)}, u32[]{:S(2)}, u32[]{:S(2)}) collective-permute-start(bf16[1040,128]{1,0:T(8,128)(2,1)S(1)} %get-tuple-element.28), channel_id=1, source_target_pairs={{0,504},{8,0},{16,8},{24,16},{32,24},{40,32},{48,40},{56,48},{64,5... | collective-permute-start | bytes 798728 | tf_op jit(solution)/shard_map/ppermute | solution.py:310
  88.0 1.9 %collective-permute-start.9 = (bf16[1040,128]{1,0:T(8,128)(2,1)S(1)}, bf16[1040,128]{1,0:T(8,128)(2,1)S(1)}, u32[]{:S(2)}, u32[]{:S(2)}) collective-permute-start(bf16[1040,128]{1,0:T(8,128)(2,1)S(1)} %get-tuple-element.29), channel_id=1, source_target_pairs={{0,8},{8,16},{16,24},{24,32},{32,40},{40,48},{48,56},{56,64},{64,7... | collective-permute-start | bytes 798728 | tf_op jit(solution)/shard_map/ppermute | solution.py:310
  89.9 3.2 %collective-permute-done.8.refs_5_ = bf16[1040,128]{1,0:T(8,128)(2,1)S(1)} collective-permute-done((bf16[1040,128]{1,0:T(8,128)(2,1)S(1)}, bf16[1040,128]{1,0:T(8,128)(2,1)S(1)}, u32[]{:S(2)}, u32[]{:S(2)}) %collective-permute-start.8) | collective-permute-done | bytes 266272 | tf_op jit(solution)/shard_map/ppermute | solution.py:310
  93.1 6.7 %collective-permute-done.9.refs_6_ = bf16[1040,128]{1,0:T(8,128)(2,1)S(1)} collective-permute-done((bf16[1040,128]{1,0:T(8,128)(2,1)S(1)}, bf16[1040,128]{1,0:T(8,128)(2,1)S(1)}, u32[]{:S(2)}, u32[]{:S(2)}) %collective-permute-start.9) | collective-permute-done | bytes 266272 | tf_op jit(solution)/shard_map/ppermute | solution.py:310
  (48 shorter events, 8.6 us)
Async XLA Ops:
  0.6 34.2 %collective-permute-start.3 = (bf16[1536,1024]{1,0:T(8,128)(2,1)}, bf16[1536,1024]{1,0:T(8,128)(2,1)S(1)}, u32[]{:S(2)}, u32[]{:S(2)}) collective-permute-start(bf16[1536,1024]{1,0:T(8,128)(2,1)} %refs_5_.5), channel_id=1, source_target_pairs={{0,4},{4,0},{1,5},{5,1},{2,6},{6,2},{3,7},{7,3},{8,12},{12,8},{9,1... | collective-permute-start | bytes 9437192 | tf_op jit(solution)/shard_map/ppermute | solution.py:316
  9.4 25.4 %collective-permute-start.4 = (bf16[128,1024]{1,0:T(8,128)(2,1)}, bf16[128,1024]{1,0:T(8,128)(2,1)}, u32[]{:S(2)}, u32[]{:S(2)}) collective-permute-start(bf16[128,1024]{1,0:T(8,128)(2,1)} %bitcast.8), channel_id=1, source_target_pairs={{0,8},{8,16},{16,24},{24,32},{32,40},{40,48},{48,56},{56,64},{64,7... | collective-permute-start | bytes 786440 | tf_op jit(solution)/shard_map/ppermute | solution.py:310
  11.4 23.4 %collective-permute-start.5 = (bf16[128,1024]{1,0:T(8,128)(2,1)}, bf16[128,1024]{1,0:T(8,128)(2,1)}, u32[]{:S(2)}, u32[]{:S(2)}) collective-permute-start(bf16[128,1024]{1,0:T(8,128)(2,1)} %bitcast.9), channel_id=1, source_target_pairs={{0,504},{8,0},{16,8},{24,16},{32,24},{40,32},{48,40},{56,48},{64,5... | collective-permute-start | bytes 786440 | tf_op jit(solution)/shard_map/ppermute | solution.py:310
  19.3 29.9 %collective-permute-start.1 = (bf16[128,1024]{1,0:T(8,128)(2,1)}, bf16[128,1024]{1,0:T(8,128)(2,1)S(1)}, u32[]{:S(2)}, u32[]{:S(2)}) collective-permute-start(bf16[128,1024]{1,0:T(8,128)(2,1)} %bitcast.10), channel_id=1, source_target_pairs={{0,16},{8,24},{16,32},{24,40},{32,48},{40,56},{48,64},{56,72},{64,... | collective-permute-start | bytes 786440 | tf_op jit(solution)/shard_map/ppermute | solution.py:310
  22.7 3.1 %collective-permute-start = (s32[6,17]{1,0:T(8,128)S(1)}, s32[6,17]{1,0:T(8,128)S(1)}, u32[]{:S(2)}, u32[]{:S(2)}) collective-permute-start(s32[6,17]{1,0:T(8,128)S(1)} %pad_add_fusion.1), channel_id=1, source_target_pairs={{0,4},{4,0},{1,5},{5,1},{2,6},{6,2},{3,7},{7,3},{8,12},{12,8},{9,1... | collective-permute-start | bytes 1232 | tf_op jit(solution)/shard_map/ppermute | solution.py:318
  25.9 23.3 %collective-permute-start.2 = (bf16[128,1024]{1,0:T(8,128)(2,1)}, bf16[128,1024]{1,0:T(8,128)(2,1)}, u32[]{:S(2)}, u32[]{:S(2)}) collective-permute-start(bf16[128,1024]{1,0:T(8,128)(2,1)} %bitcast.11), channel_id=1, source_target_pairs={{0,496},{8,504},{16,0},{24,8},{32,16},{40,24},{48,32},{56,40},{64,... | collective-permute-start | bytes 786440 | tf_op jit(solution)/shard_map/ppermute | solution.py:310
  34.8 1.7 %copy-start.2 = (bf16[1536,1024]{1,0:T(8,128)(2,1)}, bf16[1536,1024]{1,0:T(8,128)(2,1)S(1)}, u32[]{:S(2)}) copy-start(bf16[1536,1024]{1,0:T(8,128)(2,1)S(1)} %collective-permute-done.3.refs_6_.refs_5_) | copy-start | bytes 9437188
  36.5 1.9 %copy-start = (bf16[1536,1024]{1,0:T(8,128)(2,1)S(1)}, bf16[1536,1024]{1,0:T(8,128)(2,1)}, u32[]{:S(2)}) copy-start(bf16[1536,1024]{1,0:T(8,128)(2,1)} %refs_5_.5) | copy-start | bytes 9437188
  38.4 1.9 %copy-start.3 = (bf16[1536,1024]{1,0:T(8,128)(2,1)S(1)}, bf16[1536,1024]{1,0:T(8,128)(2,1)}, u32[]{:S(2)}) copy-start(bf16[1536,1024]{1,0:T(8,128)(2,1)} %copy-done.2) | copy-start | bytes 9437188
  40.2 0.9 copy-start.8
  41.2 8.0 %copy-start.1 = (bf16[1536,1024]{1,0:T(8,128)(2,1)S(1)}, bf16[1536,1024]{1,0:T(8,128)(2,1)}, u32[]{:S(2)}) copy-start(bf16[1536,1024]{1,0:T(8,128)(2,1)} %refs_5_.5) | copy-start | bytes 9437188
  41.2 8.0 %copy-start.4 = (bf16[1536,1024]{1,0:T(8,128)(2,1)S(1)}, bf16[1536,1024]{1,0:T(8,128)(2,1)}, u32[]{:S(2)}) copy-start(bf16[1536,1024]{1,0:T(8,128)(2,1)} %copy-done.2) | copy-start | bytes 9437188
  47.7 1.5 %copy-start.10 = (bf16[384,3072]{1,0:T(8,128)(2,1)}, bf16[384,3072]{1,0:T(8,128)(2,1)S(1)}, u32[]{:S(2)}) copy-start(bf16[384,3072]{1,0:T(8,128)(2,1)S(1)} %get-tuple-element.21.refs_4_) | copy-start | bytes 7077892
  54.3 1.2 %copy-start.6 = (bf16[256,3072]{1,0:T(8,128)(2,1)}, bf16[256,3072]{1,0:T(8,128)(2,1)S(1)}, u32[]{:S(2)}) copy-start(bf16[256,3072]{1,0:T(8,128)(2,1)S(1)} %get-tuple-element.25.refs_4_) | copy-start | bytes 4718596
  56.1 10.0 %all-to-all-start = ((f32[8,24,128]{2,1,0:T(8,128)}), f32[8,24,128]{2,1,0:T(8,128)S(1)}, u32[]{:S(2)}, u32[]{:S(2)}) async-start(f32[8,24,128]{2,1,0:T(8,128)} %broadcast_in_dim.20), calls=%async_computation | async-start | bytes 196608 | tf_op jit(solution)/shard_map/all_to_all | solution.py:340
  66.1 1.9 %copy-start.5 = (bf16[1536,1024]{1,0:T(8,128)(2,1)S(1)}, bf16[1536,1024]{1,0:T(8,128)(2,1)}, u32[]{:S(2)}) copy-start(bf16[1536,1024]{1,0:T(8,128)(2,1)} %copy-done.2) | copy-start | bytes 9437188
  68.0 1.4 %copy-start.7 = (bf16[256,3072]{1,0:T(8,128)(2,1)S(1)}, bf16[256,3072]{1,0:T(8,128)(2,1)}, u32[]{:S(2)}) copy-start(bf16[256,3072]{1,0:T(8,128)(2,1)} %copy-done.6) | copy-start | bytes 4718596
  69.4 10.6 %copy-start.11 = (bf16[384,3072]{1,0:T(8,128)(2,1)S(1)}, bf16[384,3072]{1,0:T(8,128)(2,1)}, u32[]{:S(2)}) copy-start(bf16[384,3072]{1,0:T(8,128)(2,1)} %copy-done.10) | copy-start | bytes 7077892
  73.2 16.7 %collective-permute-start.6 = (bf16[1040,128]{1,0:T(8,128)(2,1)S(1)}, bf16[1040,128]{1,0:T(8,128)(2,1)S(1)}, u32[]{:S(2)}, u32[]{:S(2)}) collective-permute-start(bf16[1040,128]{1,0:T(8,128)(2,1)S(1)} %get-tuple-element.26), channel_id=1, source_target_pairs={{0,496},{8,504},{16,0},{24,8},{32,16},{40,24},{48,32},{56,40},{64,... | collective-permute-start | bytes 798728 | tf_op jit(solution)/shard_map/ppermute | solution.py:310
  75.2 14.8 %collective-permute-start.7 = (bf16[1040,128]{1,0:T(8,128)(2,1)S(1)}, bf16[1040,128]{1,0:T(8,128)(2,1)S(1)}, u32[]{:S(2)}, u32[]{:S(2)}) collective-permute-start(bf16[1040,128]{1,0:T(8,128)(2,1)S(1)} %get-tuple-element.27), channel_id=1, source_target_pairs={{0,16},{8,24},{16,32},{24,40},{32,48},{40,56},{48,64},{56,72},{64,... | collective-permute-start | bytes 798728 | tf_op jit(solution)/shard_map/ppermute | solution.py:310
  80.0 19.8 %copy-start.9 = (bf16[2,64,1024]{2,1,0:T(8,128)(2,1)S(1)}, bf16[2,64,1024]{2,1,0:T(8,128)(2,1)}, u32[]{:S(2)}) copy-start(bf16[2,64,1024]{2,1,0:T(8,128)(2,1)} %param.8) | copy-start | bytes 786436
  84.3 8.8 %collective-permute-start.8 = (bf16[1040,128]{1,0:T(8,128)(2,1)S(1)}, bf16[1040,128]{1,0:T(8,128)(2,1)S(1)}, u32[]{:S(2)}, u32[]{:S(2)}) collective-permute-start(bf16[1040,128]{1,0:T(8,128)(2,1)S(1)} %get-tuple-element.28), channel_id=1, source_target_pairs={{0,504},{8,0},{16,8},{24,16},{32,24},{40,32},{48,40},{56,48},{64,5... | collective-permute-start | bytes 798728 | tf_op jit(solution)/shard_map/ppermute | solution.py:310
  88.0 11.9 %collective-permute-start.9 = (bf16[1040,128]{1,0:T(8,128)(2,1)S(1)}, bf16[1040,128]{1,0:T(8,128)(2,1)S(1)}, u32[]{:S(2)}, u32[]{:S(2)}) collective-permute-start(bf16[1040,128]{1,0:T(8,128)(2,1)S(1)} %get-tuple-element.29), channel_id=1, source_target_pairs={{0,8},{8,16},{16,24},{24,32},{32,40},{40,48},{48,56},{56,64},{64,7... | collective-permute-start | bytes 798728 | tf_op jit(solution)/shard_map/ppermute | solution.py:310

commit v2 on v0

v2 whole, which is shorter than its diff:
```python
import math

import jax
import jax.numpy as jnp
from jax import lax
from jax.experimental import pallas as pl
from jax.experimental.pallas import tpu as pltpu
from jax.sharding import Mesh
from jax.sharding import PartitionSpec as P

D = 1024
CORES = 2
ROW = 4
BLOCK = 256
LANES = 128
CHUNK = 512
GROUPS = CHUNK // LANES
FAR = -1e30
VMEM_LIMIT = 24 << 20

sharpness_factor = 1.5
prior_mass = 1.0
SHARP = sharpness_factor * math.sqrt(D) / math.log(2.0)

SMEM = pl.BlockSpec(memory_space=pltpu.SMEM)
VMEM = pl.BlockSpec(memory_space=pltpu.VMEM)


def compiler_params():
    return pltpu.CompilerParams(vmem_limit_bytes=VMEM_LIMIT)


def fill_rows(shards, rows_ref, square_ref, first):
    size = shards[0].shape[0]
    for n, shard in enumerate(shards, first):
        for r in range(0, size, 32):
            value = shard[r : r + 32, :]
            at = slice(n * size + r, n * size + r + 32)
            rows_ref[at, :] = value
            wide = value.astype(jnp.float32)
            squares = jnp.sum(wide * wide, 1, keepdims=True) * (-SHARP)
            square_ref[at, :] = jnp.broadcast_to(squares, (32, LANES))


def reached(name, chip, chips):
    low = lax.rem(chip, ROW) < ROW // 2
    step = {
        "before": chips - 1,
        "after": 1,
        "own": 0,
        "row": jnp.where(low, 2, chips - 2),
        "beyond": jnp.where(low, chips - 2, 2),
    }[name]
    return lax.rem(chip + step, chips)


def fill_mask(names, chips, local_blocks, chip_ref, core_ref, candidate_ref, mask_ref):
    count = candidate_ref.shape[1]
    own, other = candidate_ref[core_ref[0]], candidate_ref[1 - core_ref[0]]
    held = 0
    for name in names:
        owner = reached(name, chip_ref[0], chips) * CORES + core_ref[0]
        for n in range(local_blocks):
            block = owner * local_blocks + n
            for at, ids in ((0, own), (count, other)):
                here = jnp.where(ids == block, 0.0, FAR).astype(jnp.float32)
                here = jnp.max(here, 1, keepdims=True)
                mask_ref[held, at : at + count, :] = jnp.broadcast_to(here, (count, LANES))
            held += 1


def folded(op, tile):
    parts = [tile[r : r + 8] for r in range(0, tile.shape[0], 8)]
    while len(parts) > 1:
        parts = [op(a, b) for a, b in zip(parts[::2], parts[1::2])]
    return parts[0]


def score_kernel(names, chips, local_blocks, later, *refs):
    chip_ref, core_ref, candidate_ref = refs[:3]
    own_ref, other_ref = refs[3:5]
    shards = list(refs[5 : 5 + len(names)])
    rest = refs[5 + len(names) :]
    copies = []
    if later:
        early_max, early_sum, length_ref, power_ref, max_ref, message_ref = rest[:6]
        sum_ref = rest[6]
    else:
        power_ref, max_ref, sum_ref, kept_ref, centre_ref, semaphores = rest[:6]
        copies = [
            pltpu.make_async_copy(shards[-1], centre_ref, semaphores.at[0]),
            pltpu.make_async_copy(own_ref, kept_ref, semaphores.at[1]),
        ]
        own_ref, shards[-1] = kept_ref, centre_ref
    rows_ref, square_ref, mask_ref, product_ref = rest[-4:]
    half = own_ref.shape[0]
    steps = half // CHUNK
    centre_rows = shards[0].shape[0] // local_blocks
    blocks = len(names) * local_blocks

    for copy in copies:
        copy.start()
    if copies:
        fill_rows(shards[:-1], rows_ref, square_ref, 0)
        copies[0].wait()
        fill_rows(shards[-1:], rows_ref, square_ref, len(shards) - 1)
    else:
        fill_rows(shards, rows_ref, square_ref, 0)

    def multiply(step):
        source, first = (other_ref, step) if step < steps else (own_ref, step - steps)
        if step == steps and copies:
            copies[1].wait()
        product_ref[step % 2] = lax.dot_general(
            rows_ref[...],
            source[first * CHUNK : (first + 1) * CHUNK, :],
            (((1,), (1,)), ((), ())),
            preferred_element_type=jnp.float32,
        )

    multiply(0)
    fill_mask(names, chips, local_blocks, chip_ref, core_ref, candidate_ref, mask_ref)
    for step in range(2 * steps):
        if step + 1 < 2 * steps:
            multiply(step + 1)
        held = product_ref.at[step % 2]
        for n in range(GROUPS):
            lanes = slice(n * LANES, (n + 1) * LANES)
            place = (step * CHUNK + half) % (2 * half) + n * LANES
            q = place // BLOCK
            tops = []
            for b in range(blocks):
                rows = slice(b * centre_rows, (b + 1) * centre_rows)
                bias = square_ref[rows, :] + mask_ref[b, q : q + 1, :]
                logits = held[rows, lanes] * (2.0 * SHARP) + bias
                held[rows, lanes] = logits
                tops.append(folded(jnp.maximum, logits))
            top = tops[0]
            for more in tops[1:]:
                top = jnp.maximum(top, more)
            top = jnp.max(top, 0, keepdims=True)
            total = jnp.zeros((8, LANES), jnp.float32)
            for b in range(blocks):
                rows = slice(b * centre_rows, (b + 1) * centre_rows)
                power = jnp.exp2(held[rows, lanes] - top)
                total += folded(jnp.add, power)
                power_ref[rows, place : place + LANES] = power.astype(jnp.bfloat16)
            group = place // LANES
            max_ref[group : group + 1, :] = top
            sum_ref[group : group + 1, :] = jnp.sum(total, 0, keepdims=True)

    if later:
        both = jnp.maximum(max_ref[...], early_max[...])
        summed = sum_ref[...] * jnp.exp2(max_ref[...] - both)
        summed += early_sum[...] * jnp.exp2(early_max[...] - both)
        lse = both + jnp.log2(summed)
        groups = half // LANES
        here, there = lse[:groups], lse[groups:]
        first = core_ref[0] == 0
        lengths = [
            jnp.full((1, LANES), length_ref[q].astype(jnp.float32)) for q in range(half // BLOCK)
        ]
        lengths += [jnp.zeros((1, LANES), jnp.float32)] * (-len(lengths) % 8)
        message = jnp.concatenate(
            [jnp.where(first, here, there), jnp.where(first, there, here), *lengths], 0
        )
        for n in range(message_ref.shape[0]):
            message_ref[n] = message


def score(names, chips, chip, core, candidates, points, shards, local_blocks, later=None):
    size = shards[0].shape[0]
    half = points[0].shape[0]
    rows = size * len(shards)
    groups = 2 * half // LANES
    stat = jax.ShapeDtypeStruct((groups, LANES), jnp.float32)
    out_shape = [jax.ShapeDtypeStruct((rows, 2 * half), jnp.bfloat16), stat]
    scratch = []
    in_specs = [SMEM, SMEM] + [VMEM] * (3 + len(shards))
    args = [chip, core, candidates, *points, *shards]
    if later is None:
        in_specs[3] = in_specs[-1] = pl.BlockSpec(memory_space=pltpu.HBM)
        out_shape += [stat, jax.ShapeDtypeStruct(points[0].shape, points[0].dtype)]
        scratch += [pltpu.VMEM((size, D), shards[0].dtype), pltpu.SemaphoreType.DMA((2,))]
    else:
        early, lengths, copies = later
        in_specs += [VMEM, VMEM, SMEM]
        args += [*early, lengths]
        spare = -(-(half // BLOCK) // 8) * 8
        out_shape += [jax.ShapeDtypeStruct((copies, groups + spare, LANES), jnp.float32)]
        scratch += [pltpu.VMEM((groups, LANES), jnp.float32)]
    point_blocks = -(-(2 * half // BLOCK) // 8) * 8

    def kernel(*refs):
        score_kernel(names, chips, local_blocks, later is not None, *refs)

    return pl.pallas_call(
        kernel,
        in_specs=in_specs,
        out_specs=[VMEM] * len(out_shape),
        out_shape=out_shape,
        scratch_shapes=scratch
        + [
            pltpu.VMEM((rows, D), jnp.bfloat16),
            pltpu.VMEM((rows, LANES), jnp.float32),
            pltpu.VMEM((len(shards) * local_blocks, point_blocks, LANES), jnp.float32),
            pltpu.VMEM((2, rows, CHUNK), jnp.float32),
        ],
        compiler_params=compiler_params(),
        cost_estimate=pl.CostEstimate(
            flops=2 * rows * 2 * half * D,
            bytes_accessed=2 * half * D * 2 + rows * half * 4,
            transcendentals=rows * 2 * half,
        ),
    )(*args)


def write_message(out, total_ref, mass):
    size = total_ref.shape[0]
    for j in range(D // LANES):
        out[j * size : (j + 1) * size, :] = total_ref[:, j * LANES : (j + 1) * LANES].astype(
            jnp.bfloat16
        )
    coarse = mass.astype(jnp.bfloat16).astype(jnp.float32)
    out[D // LANES * size :, :] = jnp.concatenate([coarse, mass - coarse], 0).astype(jnp.bfloat16)


def merge_kernel(total_ref, mass_ref, arrived_ref, out_ref):
    size = total_ref.shape[0]
    tail = D // LANES * size
    for j in range(D // LANES):
        rows = slice(j * size, (j + 1) * size)
        total = total_ref[:, j * LANES : (j + 1) * LANES] + arrived_ref[rows, :].astype(jnp.float32)
        out_ref[rows, :] = total.astype(jnp.bfloat16)
    sent = arrived_ref[tail:, :].astype(jnp.float32)
    mass = mass_ref[...] + sent[:8] + sent[8:]
    coarse = mass.astype(jnp.bfloat16).astype(jnp.float32)
    out_ref[tail:, :] = jnp.concatenate([coarse, mass - coarse], 0).astype(jnp.bfloat16)


def merged(total, mass, arrived):
    return pl.pallas_call(
        merge_kernel,
        in_specs=[VMEM] * 3,
        out_specs=VMEM,
        out_shape=jax.ShapeDtypeStruct(arrived.shape, arrived.dtype),
        compiler_params=compiler_params(),
    )(total, mass, arrived)


def moments_kernel(sources, sent, size, keep, first, *refs):
    core_ref, all_ref, own_ref, other_ref = refs[:4]
    tops, powers = refs[4:6], refs[6:8]
    outs = refs[8:-4]
    scale_ref, total_ref, mass_ref, weight_ref = refs[-4:]
    half = own_ref.shape[0]
    steps = half // CHUNK
    groups = half // LANES
    at_zero = core_ref[0] == 0

    parts = all_ref[:, : 2 * groups, :]
    top = jnp.max(parts, 0)
    lse = top + jnp.log2(jnp.sum(jnp.exp2(parts - top[None]), 0))
    here = jnp.where(at_zero, lse[:groups], lse[groups:])
    there = jnp.where(at_zero, lse[groups:], lse[:groups])
    for n, top_ref in enumerate(tops):
        scale_ref[n] = jnp.exp2(top_ref[...] - jnp.concatenate([here, there], 0))
    if first:
        outs[-1][...] = here * math.log(2.0)
    copies = all_ref.shape[0] // CORES
    lane = lax.broadcasted_iota(jnp.int32, (1, LANES), 1).astype(jnp.float32)

    def weigh(step):
        for at in range(GROUPS):
            group = step * GROUPS + at
            q = group * LANES // BLOCK
            part = (group * LANES % BLOCK) // LANES
            row = 2 * groups + q % (half // BLOCK)
            zero, one = all_ref[0, row : row + 1, :], all_ref[copies, row : row + 1, :]
            mine = q < half // BLOCK
            length = jnp.where(at_zero, zero if mine else one, one if mine else zero)
            live = jnp.where(lane + part * LANES < length, 1.0, 0.0)
            lanes = slice(group * LANES, (group + 1) * LANES)
            for n, (which, start) in enumerate(sources):
                scale = scale_ref[which, group : group + 1, :] * live
                for r in range(0, size, 64):
                    power = powers[which][start + r : start + r + 64, lanes].astype(jnp.float32)
                    weights = (power * scale).astype(jnp.bfloat16)
                    rows = slice(n * size + r, n * size + r + 64)
                    weight_ref[rows, lanes] = weights
                    if group == 0:
                        mass_ref[rows, :] = weights.astype(jnp.float32)
                    else:
                        mass_ref[rows, :] += weights.astype(jnp.float32)

    weigh(0)
    for step in range(2 * steps):
        if step + 1 < 2 * steps:
            weigh(step + 1)
        source, at = (own_ref, step) if step < steps else (other_ref, step - steps)
        part = jnp.dot(
            weight_ref[:, step * CHUNK : (step + 1) * CHUNK],
            source[at * CHUNK : (at + 1) * CHUNK, :],
            preferred_element_type=jnp.float32,
        )
        if step == 0:
            total_ref[...] = part
        else:
            total_ref[...] += part

    for out, n in zip(outs, (*sent, keep)):
        rows = slice(n * size, (n + 1) * size)
        mass = jnp.sum(jnp.transpose(mass_ref[rows, :]), 0, keepdims=True)
        mass = jnp.broadcast_to(mass, (8, size))
        if n == keep:
            out[...] = total_ref[rows, :]
            outs[len(sent) + 1][...] = mass
        else:
            write_message(out, total_ref.at[rows, :], mass)


def moments(core, everyone, points, tops, powers, sources, size, sent, keep, first):
    half = points[0].shape[0]
    rows = len(sources) * size
    groups = 2 * half // LANES
    message = (D // LANES * size + 16, LANES)
    out_shape = [jax.ShapeDtypeStruct(message, jnp.bfloat16)] * len(sent)
    out_shape += [
        jax.ShapeDtypeStruct((size, D), jnp.float32),
        jax.ShapeDtypeStruct((8, size), jnp.float32),
    ]
    if first:
        out_shape += [jax.ShapeDtypeStruct((half // LANES, LANES), jnp.float32)]

    def kernel(*refs):
        moments_kernel(sources, sent, size, keep, first, *refs)

    return pl.pallas_call(
        kernel,
        in_specs=[SMEM] + [VMEM] * 7,
        out_specs=[VMEM] * len(out_shape),
        out_shape=out_shape,
        scratch_shapes=[
            pltpu.VMEM((len(tops), groups, LANES), jnp.float32),
            pltpu.VMEM((rows, D), jnp.float32),
            pltpu.VMEM((rows, LANES), jnp.float32),
            pltpu.VMEM((rows, 2 * half), jnp.bfloat16),
        ],
        compiler_params=compiler_params(),
        cost_estimate=pl.CostEstimate(
            flops=2 * rows * 2 * half * D,
            bytes_accessed=2 * half * D * 2 + rows * half * 4,
            transcendentals=0,
        ),
    )(core, everyone, *points, *tops, *powers)


def finish_kernel(*refs):
    home_ref, home_mass_ref, centre_ref = refs[:3]
    arrived = refs[3:-2]
    updated_ref, mass_out_ref = refs[-2:]
    size = centre_ref.shape[0]
    tail = D // LANES * size
    mass = home_mass_ref[...]
    for message in arrived:
        sent = message[tail:, :].astype(jnp.float32)
        mass += sent[:8] + sent[8:]
    rows, width = mass_out_ref.shape
    for n in range(rows):
        mass_out_ref[n : n + 1, :] = mass[:1, n * width : (n + 1) * width]
    inverse = 1.0 / (mass[:1] + prior_mass)
    inverse = jnp.transpose(jnp.broadcast_to(inverse, (LANES, size)))
    for j in range(D // LANES):
        lanes = slice(j * LANES, (j + 1) * LANES)
        total = home_ref[:, lanes] + prior_mass * centre_ref[:, lanes].astype(jnp.float32)
        for message in arrived:
            total += message[j * size : (j + 1) * size, :].astype(jnp.float32)
        updated_ref[:, lanes] = (total * inverse).astype(jnp.bfloat16)


def finish(home, home_mass, centre, arrived, local_blocks):
    size = centre.shape[0]
    return pl.pallas_call(
        finish_kernel,
        in_specs=[VMEM] * (3 + len(arrived)),
        out_specs=[VMEM] * 2,
        out_shape=[
            jax.ShapeDtypeStruct((size, D), jnp.bfloat16),
            jax.ShapeDtypeStruct((local_blocks, size // local_blocks), jnp.float32),
        ],
        compiler_params=compiler_params(),
    )(home, home_mass, centre, *arrived)


def local(points, lengths, candidates, centroids):
    chips = lax.axis_size("chip")
    copies = CORES * lax.axis_size("cen")
    chip = lax.axis_index("chip").astype(jnp.int32).reshape(1)
    core = lax.axis_index("core").astype(jnp.int32).reshape(1)
    local_blocks, centre_rows, _ = centroids.shape
    size = local_blocks * centre_rows

    def moved(value, step):
        return lax.ppermute(value, "chip", [(c, step(c) % chips) for c in range(chips)])

    def ahead(c):
        return c + 1

    def back(c):
        return c - 1

    def across(c):
        return c // ROW * ROW + (c + ROW // 2) % ROW

    def outward(c):
        return c + ROW if c % ROW < ROW // 2 else c - ROW

    def inward(c):
        return c - ROW if c % ROW < ROW // 2 else c + ROW

    def swapped(value):
        return lax.ppermute(value, "core", [(0, 1), (1, 0)])

    centre = centroids.reshape(size, D)
    row = moved(centre, across)
    near = [moved(centre, ahead), moved(centre, back)]
    beyond = moved(row, outward)
    other = swapped(points)
    candidates = lax.all_gather(candidates, "core")

    first_power, first_max, first_sum, kept = score(
        ("row", "own"),
        chips,
        chip,
        core,
        candidates,
        [pltpu.with_memory_space_constraint(points, pltpu.HBM), other],
        [row, pltpu.with_memory_space_constraint(centre, pltpu.HBM)],
        local_blocks,
    )
    points = [kept, other]
    last_power, last_max, message = score(
        ("before", "after", "beyond"),
        chips,
        chip,
        core,
        candidates,
        points,
        [*near, beyond],
        local_blocks,
        ((first_max, first_sum), lengths, copies),
    )
    everyone = lax.all_to_all(message, ("core", "cen"), 0, 0)
    tops, powers = (first_max, last_max), (first_power, last_power)
    beyond, row, row_mass, lse = moments(
        core, everyone, points, tops, powers, ((1, 2 * size), (0, 0)), size, (0,), 1, True
    )
    beyond = moved(beyond, inward)
    before, after, home, home_mass = moments(
        core, everyone, points, tops, powers, ((1, 0), (1, size), (0, size)), size, (0, 1), 2, False
    )
    arrived = [moved(before, back), moved(after, ahead)]
    arrived += [moved(merged(row, row_mass, beyond), across)]
    updated, masses = finish(home, home_mass, centre, arrived, local_blocks)
    return updated.reshape(centroids.shape), masses, lse.reshape(-1)


def solution(mesh):
    pt, cen = mesh.axis_names
    split = Mesh(
        mesh.devices.reshape(mesh.shape[pt] // CORES, CORES, mesh.shape[cen]),
        ("chip", "core", "cen"),
    )
    whole_pt = ("chip", "core")
    return jax.shard_map(
        local,
        mesh=split,
        in_specs=(P(whole_pt, None), P(whole_pt), P(whole_pt, None), P(whole_pt, "cen", None)),
        out_specs=(P(whole_pt, "cen", None), P(whole_pt, "cen"), P(whole_pt)),
        check_vma=False,
    )
```

time: 295 us -> 82.1 us (0.28); the launches traced: 292 us -> 81.7 us
  other arithmetic: 81.6 us -> 0 us
  starting transfers between devices: 97.9 us -> 35.7 us
  matrix products: 43.7 us -> 0 us
  local copies, waits for them, and re-layouts: 29.3 us -> 0.01 us
  Pallas kernels: 0 us -> 14.8 us
  waiting for transfers between devices: 22.8 us -> 17.2 us
    ppermute x24 -> x9, starting transfers between devices: 97.9 us -> 35.7 us  [the longest x8 26.9 us: moved(): lax.ppermute(value, 'chip', [(c, step(c) % chips) for c in range(chips)])]
    scatter-add x12 -> x0, other arithmetic: 62 us -> none  [the longest x6 58.2 us: gather_stats(): moments = moments.at[slots_of].add(weighted_features)]
    dot_general x12 -> x0, matrix products: 43.7 us -> none  [the longest x6 22.7 us: gather_stats(): jnp.einsum('ixn,io->xno', reshaped_input, sample_rows, preferred_element_...]
    gather x12 -> x0, local copies, waits for them, and re-layouts: 15.6 us -> none  [the longest x6 12.2 us: score_block(): gathered = window[slots_of].reshape(-1, feature_vectors)]
    pallas_call x0 -> x6, Pallas kernels: none -> 14.8 us  [the longest x2 8.38 us: score(): pl.pallas_call(kernel, in_specs=in_specs, out_specs=[VMEM] * len(out_shap...]
    all_to_all x0 -> x1, blocking collectives: none -> 11 us  [local(): everyone = lax.all_to_all(message, ('core', 'cen'), 0, 0)]
    pmax x1 -> x0, blocking collectives: 8.84 us -> none  [local(): row_max = lax.pmax(local_max, 'cen')]
    convert_element_type x3 -> x0, other arithmetic: 6.92 us -> none  [the longest x1 3.92 us: local(): weights = (jnp.exp(logits - row_max[..., None]) / row_sum[..., None] * li...]
  transfers between devices with their start and end apart: 24 -> 9, of which waited for: 9 -> 4; matrix products, arithmetic and copies ran while one was open for 2% -> 0% of each run, Pallas kernels for 0% -> 8%
where the time goes in v2:
time: 82.1 us; the launch traced here: 81.7 us
  starting transfers between devices  35.7 us (43%)
  waiting for transfers between devices  17.2 us (21%)
  Pallas kernels  14.8 us (18%)
  blocking collectives  13.2 us (16%)
    ppermute x8, starting transfers between devices, moved(): lax.ppermute(value, 'chip', [(c, step(c) % chips) for c in range(chips)])  26.9 us
    ppermute x8, waiting for transfers between devices, moved(): lax.ppermute(value, 'chip', [(c, step(c) % chips) for c in range(chips)])  17.2 us
    all_to_all x1, blocking collectives, local(): everyone = lax.all_to_all(message, ('core', 'cen'), 0, 0)  11 us
    ppermute x1, starting transfers between devices, swapped(): return lax.ppermute(value, 'core', [(0, 1), (1, 0)])  8.79 us
    pallas_call x2, Pallas kernels, score(): pl.pallas_call(kernel, in_specs=in_specs, out_specs=[VMEM] * len(out_shap...  8.38 us
    pallas_call x2, Pallas kernels, moments(): pl.pallas_call(kernel, in_specs=[SMEM] + [VMEM] * 7, out_specs=[VMEM] * l...  5.44 us
    all_gather x1, blocking collectives, local(): candidates = lax.all_gather(candidates, 'core')  2.2 us
  transfers between devices with their start and end apart: 9, of which 4 were waited for; matrix products, arithmetic and copies ran while one was open for 0% of the time, Pallas kernels for 8%

profile of v2, /device:TPU:1, one launch (start us, length us, event | category | flops | bytes accessed | tf_op | source)
XLA Modules:
  0.0 81.7 jit_solution(10130380998777534939)
XLA Ops:
  0.6 8.8 %collective-permute-start = (bf16[1536,1024]{1,0:T(8,128)(2,1)}, bf16[1536,1024]{1,0:T(8,128)(2,1)S(1)}, u32[]{:S(2)}, u32[]{:S(2)}) collective-permute-start(bf16[1536,1024]{1,0:T(8,128)(2,1)} %refs_3_.1), channel_id=1, source_target_pairs={{0,4},{4,0},{1,5},{5,1},{2,6},{6,2},{3,7},{7,3},{8,12},{12,8},{9,1... | collective-permute-start | bytes 9437192 | tf_op jit(solution)/shard_map/ppermute | solution.py:422
  9.4 1.9 %collective-permute-start.1 = (bf16[128,1024]{1,0:T(8,128)(2,1)}, bf16[128,1024]{1,0:T(8,128)(2,1)S(1)}, u32[]{:S(2)}, u32[]{:S(2)}) collective-permute-start(bf16[128,1024]{1,0:T(8,128)(2,1)} %bitcast.6), channel_id=1, source_target_pairs={{0,16},{8,24},{16,0},{24,8},{32,48},{40,56},{48,32},{56,40},{64,80... | collective-permute-start | bytes 786440 | tf_op jit(solution)/shard_map/ppermute | solution.py:404
  11.4 1.9 %collective-permute-start.2 = (bf16[128,1024]{1,0:T(8,128)(2,1)}, bf16[128,1024]{1,0:T(8,128)(2,1)}, u32[]{:S(2)}, u32[]{:S(2)}) collective-permute-start(bf16[128,1024]{1,0:T(8,128)(2,1)} %bitcast.7), channel_id=1, source_target_pairs={{0,8},{8,16},{16,24},{24,32},{32,40},{40,48},{48,56},{56,64},{64,7... | collective-permute-start | bytes 786440 | tf_op jit(solution)/shard_map/ppermute | solution.py:404
  13.3 9.1 %collective-permute-start.3 = (bf16[128,1024]{1,0:T(8,128)(2,1)}, bf16[128,1024]{1,0:T(8,128)(2,1)}, u32[]{:S(2)}, u32[]{:S(2)}) collective-permute-start(bf16[128,1024]{1,0:T(8,128)(2,1)} %bitcast.8), channel_id=1, source_target_pairs={{0,504},{8,0},{16,8},{24,16},{32,24},{40,32},{48,40},{56,48},{64,5... | collective-permute-start | bytes 786440 | tf_op jit(solution)/shard_map/ppermute | solution.py:404
  22.4 0.0 collective-permute-done.1.refs_5_
  22.4 1.9 %collective-permute-start.4 = (bf16[128,1024]{1,0:T(8,128)(2,1)S(1)}, bf16[128,1024]{1,0:T(8,128)(2,1)}, u32[]{:S(2)}, u32[]{:S(2)}) collective-permute-start(bf16[128,1024]{1,0:T(8,128)(2,1)S(1)} %collective-permute-done.1.refs_5_), channel_id=1, source_target_pairs={{0,32},{8,40},{16,496},{24,504},{32,64},{40,72},{48,16},{56,24},{6... | collective-permute-start | bytes 786440 | tf_op jit(solution)/shard_map/ppermute | solution.py:404
  24.3 2.2 %all-gather.1.refs_2_ = s32[2,6,16]{2,1,0:T(8,128)S(1)} all-gather(s32[1,6,16]{2,1,0:T(8,128)} %bitcast.11), channel_id=2, replica_groups=mesh['chip'=64,'core'=2,'cen'=4] {'core'}, dimensions={0}, use_global_device_ids=true | all-gather | bytes 1152 | tf_op jit(solution)/shard_map/all_gather | solution.py:429
  26.5 3.8 %shard_map.67 = (bf16[256,3072]{1,0:T(8,128)(2,1)S(1)}, f32[24,128]{1,0:T(8,128)S(1)}, f32[24,128]{1,0:T(8,128)S(1)}, bf16[1536,1024]{1,0:T(8,128)(2,1)S(1)}) custom-call(s32[1]{0:T(128)} %bitcast.1.refs_0_, s32[1]{0:T(128)} %bitcast.refs_1_.refs_0_, s32[2,6,16]{2,1,0:T(8,128)S(1)} %all-gather.1.refs_2_, bf16[1536,1024]{1,0:T(8,128)(2,1)} %refs_3_.1, ...), custom_call_target="tpu_custom_call" | custom-call | flops 1610612736 | bytes 7864320 | tf_op jit(solution)/shard_map/pallas_call | solution.py:197
  30.3 0.0 collective-permute-done.2.refs_5_
  30.3 0.0 collective-permute-done.3.refs_6_
  30.3 2.7 %collective-permute-done.4.refs_7_ = bf16[128,1024]{1,0:T(8,128)(2,1)} collective-permute-done((bf16[128,1024]{1,0:T(8,128)(2,1)S(1)}, bf16[128,1024]{1,0:T(8,128)(2,1)}, u32[]{:S(2)}, u32[]{:S(2)}) %collective-permute-start.4) | collective-permute-done | bytes 262176 | tf_op jit(solution)/shard_map/ppermute | solution.py:404
  33.0 4.6 %shard_map.68 = (bf16[384,3072]{1,0:T(8,128)(2,1)S(1)}, f32[24,128]{1,0:T(8,128)S(1)}, f32[8,32,128]{2,1,0:T(8,128)S(1)}) custom-call(s32[1]{0:T(128)} %bitcast.1.refs_0_, s32[1]{0:T(128)} %bitcast.refs_1_.refs_0_, s32[2,6,16]{2,1,0:T(8,128)S(1)} %all-gather.1.refs_2_, bf16[1536,1024]{1,0:T(8,128)(2,1)S(1)} %get-tuple-element.20.refs_3_.refs_2_, ...), custom_call_target="tpu_custom_call" | custom-call | flops 2415919104 | bytes 8650752 | tf_op jit(solution)/shard_map/pallas_call | solution.py:197
  37.7 11.0 %all_to_all.5.refs_1_ = f32[8,32,128]{2,1,0:T(8,128)S(1)} all-to-all(f32[8,32,128]{2,1,0:T(8,128)S(1)} %get-tuple-element.23), channel_id=1, replica_groups=mesh['chip'=64,'core'=2,'cen'=4] {'core','cen'}, dimensions={0} | all-to-all | bytes 262144 | tf_op jit(solution)/shard_map/all_to_all | solution.py:453
  48.7 2.5 %shard_map.70 = (bf16[1040,128]{1,0:T(8,128)(2,1)S(1)}, f32[128,1024]{1,0:T(8,128)S(1)}, f32[8,128]{1,0:T(8,128)S(1)}, f32[12,128]{1,0:T(8,128)}) custom-call(s32[1]{0:T(128)} %bitcast.refs_1_.refs_0_, f32[8,32,128]{2,1,0:T(8,128)S(1)} %all_to_all.5.refs_1_, bf16[1536,1024]{1,0:T(8,128)(2,1)S(1)} %get-tuple-element.20.refs_3_.refs_2_, ...), custom_call_target="tpu_custom_call" | custom-call | flops 1610612736 | bytes 7864320 | tf_op jit(solution)/shard_map/pallas_call | solution.py:338
  51.2 3.5 %collective-permute-start.7 = (bf16[1040,128]{1,0:T(8,128)(2,1)S(1)}, bf16[1040,128]{1,0:T(8,128)(2,1)S(1)}, u32[]{:S(2)}, u32[]{:S(2)}) collective-permute-start(bf16[1040,128]{1,0:T(8,128)(2,1)S(1)} %get-tuple-element.33), channel_id=1, source_target_pairs={{0,480},{8,488},{16,48},{24,56},{32,0},{40,8},{48,80},{56,88},{64,... | collective-permute-start | bytes 798728 | tf_op jit(solution)/shard_map/ppermute | solution.py:404
  54.7 2.9 %shard_map.69 = (bf16[1040,128]{1,0:T(8,128)(2,1)S(1)}, bf16[1040,128]{1,0:T(8,128)(2,1)S(1)}, f32[128,1024]{1,0:T(8,128)S(1)}, f32[8,128]{1,0:T(8,128)S(1)}) custom-call(s32[1]{0:T(128)} %bitcast.refs_1_.refs_0_, f32[8,32,128]{2,1,0:T(8,128)S(1)} %all_to_all.5.refs_1_, bf16[1536,1024]{1,0:T(8,128)(2,1)S(1)} %get-tuple-element.20.refs_3_.refs_2_, ...), custom_call_target="tpu_custom_call" | custom-call | flops 2415919104 | bytes 8650752 | tf_op jit(solution)/shard_map/pallas_call | solution.py:338
  57.6 4.8 %collective-permute-start.5 = (bf16[1040,128]{1,0:T(8,128)(2,1)S(1)}, bf16[1040,128]{1,0:T(8,128)(2,1)S(1)}, u32[]{:S(2)}, u32[]{:S(2)}) collective-permute-start(bf16[1040,128]{1,0:T(8,128)(2,1)S(1)} %get-tuple-element.29), channel_id=1, source_target_pairs={{0,504},{8,0},{16,8},{24,16},{32,24},{40,32},{48,40},{56,48},{64,5... | collective-permute-start | bytes 798728 | tf_op jit(solution)/shard_map/ppermute | solution.py:404
  62.4 1.9 %collective-permute-start.6 = (bf16[1040,128]{1,0:T(8,128)(2,1)S(1)}, bf16[1040,128]{1,0:T(8,128)(2,1)S(1)}, u32[]{:S(2)}, u32[]{:S(2)}) collective-permute-start(bf16[1040,128]{1,0:T(8,128)(2,1)S(1)} %get-tuple-element.30), channel_id=1, source_target_pairs={{0,8},{8,16},{16,24},{24,32},{32,40},{40,48},{48,56},{56,64},{64,7... | collective-permute-start | bytes 798728 | tf_op jit(solution)/shard_map/ppermute | solution.py:404
  64.3 0.1 shard_map.71
  64.4 1.9 %collective-permute-start.8 = (bf16[1040,128]{1,0:T(8,128)(2,1)S(1)}, bf16[1040,128]{1,0:T(8,128)(2,1)S(1)}, u32[]{:S(2)}, u32[]{:S(2)}) collective-permute-start(bf16[1040,128]{1,0:T(8,128)(2,1)S(1)} %shard_map.71), channel_id=1, source_target_pairs={{0,16},{8,24},{16,0},{24,8},{32,48},{40,56},{48,32},{56,40},{64,80... | collective-permute-start | bytes 798728 | tf_op jit(solution)/shard_map/ppermute | solution.py:404
  66.3 1.4 %collective-permute-done.5.refs_3_ = bf16[1040,128]{1,0:T(8,128)(2,1)S(1)} collective-permute-done((bf16[1040,128]{1,0:T(8,128)(2,1)S(1)}, bf16[1040,128]{1,0:T(8,128)(2,1)S(1)}, u32[]{:S(2)}, u32[]{:S(2)}) %collective-permute-start.5) | collective-permute-done | bytes 266272 | tf_op jit(solution)/shard_map/ppermute | solution.py:404
  67.7 9.7 %collective-permute-done.6.refs_4_ = bf16[1040,128]{1,0:T(8,128)(2,1)S(1)} collective-permute-done((bf16[1040,128]{1,0:T(8,128)(2,1)S(1)}, bf16[1040,128]{1,0:T(8,128)(2,1)S(1)}, u32[]{:S(2)}, u32[]{:S(2)}) %collective-permute-start.6) | collective-permute-done | bytes 266272 | tf_op jit(solution)/shard_map/ppermute | solution.py:404
  77.4 3.4 %collective-permute-done.8.refs_5_ = bf16[1040,128]{1,0:T(8,128)(2,1)S(1)} collective-permute-done((bf16[1040,128]{1,0:T(8,128)(2,1)S(1)}, bf16[1040,128]{1,0:T(8,128)(2,1)S(1)}, u32[]{:S(2)}, u32[]{:S(2)}) %collective-permute-start.8) | collective-permute-done | bytes 266272 | tf_op jit(solution)/shard_map/ppermute | solution.py:404
  80.8 0.9 %shard_map.72 = (bf16[128,1024]{1,0:T(8,128)(2,1)}, f32[2,64]{1,0:T(2,128)}) custom-call(f32[128,1024]{1,0:T(8,128)S(1)} %get-tuple-element.27.refs_0_, f32[8,128]{1,0:T(8,128)S(1)} %get-tuple-element.28.refs_1_, bf16[128,1024]{1,0:T(8,128)(2,1)S(1)} %bitcast.10, bf16[1040,128]{1,0:T(8,128)(2,1)S(1)} %collective-permute-done.5.refs_3_, ...), custom_call_target="tpu_custom_call" | custom-call | tf_op jit(solution)/shard_map/pallas_call | solution.py:383
  (6 shorter events, 0.0 us)
Async XLA Ops:
  0.6 25.9 %collective-permute-start = (bf16[1536,1024]{1,0:T(8,128)(2,1)}, bf16[1536,1024]{1,0:T(8,128)(2,1)S(1)}, u32[]{:S(2)}, u32[]{:S(2)}) collective-permute-start(bf16[1536,1024]{1,0:T(8,128)(2,1)} %refs_3_.1), channel_id=1, source_target_pairs={{0,4},{4,0},{1,5},{5,1},{2,6},{6,2},{3,7},{7,3},{8,12},{12,8},{9,1... | collective-permute-start | bytes 9437192 | tf_op jit(solution)/shard_map/ppermute | solution.py:422
  9.4 12.9 %collective-permute-start.1 = (bf16[128,1024]{1,0:T(8,128)(2,1)}, bf16[128,1024]{1,0:T(8,128)(2,1)S(1)}, u32[]{:S(2)}, u32[]{:S(2)}) collective-permute-start(bf16[128,1024]{1,0:T(8,128)(2,1)} %bitcast.6), channel_id=1, source_target_pairs={{0,16},{8,24},{16,0},{24,8},{32,48},{40,56},{48,32},{56,40},{64,80... | collective-permute-start | bytes 786440 | tf_op jit(solution)/shard_map/ppermute | solution.py:404
  11.4 18.9 %collective-permute-start.2 = (bf16[128,1024]{1,0:T(8,128)(2,1)}, bf16[128,1024]{1,0:T(8,128)(2,1)}, u32[]{:S(2)}, u32[]{:S(2)}) collective-permute-start(bf16[128,1024]{1,0:T(8,128)(2,1)} %bitcast.7), channel_id=1, source_target_pairs={{0,8},{8,16},{16,24},{24,32},{32,40},{40,48},{48,56},{56,64},{64,7... | collective-permute-start | bytes 786440 | tf_op jit(solution)/shard_map/ppermute | solution.py:404
  13.3 17.0 %collective-permute-start.3 = (bf16[128,1024]{1,0:T(8,128)(2,1)}, bf16[128,1024]{1,0:T(8,128)(2,1)}, u32[]{:S(2)}, u32[]{:S(2)}) collective-permute-start(bf16[128,1024]{1,0:T(8,128)(2,1)} %bitcast.8), channel_id=1, source_target_pairs={{0,504},{8,0},{16,8},{24,16},{32,24},{40,32},{48,40},{56,48},{64,5... | collective-permute-start | bytes 786440 | tf_op jit(solution)/shard_map/ppermute | solution.py:404
  22.4 10.7 %collective-permute-start.4 = (bf16[128,1024]{1,0:T(8,128)(2,1)S(1)}, bf16[128,1024]{1,0:T(8,128)(2,1)}, u32[]{:S(2)}, u32[]{:S(2)}) collective-permute-start(bf16[128,1024]{1,0:T(8,128)(2,1)S(1)} %collective-permute-done.1.refs_5_), channel_id=1, source_target_pairs={{0,32},{8,40},{16,496},{24,504},{32,64},{40,72},{48,16},{56,24},{6... | collective-permute-start | bytes 786440 | tf_op jit(solution)/shard_map/ppermute | solution.py:404
  26.5 6.5 %copy-start.1 = (s32[6]{0:T(128)S(1)}, s32[6]{0:T(128)}, u32[]{:S(2)}) copy-start(s32[6]{0:T(128)} %refs_10_.1) | copy-start | bytes 76
  51.2 29.6 %copy-start = (bf16[2,64,1024]{2,1,0:T(8,128)(2,1)S(1)}, bf16[2,64,1024]{2,1,0:T(8,128)(2,1)}, u32[]{:S(2)}) copy-start(bf16[2,64,1024]{2,1,0:T(8,128)(2,1)} %param.7) | copy-start | bytes 786436
  51.2 13.1 %collective-permute-start.7 = (bf16[1040,128]{1,0:T(8,128)(2,1)S(1)}, bf16[1040,128]{1,0:T(8,128)(2,1)S(1)}, u32[]{:S(2)}, u32[]{:S(2)}) collective-permute-start(bf16[1040,128]{1,0:T(8,128)(2,1)S(1)} %get-tuple-element.33), channel_id=1, source_target_pairs={{0,480},{8,488},{16,48},{24,56},{32,0},{40,8},{48,80},{56,88},{64,... | collective-permute-start | bytes 798728 | tf_op jit(solution)/shard_map/ppermute | solution.py:404
  57.6 10.1 %collective-permute-start.5 = (bf16[1040,128]{1,0:T(8,128)(2,1)S(1)}, bf16[1040,128]{1,0:T(8,128)(2,1)S(1)}, u32[]{:S(2)}, u32[]{:S(2)}) collective-permute-start(bf16[1040,128]{1,0:T(8,128)(2,1)S(1)} %get-tuple-element.29), channel_id=1, source_target_pairs={{0,504},{8,0},{16,8},{24,16},{32,24},{40,32},{48,40},{56,48},{64,5... | collective-permute-start | bytes 798728 | tf_op jit(solution)/shard_map/ppermute | solution.py:404
  62.4 15.0 %collective-permute-start.6 = (bf16[1040,128]{1,0:T(8,128)(2,1)S(1)}, bf16[1040,128]{1,0:T(8,128)(2,1)S(1)}, u32[]{:S(2)}, u32[]{:S(2)}) collective-permute-start(bf16[1040,128]{1,0:T(8,128)(2,1)S(1)} %get-tuple-element.30), channel_id=1, source_target_pairs={{0,8},{8,16},{16,24},{24,32},{32,40},{40,48},{48,56},{56,64},{64,7... | collective-permute-start | bytes 798728 | tf_op jit(solution)/shard_map/ppermute | solution.py:404
  64.4 16.4 %collective-permute-start.8 = (bf16[1040,128]{1,0:T(8,128)(2,1)S(1)}, bf16[1040,128]{1,0:T(8,128)(2,1)S(1)}, u32[]{:S(2)}, u32[]{:S(2)}) collective-permute-start(bf16[1040,128]{1,0:T(8,128)(2,1)S(1)} %shard_map.71), channel_id=1, source_target_pairs={{0,16},{8,24},{16,0},{24,8},{32,48},{40,56},{48,32},{56,40},{64,80... | collective-permute-start | bytes 798728 | tf_op jit(solution)/shard_map/ppermute | solution.py:404

commit v3 on v2

--- a/solution.py
+++ b/solution.py
@@ -459,7 +459,7 @@
     before, after, home, home_mass = moments(
         core, everyone, points, tops, powers, ((1, 0), (1, size), (0, size)), size, (0, 1), 2, False
     )
-    arrived = [moved(before, back), moved(after, ahead)]
+    arrived = [moved(after, ahead), moved(before, back)]
     arrived += [moved(merged(row, row_mass, beyond), across)]
     updated, masses = finish(home, home_mass, centre, arrived, local_blocks)
     return updated.reshape(centroids.shape), masses, lse.reshape(-1)

time: 82.1 us -> 77.8 us (0.948)
  waiting for transfers between devices: 17.2 us -> 10.8 us
  starting transfers between devices: 35.7 us -> 37.6 us
    ppermute x8, waiting for transfers between devices: 17.2 us -> 10.8 us  [moved(): lax.ppermute(value, 'chip', [(c, step(c) % chips) for c in range(chips)])]
    ppermute x8, starting transfers between devices: 26.9 us -> 28.8 us  [moved(): lax.ppermute(value, 'chip', [(c, step(c) % chips) for c in range(chips)])]
  transfers between devices with their start and end apart: 9 -> 9, of which waited for: 4 -> 4; matrix products, arithmetic and copies ran while one was open for 0% -> 0% of each run, Pallas kernels for 8% -> 9%
where the time goes in v3:
time: 77.8 us; the launch traced here: 77.3 us
  starting transfers between devices  37.6 us (48%)
  Pallas kernels  14.8 us (19%)
  blocking collectives  13.2 us (17%)
  waiting for transfers between devices  10.8 us (14%)
    ppermute x8, starting transfers between devices, moved(): lax.ppermute(value, 'chip', [(c, step(c) % chips) for c in range(chips)])  28.8 us
    all_to_all x1, blocking collectives, local(): everyone = lax.all_to_all(message, ('core', 'cen'), 0, 0)  11 us
    ppermute x8, waiting for transfers between devices, moved(): lax.ppermute(value, 'chip', [(c, step(c) % chips) for c in range(chips)])  10.8 us
    ppermute x1, starting transfers between devices, swapped(): return lax.ppermute(value, 'core', [(0, 1), (1, 0)])  8.79 us
    pallas_call x2, Pallas kernels, score(): pl.pallas_call(kernel, in_specs=in_specs, out_specs=[VMEM] * len(out_shap...  8.38 us
    pallas_call x2, Pallas kernels, moments(): pl.pallas_call(kernel, in_specs=[SMEM] + [VMEM] * 7, out_specs=[VMEM] * l...  5.44 us
    all_gather x1, blocking collectives, local(): candidates = lax.all_gather(candidates, 'core')  2.2 us
  transfers between devices with their start and end apart: 9, of which 4 were waited for; matrix products, arithmetic and copies ran while one was open for 0% of the time, Pallas kernels for 9%

profile of v3, /device:TPU:1, one launch (start us, length us, event | category | flops | bytes accessed | tf_op | source)
XLA Modules:
  0.0 77.3 jit_solution(15427103985688003494)
XLA Ops:
  0.6 8.8 %collective-permute-start = (bf16[1536,1024]{1,0:T(8,128)(2,1)}, bf16[1536,1024]{1,0:T(8,128)(2,1)S(1)}, u32[]{:S(2)}, u32[]{:S(2)}) collective-permute-start(bf16[1536,1024]{1,0:T(8,128)(2,1)} %refs_3_.1), channel_id=1, source_target_pairs={{0,4},{4,0},{1,5},{5,1},{2,6},{6,2},{3,7},{7,3},{8,12},{12,8},{9,1... | collective-permute-start | bytes 9437192 | tf_op jit(solution)/shard_map/ppermute | solution.py:422
  9.4 1.9 %collective-permute-start.1 = (bf16[128,1024]{1,0:T(8,128)(2,1)}, bf16[128,1024]{1,0:T(8,128)(2,1)S(1)}, u32[]{:S(2)}, u32[]{:S(2)}) collective-permute-start(bf16[128,1024]{1,0:T(8,128)(2,1)} %bitcast.6), channel_id=1, source_target_pairs={{0,16},{8,24},{16,0},{24,8},{32,48},{40,56},{48,32},{56,40},{64,80... | collective-permute-start | bytes 786440 | tf_op jit(solution)/shard_map/ppermute | solution.py:404
  11.4 1.9 %collective-permute-start.2 = (bf16[128,1024]{1,0:T(8,128)(2,1)}, bf16[128,1024]{1,0:T(8,128)(2,1)}, u32[]{:S(2)}, u32[]{:S(2)}) collective-permute-start(bf16[128,1024]{1,0:T(8,128)(2,1)} %bitcast.7), channel_id=1, source_target_pairs={{0,8},{8,16},{16,24},{24,32},{32,40},{40,48},{48,56},{56,64},{64,7... | collective-permute-start | bytes 786440 | tf_op jit(solution)/shard_map/ppermute | solution.py:404
  13.3 9.1 %collective-permute-start.3 = (bf16[128,1024]{1,0:T(8,128)(2,1)}, bf16[128,1024]{1,0:T(8,128)(2,1)}, u32[]{:S(2)}, u32[]{:S(2)}) collective-permute-start(bf16[128,1024]{1,0:T(8,128)(2,1)} %bitcast.8), channel_id=1, source_target_pairs={{0,504},{8,0},{16,8},{24,16},{32,24},{40,32},{48,40},{56,48},{64,5... | collective-permute-start | bytes 786440 | tf_op jit(solution)/shard_map/ppermute | solution.py:404
  22.4 0.0 collective-permute-done.1.refs_5_
  22.4 1.9 %collective-permute-start.4 = (bf16[128,1024]{1,0:T(8,128)(2,1)S(1)}, bf16[128,1024]{1,0:T(8,128)(2,1)}, u32[]{:S(2)}, u32[]{:S(2)}) collective-permute-start(bf16[128,1024]{1,0:T(8,128)(2,1)S(1)} %collective-permute-done.1.refs_5_), channel_id=1, source_target_pairs={{0,32},{8,40},{16,496},{24,504},{32,64},{40,72},{48,16},{56,24},{6... | collective-permute-start | bytes 786440 | tf_op jit(solution)/shard_map/ppermute | solution.py:404
  24.3 2.2 %all-gather.1.refs_2_ = s32[2,6,16]{2,1,0:T(8,128)S(1)} all-gather(s32[1,6,16]{2,1,0:T(8,128)} %bitcast.11), channel_id=2, replica_groups=mesh['chip'=64,'core'=2,'cen'=4] {'core'}, dimensions={0}, use_global_device_ids=true | all-gather | bytes 1152 | tf_op jit(solution)/shard_map/all_gather | solution.py:429
  26.5 3.8 %shard_map.67 = (bf16[256,3072]{1,0:T(8,128)(2,1)S(1)}, f32[24,128]{1,0:T(8,128)S(1)}, f32[24,128]{1,0:T(8,128)S(1)}, bf16[1536,1024]{1,0:T(8,128)(2,1)S(1)}) custom-call(s32[1]{0:T(128)} %bitcast.1.refs_0_, s32[1]{0:T(128)} %bitcast.refs_1_.refs_0_, s32[2,6,16]{2,1,0:T(8,128)S(1)} %all-gather.1.refs_2_, bf16[1536,1024]{1,0:T(8,128)(2,1)} %refs_3_.1, ...), custom_call_target="tpu_custom_call" | custom-call | flops 1610612736 | bytes 7864320 | tf_op jit(solution)/shard_map/pallas_call | solution.py:197
  30.3 0.0 collective-permute-done.2.refs_5_
  30.3 0.0 collective-permute-done.3.refs_6_
  30.3 2.7 %collective-permute-done.4.refs_7_ = bf16[128,1024]{1,0:T(8,128)(2,1)} collective-permute-done((bf16[128,1024]{1,0:T(8,128)(2,1)S(1)}, bf16[128,1024]{1,0:T(8,128)(2,1)}, u32[]{:S(2)}, u32[]{:S(2)}) %collective-permute-start.4) | collective-permute-done | bytes 262176 | tf_op jit(solution)/shard_map/ppermute | solution.py:404
  33.0 4.6 %shard_map.68 = (bf16[384,3072]{1,0:T(8,128)(2,1)S(1)}, f32[24,128]{1,0:T(8,128)S(1)}, f32[8,32,128]{2,1,0:T(8,128)S(1)}) custom-call(s32[1]{0:T(128)} %bitcast.1.refs_0_, s32[1]{0:T(128)} %bitcast.refs_1_.refs_0_, s32[2,6,16]{2,1,0:T(8,128)S(1)} %all-gather.1.refs_2_, bf16[1536,1024]{1,0:T(8,128)(2,1)S(1)} %get-tuple-element.20.refs_3_.refs_2_, ...), custom_call_target="tpu_custom_call" | custom-call | flops 2415919104 | bytes 8650752 | tf_op jit(solution)/shard_map/pallas_call | solution.py:197
  37.7 11.0 %all_to_all.5.refs_1_ = f32[8,32,128]{2,1,0:T(8,128)S(1)} all-to-all(f32[8,32,128]{2,1,0:T(8,128)S(1)} %get-tuple-element.23), channel_id=1, replica_groups=mesh['chip'=64,'core'=2,'cen'=4] {'core','cen'}, dimensions={0} | all-to-all | bytes 262144 | tf_op jit(solution)/shard_map/all_to_all | solution.py:453
  48.7 2.5 %shard_map.70 = (bf16[1040,128]{1,0:T(8,128)(2,1)S(1)}, f32[128,1024]{1,0:T(8,128)S(1)}, f32[8,128]{1,0:T(8,128)S(1)}, f32[12,128]{1,0:T(8,128)}) custom-call(s32[1]{0:T(128)} %bitcast.refs_1_.refs_0_, f32[8,32,128]{2,1,0:T(8,128)S(1)} %all_to_all.5.refs_1_, bf16[1536,1024]{1,0:T(8,128)(2,1)S(1)} %get-tuple-element.20.refs_3_.refs_2_, ...), custom_call_target="tpu_custom_call" | custom-call | flops 1610612736 | bytes 7864320 | tf_op jit(solution)/shard_map/pallas_call | solution.py:338
  51.2 3.5 %collective-permute-start.7 = (bf16[1040,128]{1,0:T(8,128)(2,1)S(1)}, bf16[1040,128]{1,0:T(8,128)(2,1)S(1)}, u32[]{:S(2)}, u32[]{:S(2)}) collective-permute-start(bf16[1040,128]{1,0:T(8,128)(2,1)S(1)} %get-tuple-element.33), channel_id=1, source_target_pairs={{0,480},{8,488},{16,48},{24,56},{32,0},{40,8},{48,80},{56,88},{64,... | collective-permute-start | bytes 798728 | tf_op jit(solution)/shard_map/ppermute | solution.py:404
  54.7 2.9 %shard_map.69 = (bf16[1040,128]{1,0:T(8,128)(2,1)S(1)}, bf16[1040,128]{1,0:T(8,128)(2,1)S(1)}, f32[128,1024]{1,0:T(8,128)S(1)}, f32[8,128]{1,0:T(8,128)S(1)}) custom-call(s32[1]{0:T(128)} %bitcast.refs_1_.refs_0_, f32[8,32,128]{2,1,0:T(8,128)S(1)} %all_to_all.5.refs_1_, bf16[1536,1024]{1,0:T(8,128)(2,1)S(1)} %get-tuple-element.20.refs_3_.refs_2_, ...), custom_call_target="tpu_custom_call" | custom-call | flops 2415919104 | bytes 8650752 | tf_op jit(solution)/shard_map/pallas_call | solution.py:338
  57.6 2.6 %collective-permute-start.5 = (bf16[1040,128]{1,0:T(8,128)(2,1)S(1)}, bf16[1040,128]{1,0:T(8,128)(2,1)S(1)}, u32[]{:S(2)}, u32[]{:S(2)}) collective-permute-start(bf16[1040,128]{1,0:T(8,128)(2,1)S(1)} %get-tuple-element.29), channel_id=1, source_target_pairs={{0,8},{8,16},{16,24},{24,32},{32,40},{40,48},{48,56},{56,64},{64,7... | collective-permute-start | bytes 798728 | tf_op jit(solution)/shard_map/ppermute | solution.py:404
  60.2 6.0 %collective-permute-start.6 = (bf16[1040,128]{1,0:T(8,128)(2,1)S(1)}, bf16[1040,128]{1,0:T(8,128)(2,1)S(1)}, u32[]{:S(2)}, u32[]{:S(2)}) collective-permute-start(bf16[1040,128]{1,0:T(8,128)(2,1)S(1)} %get-tuple-element.30), channel_id=1, source_target_pairs={{0,504},{8,0},{16,8},{24,16},{32,24},{40,32},{48,40},{56,48},{64,5... | collective-permute-start | bytes 798728 | tf_op jit(solution)/shard_map/ppermute | solution.py:404
  66.2 0.1 shard_map.71
  66.3 1.9 %collective-permute-start.8 = (bf16[1040,128]{1,0:T(8,128)(2,1)S(1)}, bf16[1040,128]{1,0:T(8,128)(2,1)S(1)}, u32[]{:S(2)}, u32[]{:S(2)}) collective-permute-start(bf16[1040,128]{1,0:T(8,128)(2,1)S(1)} %shard_map.71), channel_id=1, source_target_pairs={{0,16},{8,24},{16,0},{24,8},{32,48},{40,56},{48,32},{56,40},{64,80... | collective-permute-start | bytes 798728 | tf_op jit(solution)/shard_map/ppermute | solution.py:404
  68.2 1.8 %collective-permute-done.5.refs_3_ = bf16[1040,128]{1,0:T(8,128)(2,1)S(1)} collective-permute-done((bf16[1040,128]{1,0:T(8,128)(2,1)S(1)}, bf16[1040,128]{1,0:T(8,128)(2,1)S(1)}, u32[]{:S(2)}, u32[]{:S(2)}) %collective-permute-start.5) | collective-permute-done | bytes 266272 | tf_op jit(solution)/shard_map/ppermute | solution.py:404
  70.1 1.7 %collective-permute-done.6.refs_4_ = bf16[1040,128]{1,0:T(8,128)(2,1)S(1)} collective-permute-done((bf16[1040,128]{1,0:T(8,128)(2,1)S(1)}, bf16[1040,128]{1,0:T(8,128)(2,1)S(1)}, u32[]{:S(2)}, u32[]{:S(2)}) %collective-permute-start.6) | collective-permute-done | bytes 266272 | tf_op jit(solution)/shard_map/ppermute | solution.py:404
  71.8 4.6 %collective-permute-done.8.refs_5_ = bf16[1040,128]{1,0:T(8,128)(2,1)S(1)} collective-permute-done((bf16[1040,128]{1,0:T(8,128)(2,1)S(1)}, bf16[1040,128]{1,0:T(8,128)(2,1)S(1)}, u32[]{:S(2)}, u32[]{:S(2)}) %collective-permute-start.8) | collective-permute-done | bytes 266272 | tf_op jit(solution)/shard_map/ppermute | solution.py:404
  76.3 0.9 %shard_map.72 = (bf16[128,1024]{1,0:T(8,128)(2,1)}, f32[2,64]{1,0:T(2,128)}) custom-call(f32[128,1024]{1,0:T(8,128)S(1)} %get-tuple-element.27.refs_0_, f32[8,128]{1,0:T(8,128)S(1)} %get-tuple-element.28.refs_1_, bf16[128,1024]{1,0:T(8,128)(2,1)S(1)} %bitcast.10, bf16[1040,128]{1,0:T(8,128)(2,1)S(1)} %collective-permute-done.5.refs_3_, ...), custom_call_target="tpu_custom_call" | custom-call | tf_op jit(solution)/shard_map/pallas_call | solution.py:383
  (6 shorter events, 0.0 us)
Async XLA Ops:
  0.6 25.9 %collective-permute-start = (bf16[1536,1024]{1,0:T(8,128)(2,1)}, bf16[1536,1024]{1,0:T(8,128)(2,1)S(1)}, u32[]{:S(2)}, u32[]{:S(2)}) collective-permute-start(bf16[1536,1024]{1,0:T(8,128)(2,1)} %refs_3_.1), channel_id=1, source_target_pairs={{0,4},{4,0},{1,5},{5,1},{2,6},{6,2},{3,7},{7,3},{8,12},{12,8},{9,1... | collective-permute-start | bytes 9437192 | tf_op jit(solution)/shard_map/ppermute | solution.py:422
  9.4 12.9 %collective-permute-start.1 = (bf16[128,1024]{1,0:T(8,128)(2,1)}, bf16[128,1024]{1,0:T(8,128)(2,1)S(1)}, u32[]{:S(2)}, u32[]{:S(2)}) collective-permute-start(bf16[128,1024]{1,0:T(8,128)(2,1)} %bitcast.6), channel_id=1, source_target_pairs={{0,16},{8,24},{16,0},{24,8},{32,48},{40,56},{48,32},{56,40},{64,80... | collective-permute-start | bytes 786440 | tf_op jit(solution)/shard_map/ppermute | solution.py:404
  11.4 18.9 %collective-permute-start.2 = (bf16[128,1024]{1,0:T(8,128)(2,1)}, bf16[128,1024]{1,0:T(8,128)(2,1)}, u32[]{:S(2)}, u32[]{:S(2)}) collective-permute-start(bf16[128,1024]{1,0:T(8,128)(2,1)} %bitcast.7), channel_id=1, source_target_pairs={{0,8},{8,16},{16,24},{24,32},{32,40},{40,48},{48,56},{56,64},{64,7... | collective-permute-start | bytes 786440 | tf_op jit(solution)/shard_map/ppermute | solution.py:404
  13.3 17.0 %collective-permute-start.3 = (bf16[128,1024]{1,0:T(8,128)(2,1)}, bf16[128,1024]{1,0:T(8,128)(2,1)}, u32[]{:S(2)}, u32[]{:S(2)}) collective-permute-start(bf16[128,1024]{1,0:T(8,128)(2,1)} %bitcast.8), channel_id=1, source_target_pairs={{0,504},{8,0},{16,8},{24,16},{32,24},{40,32},{48,40},{56,48},{64,5... | collective-permute-start | bytes 786440 | tf_op jit(solution)/shard_map/ppermute | solution.py:404
  22.4 10.7 %collective-permute-start.4 = (bf16[128,1024]{1,0:T(8,128)(2,1)S(1)}, bf16[128,1024]{1,0:T(8,128)(2,1)}, u32[]{:S(2)}, u32[]{:S(2)}) collective-permute-start(bf16[128,1024]{1,0:T(8,128)(2,1)S(1)} %collective-permute-done.1.refs_5_), channel_id=1, source_target_pairs={{0,32},{8,40},{16,496},{24,504},{32,64},{40,72},{48,16},{56,24},{6... | collective-permute-start | bytes 786440 | tf_op jit(solution)/shard_map/ppermute | solution.py:404
  26.5 6.5 %copy-start.1 = (s32[6]{0:T(128)S(1)}, s32[6]{0:T(128)}, u32[]{:S(2)}) copy-start(s32[6]{0:T(128)} %refs_10_.1) | copy-start | bytes 76
  51.2 25.2 %copy-start = (bf16[2,64,1024]{2,1,0:T(8,128)(2,1)S(1)}, bf16[2,64,1024]{2,1,0:T(8,128)(2,1)}, u32[]{:S(2)}) copy-start(bf16[2,64,1024]{2,1,0:T(8,128)(2,1)} %param.7) | copy-start | bytes 786436
  51.2 15.0 %collective-permute-start.7 = (bf16[1040,128]{1,0:T(8,128)(2,1)S(1)}, bf16[1040,128]{1,0:T(8,128)(2,1)S(1)}, u32[]{:S(2)}, u32[]{:S(2)}) collective-permute-start(bf16[1040,128]{1,0:T(8,128)(2,1)S(1)} %get-tuple-element.33), channel_id=1, source_target_pairs={{0,480},{8,488},{16,48},{24,56},{32,0},{40,8},{48,80},{56,88},{64,... | collective-permute-start | bytes 798728 | tf_op jit(solution)/shard_map/ppermute | solution.py:404
  57.6 12.5 %collective-permute-start.5 = (bf16[1040,128]{1,0:T(8,128)(2,1)S(1)}, bf16[1040,128]{1,0:T(8,128)(2,1)S(1)}, u32[]{:S(2)}, u32[]{:S(2)}) collective-permute-start(bf16[1040,128]{1,0:T(8,128)(2,1)S(1)} %get-tuple-element.29), channel_id=1, source_target_pairs={{0,8},{8,16},{16,24},{24,32},{32,40},{40,48},{48,56},{56,64},{64,7... | collective-permute-start | bytes 798728 | tf_op jit(solution)/shard_map/ppermute | solution.py:404
  60.2 11.6 %collective-permute-start.6 = (bf16[1040,128]{1,0:T(8,128)(2,1)S(1)}, bf16[1040,128]{1,0:T(8,128)(2,1)S(1)}, u32[]{:S(2)}, u32[]{:S(2)}) collective-permute-start(bf16[1040,128]{1,0:T(8,128)(2,1)S(1)} %get-tuple-element.30), channel_id=1, source_target_pairs={{0,504},{8,0},{16,8},{24,16},{32,24},{40,32},{48,40},{56,48},{64,5... | collective-permute-start | bytes 798728 | tf_op jit(solution)/shard_map/ppermute | solution.py:404
  66.3 10.0 %collective-permute-start.8 = (bf16[1040,128]{1,0:T(8,128)(2,1)S(1)}, bf16[1040,128]{1,0:T(8,128)(2,1)S(1)}, u32[]{:S(2)}, u32[]{:S(2)}) collective-permute-start(bf16[1040,128]{1,0:T(8,128)(2,1)S(1)} %shard_map.71), channel_id=1, source_target_pairs={{0,16},{8,24},{16,0},{24,8},{32,48},{40,56},{48,32},{56,40},{64,80... | collective-permute-start | bytes 798728 | tf_op jit(solution)/shard_map/ppermute | solution.py:404

commit v4 on v3

--- a/solution.py
+++ b/solution.py
@@ -308,7 +308,7 @@
         else:
             total_ref[...] += part
 
-    for out, n in zip(outs, (*sent, keep)):
+    for out, n in zip(outs, sent if keep is None else (*sent, keep)):
         rows = slice(n * size, (n + 1) * size)
         mass = jnp.sum(jnp.transpose(mass_ref[rows, :]), 0, keepdims=True)
         mass = jnp.broadcast_to(mass, (8, size))
@@ -325,10 +325,11 @@
     groups = 2 * half // LANES
     message = (D // LANES * size + 16, LANES)
     out_shape = [jax.ShapeDtypeStruct(message, jnp.bfloat16)] * len(sent)
-    out_shape += [
-        jax.ShapeDtypeStruct((size, D), jnp.float32),
-        jax.ShapeDtypeStruct((8, size), jnp.float32),
-    ]
+    if keep is not None:
+        out_shape += [
+            jax.ShapeDtypeStruct((size, D), jnp.float32),
+            jax.ShapeDtypeStruct((8, size), jnp.float32),
+        ]
     if first:
         out_shape += [jax.ShapeDtypeStruct((half // LANES, LANES), jnp.float32)]
 
@@ -429,38 +430,41 @@
     candidates = lax.all_gather(candidates, "core")
 
     first_power, first_max, first_sum, kept = score(
-        ("row", "own"),
+        ("row", "before", "own"),
         chips,
         chip,
         core,
         candidates,
         [pltpu.with_memory_space_constraint(points, pltpu.HBM), other],
-        [row, pltpu.with_memory_space_constraint(centre, pltpu.HBM)],
+        [row, near[0], pltpu.with_memory_space_constraint(centre, pltpu.HBM)],
         local_blocks,
     )
     points = [kept, other]
     last_power, last_max, message = score(
-        ("before", "after", "beyond"),
+        ("after", "beyond"),
         chips,
         chip,
         core,
         candidates,
         points,
-        [*near, beyond],
+        [near[1], beyond],
         local_blocks,
         ((first_max, first_sum), lengths, copies),
     )
     everyone = lax.all_to_all(message, ("core", "cen"), 0, 0)
     tops, powers = (first_max, last_max), (first_power, last_power)
-    beyond, row, row_mass, lse = moments(
-        core, everyone, points, tops, powers, ((1, 2 * size), (0, 0)), size, (0,), 1, True
+    beyond, lse = moments(
+        core, everyone, points, tops, powers, ((1, size),), size, (0,), None, True
     )
     beyond = moved(beyond, inward)
-    before, after, home, home_mass = moments(
-        core, everyone, points, tops, powers, ((1, 0), (1, size), (0, size)), size, (0, 1), 2, False
+    before, after, row, row_mass = moments(
+        core, everyone, points, tops, powers, ((0, size), (1, 0), (0, 0)), size, (0, 1), 2, False
     )
     arrived = [moved(after, ahead), moved(before, back)]
     arrived += [moved(merged(row, row_mass, beyond), across)]
+    home, home_mass = moments(
+        core, everyone, points, tops, powers, ((0, 2 * size),), size, (), 0, False
+    )
     updated, masses = finish(home, home_mass, centre, arrived, local_blocks)
     return updated.reshape(centroids.shape), masses, lse.reshape(-1)
 

time: 77.8 us -> 76.8 us (0.987)
  waiting for transfers between devices: 10.8 us -> 7.88 us
  Pallas kernels: 14.8 us -> 15.9 us
  starting transfers between devices: 37.6 us -> 38.5 us
    ppermute x8, waiting for transfers between devices: 10.8 us -> 7.88 us  [moved(): lax.ppermute(value, 'chip', [(c, step(c) % chips) for c in range(chips)])]
    ppermute x8, starting transfers between devices: 28.8 us -> 29.7 us  [moved(): lax.ppermute(value, 'chip', [(c, step(c) % chips) for c in range(chips)])]
    pallas_call x2, Pallas kernels: 8.38 us -> 9.21 us  [score(): pl.pallas_call(kernel, in_specs=in_specs, out_specs=[VMEM] * len(out_shap...]
    pallas_call x2 -> x3, Pallas kernels: 5.44 us -> 5.7 us  [moments(): pl.pallas_call(kernel, in_specs=[SMEM] + [VMEM] * 7, out_specs=[VMEM] * l...]
  transfers between devices with their start and end apart: 9 -> 9, of which waited for: 4 -> 5; matrix products, arithmetic and copies ran while one was open for 0% -> 0% of each run, Pallas kernels for 9% -> 13%
where the time goes in v4:
time: 76.8 us; the launch traced here: 76.4 us
  starting transfers between devices  38.5 us (50%)
  Pallas kernels  15.9 us (21%)
  blocking collectives  13.4 us (17%)
  waiting for transfers between devices  7.88 us (10%)
  between operations  0.77 us (1%)
    ppermute x8, starting transfers between devices, moved(): lax.ppermute(value, 'chip', [(c, step(c) % chips) for c in range(chips)])  29.7 us
    all_to_all x1, blocking collectives, local(): everyone = lax.all_to_all(message, ('core', 'cen'), 0, 0)  11.2 us
    pallas_call x2, Pallas kernels, score(): pl.pallas_call(kernel, in_specs=in_specs, out_specs=[VMEM] * len(out_shap...  9.21 us
    ppermute x1, starting transfers between devices, swapped(): return lax.ppermute(value, 'core', [(0, 1), (1, 0)])  8.79 us
    ppermute x8, waiting for transfers between devices, moved(): lax.ppermute(value, 'chip', [(c, step(c) % chips) for c in range(chips)])  7.88 us
    pallas_call x3, Pallas kernels, moments(): pl.pallas_call(kernel, in_specs=[SMEM] + [VMEM] * 7, out_specs=[VMEM] * l...  5.7 us
    all_gather x1, blocking collectives, local(): candidates = lax.all_gather(candidates, 'core')  2.2 us
  transfers between devices with their start and end apart: 9, of which 5 were waited for; matrix products, arithmetic and copies ran while one was open for 0% of the time, Pallas kernels for 13%

profile of v4, /device:TPU:1, one launch (start us, length us, event | category | flops | bytes accessed | tf_op | source)
XLA Modules:
  0.0 76.4 jit_solution(11518764872680806249)
XLA Ops:
  0.6 8.8 %collective-permute-start = (bf16[1536,1024]{1,0:T(8,128)(2,1)}, bf16[1536,1024]{1,0:T(8,128)(2,1)S(1)}, u32[]{:S(2)}, u32[]{:S(2)}) collective-permute-start(bf16[1536,1024]{1,0:T(8,128)(2,1)} %refs_3_.1), channel_id=1, source_target_pairs={{0,4},{4,0},{1,5},{5,1},{2,6},{6,2},{3,7},{7,3},{8,12},{12,8},{9,1... | collective-permute-start | bytes 9437192 | tf_op jit(solution)/shard_map/ppermute | solution.py:423
  9.4 1.9 %collective-permute-start.1 = (bf16[128,1024]{1,0:T(8,128)(2,1)}, bf16[128,1024]{1,0:T(8,128)(2,1)}, u32[]{:S(2)}, u32[]{:S(2)}) collective-permute-start(bf16[128,1024]{1,0:T(8,128)(2,1)} %bitcast.6), channel_id=1, source_target_pairs={{0,16},{8,24},{16,0},{24,8},{32,48},{40,56},{48,32},{56,40},{64,80... | collective-permute-start | bytes 786440 | tf_op jit(solution)/shard_map/ppermute | solution.py:405
  11.4 1.9 %collective-permute-start.2 = (bf16[128,1024]{1,0:T(8,128)(2,1)}, bf16[128,1024]{1,0:T(8,128)(2,1)}, u32[]{:S(2)}, u32[]{:S(2)}) collective-permute-start(bf16[128,1024]{1,0:T(8,128)(2,1)} %bitcast.7), channel_id=1, source_target_pairs={{0,8},{8,16},{16,24},{24,32},{32,40},{40,48},{48,56},{56,64},{64,7... | collective-permute-start | bytes 786440 | tf_op jit(solution)/shard_map/ppermute | solution.py:405
  13.3 9.1 %collective-permute-start.3 = (bf16[128,1024]{1,0:T(8,128)(2,1)}, bf16[128,1024]{1,0:T(8,128)(2,1)S(1)}, u32[]{:S(2)}, u32[]{:S(2)}) collective-permute-start(bf16[128,1024]{1,0:T(8,128)(2,1)} %bitcast.8), channel_id=1, source_target_pairs={{0,504},{8,0},{16,8},{24,16},{32,24},{40,32},{48,40},{56,48},{64,5... | collective-permute-start | bytes 786440 | tf_op jit(solution)/shard_map/ppermute | solution.py:405
  22.4 1.9 %collective-permute-start.4 = (bf16[128,1024]{1,0:T(8,128)(2,1)}, bf16[128,1024]{1,0:T(8,128)(2,1)}, u32[]{:S(2)}, u32[]{:S(2)}) collective-permute-start(bf16[128,1024]{1,0:T(8,128)(2,1)} %collective-permute-done.1.refs_5_), channel_id=1, source_target_pairs={{0,32},{8,40},{16,496},{24,504},{32,64},{40,72},{48,16},{56,24},{6... | collective-permute-start | bytes 786440 | tf_op jit(solution)/shard_map/ppermute | solution.py:405
  24.3 2.2 %all-gather.1.refs_2_ = s32[2,6,16]{2,1,0:T(8,128)S(1)} all-gather(s32[1,6,16]{2,1,0:T(8,128)} %bitcast.11), channel_id=2, replica_groups=mesh['chip'=64,'core'=2,'cen'=4] {'core'}, dimensions={0}, use_global_device_ids=true | all-gather | bytes 1152 | tf_op jit(solution)/shard_map/all_gather | solution.py:430
  26.5 0.7 collective-permute-done.2.refs_6_
  27.2 5.7 %shard_map.67 = (bf16[384,3072]{1,0:T(8,128)(2,1)S(1)}, f32[24,128]{1,0:T(8,128)S(1)}, f32[24,128]{1,0:T(8,128)S(1)}, bf16[1536,1024]{1,0:T(8,128)(2,1)S(1)}) custom-call(s32[1]{0:T(128)} %bitcast.1.refs_0_, s32[1]{0:T(128)} %bitcast.refs_1_.refs_0_, s32[2,6,16]{2,1,0:T(8,128)S(1)} %all-gather.1.refs_2_, bf16[1536,1024]{1,0:T(8,128)(2,1)} %refs_3_.1, ...), custom_call_target="tpu_custom_call" | custom-call | flops 2415919104 | bytes 8650752 | tf_op jit(solution)/shard_map/pallas_call | solution.py:197
  32.9 0.2 collective-permute-done.4.refs_6_
  33.1 3.5 %shard_map.68 = (bf16[256,3072]{1,0:T(8,128)(2,1)S(1)}, f32[24,128]{1,0:T(8,128)S(1)}, f32[8,32,128]{2,1,0:T(8,128)S(1)}) custom-call(s32[1]{0:T(128)} %bitcast.1.refs_0_, s32[1]{0:T(128)} %bitcast.refs_1_.refs_0_, s32[2,6,16]{2,1,0:T(8,128)S(1)} %all-gather.1.refs_2_, bf16[1536,1024]{1,0:T(8,128)(2,1)S(1)} %get-tuple-element.20.refs_3_.refs_2_, ...), custom_call_target="tpu_custom_call" | custom-call | flops 1610612736 | bytes 7864320 | tf_op jit(solution)/shard_map/pallas_call | solution.py:197
  36.6 11.2 %all_to_all.5.refs_1_ = f32[8,32,128]{2,1,0:T(8,128)S(1)} all-to-all(f32[8,32,128]{2,1,0:T(8,128)S(1)} %get-tuple-element.23), channel_id=1, replica_groups=mesh['chip'=64,'core'=2,'cen'=4] {'core','cen'}, dimensions={0} | all-to-all | bytes 262144 | tf_op jit(solution)/shard_map/all_to_all | solution.py:454
  47.8 1.6 %shard_map.71 = (bf16[1040,128]{1,0:T(8,128)(2,1)S(1)}, f32[12,128]{1,0:T(8,128)}) custom-call(s32[1]{0:T(128)} %bitcast.refs_1_.refs_0_, f32[8,32,128]{2,1,0:T(8,128)S(1)} %all_to_all.5.refs_1_, bf16[1536,1024]{1,0:T(8,128)(2,1)S(1)} %get-tuple-element.20.refs_3_.refs_2_, bf16[1536,1024]{1,0:T(8,128)(2,1)S(1)} %collective-permute-done.refs_4_.refs_3_, ...), custom_call_target="tpu_custom_call" | custom-call | flops 805306368 | bytes 7077888 | tf_op jit(solution)/shard_map/pallas_call | solution.py:339
  49.4 4.2 %collective-permute-start.7 = (bf16[1040,128]{1,0:T(8,128)(2,1)S(1)}, bf16[1040,128]{1,0:T(8,128)(2,1)S(1)}, u32[]{:S(2)}, u32[]{:S(2)}) collective-permute-start(bf16[1040,128]{1,0:T(8,128)(2,1)S(1)} %get-tuple-element.33), channel_id=1, source_target_pairs={{0,480},{8,488},{16,48},{24,56},{32,0},{40,8},{48,80},{56,88},{64,... | collective-permute-start | bytes 798728 | tf_op jit(solution)/shard_map/ppermute | solution.py:405
  53.6 3.0 %shard_map.70 = (bf16[1040,128]{1,0:T(8,128)(2,1)S(1)}, bf16[1040,128]{1,0:T(8,128)(2,1)S(1)}, f32[128,1024]{1,0:T(8,128)S(1)}, f32[8,128]{1,0:T(8,128)S(1)}) custom-call(s32[1]{0:T(128)} %bitcast.refs_1_.refs_0_, f32[8,32,128]{2,1,0:T(8,128)S(1)} %all_to_all.5.refs_1_, bf16[1536,1024]{1,0:T(8,128)(2,1)S(1)} %get-tuple-element.20.refs_3_.refs_2_, ...), custom_call_target="tpu_custom_call" | custom-call | flops 2415919104 | bytes 8650752 | tf_op jit(solution)/shard_map/pallas_call | solution.py:339
  56.6 3.2 %collective-permute-start.5 = (bf16[1040,128]{1,0:T(8,128)(2,1)S(1)}, bf16[1040,128]{1,0:T(8,128)(2,1)S(1)}, u32[]{:S(2)}, u32[]{:S(2)}) collective-permute-start(bf16[1040,128]{1,0:T(8,128)(2,1)S(1)} %get-tuple-element.29), channel_id=1, source_target_pairs={{0,8},{8,16},{16,24},{24,32},{32,40},{40,48},{48,56},{56,64},{64,7... | collective-permute-start | bytes 798728 | tf_op jit(solution)/shard_map/ppermute | solution.py:405
  59.7 5.4 %collective-permute-start.6 = (bf16[1040,128]{1,0:T(8,128)(2,1)S(1)}, bf16[1040,128]{1,0:T(8,128)(2,1)S(1)}, u32[]{:S(2)}, u32[]{:S(2)}) collective-permute-start(bf16[1040,128]{1,0:T(8,128)(2,1)S(1)} %get-tuple-element.30), channel_id=1, source_target_pairs={{0,504},{8,0},{16,8},{24,16},{32,24},{40,32},{48,40},{56,48},{64,5... | collective-permute-start | bytes 798728 | tf_op jit(solution)/shard_map/ppermute | solution.py:405
  65.2 0.1 shard_map.72
  65.3 0.0 copy-start
  65.3 2.1 %collective-permute-start.8 = (bf16[1040,128]{1,0:T(8,128)(2,1)S(1)}, bf16[1040,128]{1,0:T(8,128)(2,1)S(1)}, u32[]{:S(2)}, u32[]{:S(2)}) collective-permute-start(bf16[1040,128]{1,0:T(8,128)(2,1)S(1)} %shard_map.72), channel_id=1, source_target_pairs={{0,16},{8,24},{16,0},{24,8},{32,48},{40,56},{48,32},{56,40},{64,80... | collective-permute-start | bytes 798728 | tf_op jit(solution)/shard_map/ppermute | solution.py:405
  67.3 1.1 %shard_map.69 = (f32[128,1024]{1,0:T(8,128)S(1)}, f32[8,128]{1,0:T(8,128)S(1)}) custom-call(s32[1]{0:T(128)} %bitcast.refs_1_.refs_0_, f32[8,32,128]{2,1,0:T(8,128)S(1)} %all_to_all.5.refs_1_, bf16[1536,1024]{1,0:T(8,128)(2,1)S(1)} %get-tuple-element.20.refs_3_.refs_2_, bf16[1536,1024]{1,0:T(8,128)(2,1)S(1)} %collective-permute-done.refs_4_.refs_3_, ...), custom_call_target="tpu_custom_call" | custom-call | flops 805306368 | bytes 7077888 | tf_op jit(solution)/shard_map/pallas_call | solution.py:339
  68.4 0.6 collective-permute-done.5.refs_3_
  69.0 1.3 %collective-permute-done.6.refs_4_ = bf16[1040,128]{1,0:T(8,128)(2,1)S(1)} collective-permute-done((bf16[1040,128]{1,0:T(8,128)(2,1)S(1)}, bf16[1040,128]{1,0:T(8,128)(2,1)S(1)}, u32[]{:S(2)}, u32[]{:S(2)}) %collective-permute-start.6) | collective-permute-done | bytes 266272 | tf_op jit(solution)/shard_map/ppermute | solution.py:405
  70.3 5.1 %collective-permute-done.8.refs_5_ = bf16[1040,128]{1,0:T(8,128)(2,1)S(1)} collective-permute-done((bf16[1040,128]{1,0:T(8,128)(2,1)S(1)}, bf16[1040,128]{1,0:T(8,128)(2,1)S(1)}, u32[]{:S(2)}, u32[]{:S(2)}) %collective-permute-start.8) | collective-permute-done | bytes 266272 | tf_op jit(solution)/shard_map/ppermute | solution.py:405
  75.4 0.9 %shard_map.73 = (bf16[128,1024]{1,0:T(8,128)(2,1)}, f32[2,64]{1,0:T(2,128)}) custom-call(f32[128,1024]{1,0:T(8,128)S(1)} %get-tuple-element.27.refs_0_, f32[8,128]{1,0:T(8,128)S(1)} %get-tuple-element.28.refs_1_, bf16[128,1024]{1,0:T(8,128)(2,1)S(1)} %bitcast.10, bf16[1040,128]{1,0:T(8,128)(2,1)S(1)} %collective-permute-done.5.refs_3_, ...), custom_call_target="tpu_custom_call" | custom-call | tf_op jit(solution)/shard_map/pallas_call | solution.py:384
  (7 shorter events, 0.0 us)
Async XLA Ops:
  0.6 26.6 %collective-permute-start = (bf16[1536,1024]{1,0:T(8,128)(2,1)}, bf16[1536,1024]{1,0:T(8,128)(2,1)S(1)}, u32[]{:S(2)}, u32[]{:S(2)}) collective-permute-start(bf16[1536,1024]{1,0:T(8,128)(2,1)} %refs_3_.1), channel_id=1, source_target_pairs={{0,4},{4,0},{1,5},{5,1},{2,6},{6,2},{3,7},{7,3},{8,12},{12,8},{9,1... | collective-permute-start | bytes 9437192 | tf_op jit(solution)/shard_map/ppermute | solution.py:423
  9.4 12.9 %collective-permute-start.1 = (bf16[128,1024]{1,0:T(8,128)(2,1)}, bf16[128,1024]{1,0:T(8,128)(2,1)}, u32[]{:S(2)}, u32[]{:S(2)}) collective-permute-start(bf16[128,1024]{1,0:T(8,128)(2,1)} %bitcast.6), channel_id=1, source_target_pairs={{0,16},{8,24},{16,0},{24,8},{32,48},{40,56},{48,32},{56,40},{64,80... | collective-permute-start | bytes 786440 | tf_op jit(solution)/shard_map/ppermute | solution.py:405
  11.4 15.8 %collective-permute-start.2 = (bf16[128,1024]{1,0:T(8,128)(2,1)}, bf16[128,1024]{1,0:T(8,128)(2,1)}, u32[]{:S(2)}, u32[]{:S(2)}) collective-permute-start(bf16[128,1024]{1,0:T(8,128)(2,1)} %bitcast.7), channel_id=1, source_target_pairs={{0,8},{8,16},{16,24},{24,32},{32,40},{40,48},{48,56},{56,64},{64,7... | collective-permute-start | bytes 786440 | tf_op jit(solution)/shard_map/ppermute | solution.py:405
  13.3 19.6 %collective-permute-start.3 = (bf16[128,1024]{1,0:T(8,128)(2,1)}, bf16[128,1024]{1,0:T(8,128)(2,1)S(1)}, u32[]{:S(2)}, u32[]{:S(2)}) collective-permute-start(bf16[128,1024]{1,0:T(8,128)(2,1)} %bitcast.8), channel_id=1, source_target_pairs={{0,504},{8,0},{16,8},{24,16},{32,24},{40,32},{48,40},{56,48},{64,5... | collective-permute-start | bytes 786440 | tf_op jit(solution)/shard_map/ppermute | solution.py:405
  22.4 10.7 %collective-permute-start.4 = (bf16[128,1024]{1,0:T(8,128)(2,1)}, bf16[128,1024]{1,0:T(8,128)(2,1)}, u32[]{:S(2)}, u32[]{:S(2)}) collective-permute-start(bf16[128,1024]{1,0:T(8,128)(2,1)} %collective-permute-done.1.refs_5_), channel_id=1, source_target_pairs={{0,32},{8,40},{16,496},{24,504},{32,64},{40,72},{48,16},{56,24},{6... | collective-permute-start | bytes 786440 | tf_op jit(solution)/shard_map/ppermute | solution.py:405
  27.2 5.9 %copy-start.1 = (s32[6]{0:T(128)S(1)}, s32[6]{0:T(128)}, u32[]{:S(2)}) copy-start(s32[6]{0:T(128)} %refs_9_.1) | copy-start | bytes 76
  49.4 15.8 %collective-permute-start.7 = (bf16[1040,128]{1,0:T(8,128)(2,1)S(1)}, bf16[1040,128]{1,0:T(8,128)(2,1)S(1)}, u32[]{:S(2)}, u32[]{:S(2)}) collective-permute-start(bf16[1040,128]{1,0:T(8,128)(2,1)S(1)} %get-tuple-element.33), channel_id=1, source_target_pairs={{0,480},{8,488},{16,48},{24,56},{32,0},{40,8},{48,80},{56,88},{64,... | collective-permute-start | bytes 798728 | tf_op jit(solution)/shard_map/ppermute | solution.py:405
  56.6 12.5 %collective-permute-start.5 = (bf16[1040,128]{1,0:T(8,128)(2,1)S(1)}, bf16[1040,128]{1,0:T(8,128)(2,1)S(1)}, u32[]{:S(2)}, u32[]{:S(2)}) collective-permute-start(bf16[1040,128]{1,0:T(8,128)(2,1)S(1)} %get-tuple-element.29), channel_id=1, source_target_pairs={{0,8},{8,16},{16,24},{24,32},{32,40},{40,48},{48,56},{56,64},{64,7... | collective-permute-start | bytes 798728 | tf_op jit(solution)/shard_map/ppermute | solution.py:405
  59.7 10.6 %collective-permute-start.6 = (bf16[1040,128]{1,0:T(8,128)(2,1)S(1)}, bf16[1040,128]{1,0:T(8,128)(2,1)S(1)}, u32[]{:S(2)}, u32[]{:S(2)}) collective-permute-start(bf16[1040,128]{1,0:T(8,128)(2,1)S(1)} %get-tuple-element.30), channel_id=1, source_target_pairs={{0,504},{8,0},{16,8},{24,16},{32,24},{40,32},{48,40},{56,48},{64,5... | collective-permute-start | bytes 798728 | tf_op jit(solution)/shard_map/ppermute | solution.py:405
  65.3 10.2 %copy-start = (bf16[2,64,1024]{2,1,0:T(8,128)(2,1)S(1)}, bf16[2,64,1024]{2,1,0:T(8,128)(2,1)}, u32[]{:S(2)}) copy-start(bf16[2,64,1024]{2,1,0:T(8,128)(2,1)} %param.7) | copy-start | bytes 786436
  65.3 10.2 %collective-permute-start.8 = (bf16[1040,128]{1,0:T(8,128)(2,1)S(1)}, bf16[1040,128]{1,0:T(8,128)(2,1)S(1)}, u32[]{:S(2)}, u32[]{:S(2)}) collective-permute-start(bf16[1040,128]{1,0:T(8,128)(2,1)S(1)} %shard_map.72), channel_id=1, source_target_pairs={{0,16},{8,24},{16,0},{24,8},{32,48},{40,56},{48,32},{56,40},{64,80... | collective-permute-start | bytes 798728 | tf_op jit(solution)/shard_map/ppermute | solution.py:405

commit v5 on v4

--- a/solution.py
+++ b/solution.py
@@ -424,46 +424,46 @@
 
     centre = centroids.reshape(size, D)
     row = moved(centre, across)
-    near = [moved(centre, ahead), moved(centre, back)]
+    near = [moved(centre, back), moved(centre, ahead)]
     beyond = moved(row, outward)
     other = swapped(points)
     candidates = lax.all_gather(candidates, "core")
 
     first_power, first_max, first_sum, kept = score(
-        ("row", "before", "own"),
+        ("row", "own"),
         chips,
         chip,
         core,
         candidates,
         [pltpu.with_memory_space_constraint(points, pltpu.HBM), other],
-        [row, near[0], pltpu.with_memory_space_constraint(centre, pltpu.HBM)],
+        [row, pltpu.with_memory_space_constraint(centre, pltpu.HBM)],
         local_blocks,
     )
     points = [kept, other]
     last_power, last_max, message = score(
-        ("after", "beyond"),
+        ("after", "before", "beyond"),
         chips,
         chip,
         core,
         candidates,
         points,
-        [near[1], beyond],
+        [*near, beyond],
         local_blocks,
         ((first_max, first_sum), lengths, copies),
     )
     everyone = lax.all_to_all(message, ("core", "cen"), 0, 0)
     tops, powers = (first_max, last_max), (first_power, last_power)
     beyond, lse = moments(
-        core, everyone, points, tops, powers, ((1, size),), size, (0,), None, True
+        core, everyone, points, tops, powers, ((1, 2 * size),), size, (0,), None, True
     )
     beyond = moved(beyond, inward)
-    before, after, row, row_mass = moments(
-        core, everyone, points, tops, powers, ((0, size), (1, 0), (0, 0)), size, (0, 1), 2, False
+    after, before, row, row_mass = moments(
+        core, everyone, points, tops, powers, ((1, 0), (1, size), (0, 0)), size, (0, 1), 2, False
     )
     arrived = [moved(after, ahead), moved(before, back)]
     arrived += [moved(merged(row, row_mass, beyond), across)]
     home, home_mass = moments(
-        core, everyone, points, tops, powers, ((0, 2 * size),), size, (), 0, False
+        core, everyone, points, tops, powers, ((0, size),), size, (), 0, False
     )
     updated, masses = finish(home, home_mass, centre, arrived, local_blocks)
     return updated.reshape(centroids.shape), masses, lse.reshape(-1)

time: 76.8 us -> 76.8 us (level)
  waiting for transfers between devices: 7.88 us -> 9.96 us
  starting transfers between devices: 38.5 us -> 37 us
  Pallas kernels: 15.9 us -> 15 us
    ppermute x8, waiting for transfers between devices: 7.88 us -> 9.96 us  [moved(): lax.ppermute(value, 'chip', [(c, step(c) % chips) for c in range(chips)])]
    ppermute x8, starting transfers between devices: 29.7 us -> 28.2 us  [moved(): lax.ppermute(value, 'chip', [(c, step(c) % chips) for c in range(chips)])]
    pallas_call x2, Pallas kernels: 9.21 us -> 8.39 us  [score(): pl.pallas_call(kernel, in_specs=in_specs, out_specs=[VMEM] * len(out_shap...]
  transfers between devices with their start and end apart: 9 -> 9, of which waited for: 5 -> 4; matrix products, arithmetic and copies ran while one was open for 0% -> 0% of each run, Pallas kernels for 13% -> 10%
where the time goes in v5:
time: 76.8 us; the launch traced here: 75.8 us
  starting transfers between devices  37 us (48%)
  Pallas kernels  15 us (20%)
  blocking collectives  13.1 us (17%)
  waiting for transfers between devices  9.96 us (13%)
  between operations  0.77 us (1%)
    ppermute x8, starting transfers between devices, moved(): lax.ppermute(value, 'chip', [(c, step(c) % chips) for c in range(chips)])  28.2 us
    all_to_all x1, blocking collectives, local(): everyone = lax.all_to_all(message, ('core', 'cen'), 0, 0)  10.9 us
    ppermute x8, waiting for transfers between devices, moved(): lax.ppermute(value, 'chip', [(c, step(c) % chips) for c in range(chips)])  9.96 us
    ppermute x1, starting transfers between devices, swapped(): return lax.ppermute(value, 'core', [(0, 1), (1, 0)])  8.79 us
    pallas_call x2, Pallas kernels, score(): pl.pallas_call(kernel, in_specs=in_specs, out_specs=[VMEM] * len(out_shap...  8.39 us
    pallas_call x3, Pallas kernels, moments(): pl.pallas_call(kernel, in_specs=[SMEM] + [VMEM] * 7, out_specs=[VMEM] * l...  5.65 us
    all_gather x1, blocking collectives, local(): candidates = lax.all_gather(candidates, 'core')  2.2 us
  transfers between devices with their start and end apart: 9, of which 4 were waited for; matrix products, arithmetic and copies ran while one was open for 0% of the time, Pallas kernels for 10%

profile of v5, /device:TPU:1, one launch (start us, length us, event | category | flops | bytes accessed | tf_op | source)
XLA Modules:
  0.0 75.8 jit_solution(15192711768182611684)
XLA Ops:
  0.6 8.8 %collective-permute-start = (bf16[1536,1024]{1,0:T(8,128)(2,1)}, bf16[1536,1024]{1,0:T(8,128)(2,1)S(1)}, u32[]{:S(2)}, u32[]{:S(2)}) collective-permute-start(bf16[1536,1024]{1,0:T(8,128)(2,1)} %refs_3_.1), channel_id=1, source_target_pairs={{0,4},{4,0},{1,5},{5,1},{2,6},{6,2},{3,7},{7,3},{8,12},{12,8},{9,1... | collective-permute-start | bytes 9437192 | tf_op jit(solution)/shard_map/ppermute | solution.py:423
  9.4 1.9 %collective-permute-start.1 = (bf16[128,1024]{1,0:T(8,128)(2,1)}, bf16[128,1024]{1,0:T(8,128)(2,1)S(1)}, u32[]{:S(2)}, u32[]{:S(2)}) collective-permute-start(bf16[128,1024]{1,0:T(8,128)(2,1)} %bitcast.6), channel_id=1, source_target_pairs={{0,16},{8,24},{16,0},{24,8},{32,48},{40,56},{48,32},{56,40},{64,80... | collective-permute-start | bytes 786440 | tf_op jit(solution)/shard_map/ppermute | solution.py:405
  11.4 9.1 %collective-permute-start.2 = (bf16[128,1024]{1,0:T(8,128)(2,1)}, bf16[128,1024]{1,0:T(8,128)(2,1)}, u32[]{:S(2)}, u32[]{:S(2)}) collective-permute-start(bf16[128,1024]{1,0:T(8,128)(2,1)} %bitcast.7), channel_id=1, source_target_pairs={{0,504},{8,0},{16,8},{24,16},{32,24},{40,32},{48,40},{56,48},{64,5... | collective-permute-start | bytes 786440 | tf_op jit(solution)/shard_map/ppermute | solution.py:405
  20.4 1.9 %collective-permute-start.3 = (bf16[128,1024]{1,0:T(8,128)(2,1)}, bf16[128,1024]{1,0:T(8,128)(2,1)}, u32[]{:S(2)}, u32[]{:S(2)}) collective-permute-start(bf16[128,1024]{1,0:T(8,128)(2,1)} %bitcast.8), channel_id=1, source_target_pairs={{0,8},{8,16},{16,24},{24,32},{32,40},{40,48},{48,56},{56,64},{64,7... | collective-permute-start | bytes 786440 | tf_op jit(solution)/shard_map/ppermute | solution.py:405
  22.4 0.0 collective-permute-done.1.refs_5_
  22.4 1.9 %collective-permute-start.4 = (bf16[128,1024]{1,0:T(8,128)(2,1)S(1)}, bf16[128,1024]{1,0:T(8,128)(2,1)}, u32[]{:S(2)}, u32[]{:S(2)}) collective-permute-start(bf16[128,1024]{1,0:T(8,128)(2,1)S(1)} %collective-permute-done.1.refs_5_), channel_id=1, source_target_pairs={{0,32},{8,40},{16,496},{24,504},{32,64},{40,72},{48,16},{56,24},{6... | collective-permute-start | bytes 786440 | tf_op jit(solution)/shard_map/ppermute | solution.py:405
  24.3 2.2 %all-gather.1.refs_2_ = s32[2,6,16]{2,1,0:T(8,128)S(1)} all-gather(s32[1,6,16]{2,1,0:T(8,128)} %bitcast.11), channel_id=2, replica_groups=mesh['chip'=64,'core'=2,'cen'=4] {'core'}, dimensions={0}, use_global_device_ids=true | all-gather | bytes 1152 | tf_op jit(solution)/shard_map/all_gather | solution.py:430
  26.5 3.8 %shard_map.67 = (bf16[256,3072]{1,0:T(8,128)(2,1)S(1)}, f32[24,128]{1,0:T(8,128)S(1)}, f32[24,128]{1,0:T(8,128)S(1)}, bf16[1536,1024]{1,0:T(8,128)(2,1)S(1)}) custom-call(s32[1]{0:T(128)} %bitcast.1.refs_0_, s32[1]{0:T(128)} %bitcast.refs_1_.refs_0_, s32[2,6,16]{2,1,0:T(8,128)S(1)} %all-gather.1.refs_2_, bf16[1536,1024]{1,0:T(8,128)(2,1)} %refs_3_.1, ...), custom_call_target="tpu_custom_call" | custom-call | flops 1610612736 | bytes 7864320 | tf_op jit(solution)/shard_map/pallas_call | solution.py:197
  30.3 3.0 %collective-permute-done.3.refs_6_ = bf16[128,1024]{1,0:T(8,128)(2,1)} collective-permute-done((bf16[128,1024]{1,0:T(8,128)(2,1)}, bf16[128,1024]{1,0:T(8,128)(2,1)}, u32[]{:S(2)}, u32[]{:S(2)}) %collective-permute-start.3) | collective-permute-done | bytes 262176 | tf_op jit(solution)/shard_map/ppermute | solution.py:405
  33.3 4.6 %shard_map.68 = (bf16[384,3072]{1,0:T(8,128)(2,1)S(1)}, f32[24,128]{1,0:T(8,128)S(1)}, f32[8,32,128]{2,1,0:T(8,128)S(1)}) custom-call(s32[1]{0:T(128)} %bitcast.1.refs_0_, s32[1]{0:T(128)} %bitcast.refs_1_.refs_0_, s32[2,6,16]{2,1,0:T(8,128)S(1)} %all-gather.1.refs_2_, bf16[1536,1024]{1,0:T(8,128)(2,1)S(1)} %get-tuple-element.20.refs_3_.refs_2_, ...), custom_call_target="tpu_custom_call" | custom-call | flops 2415919104 | bytes 8650752 | tf_op jit(solution)/shard_map/pallas_call | solution.py:197
  37.9 10.9 %all_to_all.5.refs_1_ = f32[8,32,128]{2,1,0:T(8,128)S(1)} all-to-all(f32[8,32,128]{2,1,0:T(8,128)S(1)} %get-tuple-element.23), channel_id=1, replica_groups=mesh['chip'=64,'core'=2,'cen'=4] {'core','cen'}, dimensions={0} | all-to-all | bytes 262144 | tf_op jit(solution)/shard_map/all_to_all | solution.py:454
  48.7 1.6 %shard_map.71 = (bf16[1040,128]{1,0:T(8,128)(2,1)S(1)}, f32[12,128]{1,0:T(8,128)}) custom-call(s32[1]{0:T(128)} %bitcast.refs_1_.refs_0_, f32[8,32,128]{2,1,0:T(8,128)S(1)} %all_to_all.5.refs_1_, bf16[1536,1024]{1,0:T(8,128)(2,1)S(1)} %get-tuple-element.20.refs_3_.refs_2_, bf16[1536,1024]{1,0:T(8,128)(2,1)S(1)} %collective-permute-done.refs_4_.refs_3_, ...), custom_call_target="tpu_custom_call" | custom-call | flops 805306368 | bytes 7077888 | tf_op jit(solution)/shard_map/pallas_call | solution.py:339
  50.4 2.7 %collective-permute-start.7 = (bf16[1040,128]{1,0:T(8,128)(2,1)S(1)}, bf16[1040,128]{1,0:T(8,128)(2,1)S(1)}, u32[]{:S(2)}, u32[]{:S(2)}) collective-permute-start(bf16[1040,128]{1,0:T(8,128)(2,1)S(1)} %get-tuple-element.33), channel_id=1, source_target_pairs={{0,480},{8,488},{16,48},{24,56},{32,0},{40,8},{48,80},{56,88},{64,... | collective-permute-start | bytes 798728 | tf_op jit(solution)/shard_map/ppermute | solution.py:405
  53.1 2.9 %shard_map.70 = (bf16[1040,128]{1,0:T(8,128)(2,1)S(1)}, bf16[1040,128]{1,0:T(8,128)(2,1)S(1)}, f32[128,1024]{1,0:T(8,128)S(1)}, f32[8,128]{1,0:T(8,128)S(1)}) custom-call(s32[1]{0:T(128)} %bitcast.refs_1_.refs_0_, f32[8,32,128]{2,1,0:T(8,128)S(1)} %all_to_all.5.refs_1_, bf16[1536,1024]{1,0:T(8,128)(2,1)S(1)} %get-tuple-element.20.refs_3_.refs_2_, ...), custom_call_target="tpu_custom_call" | custom-call | flops 2415919104 | bytes 8650752 | tf_op jit(solution)/shard_map/pallas_call | solution.py:339
  56.0 3.2 %collective-permute-start.5 = (bf16[1040,128]{1,0:T(8,128)(2,1)S(1)}, bf16[1040,128]{1,0:T(8,128)(2,1)S(1)}, u32[]{:S(2)}, u32[]{:S(2)}) collective-permute-start(bf16[1040,128]{1,0:T(8,128)(2,1)S(1)} %get-tuple-element.29), channel_id=1, source_target_pairs={{0,8},{8,16},{16,24},{24,32},{32,40},{40,48},{48,56},{56,64},{64,7... | collective-permute-start | bytes 798728 | tf_op jit(solution)/shard_map/ppermute | solution.py:405
  59.2 5.4 %collective-permute-start.6 = (bf16[1040,128]{1,0:T(8,128)(2,1)S(1)}, bf16[1040,128]{1,0:T(8,128)(2,1)S(1)}, u32[]{:S(2)}, u32[]{:S(2)}) collective-permute-start(bf16[1040,128]{1,0:T(8,128)(2,1)S(1)} %get-tuple-element.30), channel_id=1, source_target_pairs={{0,504},{8,0},{16,8},{24,16},{32,24},{40,32},{48,40},{56,48},{64,5... | collective-permute-start | bytes 798728 | tf_op jit(solution)/shard_map/ppermute | solution.py:405
  64.6 0.1 shard_map.72
  64.7 0.0 copy-start
  64.7 2.1 %collective-permute-start.8 = (bf16[1040,128]{1,0:T(8,128)(2,1)S(1)}, bf16[1040,128]{1,0:T(8,128)(2,1)S(1)}, u32[]{:S(2)}, u32[]{:S(2)}) collective-permute-start(bf16[1040,128]{1,0:T(8,128)(2,1)S(1)} %shard_map.72), channel_id=1, source_target_pairs={{0,16},{8,24},{16,0},{24,8},{32,48},{40,56},{48,32},{56,40},{64,80... | collective-permute-start | bytes 798728 | tf_op jit(solution)/shard_map/ppermute | solution.py:405
  66.8 1.1 %shard_map.69 = (f32[128,1024]{1,0:T(8,128)S(1)}, f32[8,128]{1,0:T(8,128)S(1)}) custom-call(s32[1]{0:T(128)} %bitcast.refs_1_.refs_0_, f32[8,32,128]{2,1,0:T(8,128)S(1)} %all_to_all.5.refs_1_, bf16[1536,1024]{1,0:T(8,128)(2,1)S(1)} %get-tuple-element.20.refs_3_.refs_2_, bf16[1536,1024]{1,0:T(8,128)(2,1)S(1)} %collective-permute-done.refs_4_.refs_3_, ...), custom_call_target="tpu_custom_call" | custom-call | flops 805306368 | bytes 7077888 | tf_op jit(solution)/shard_map/pallas_call | solution.py:339
  67.9 0.9 %collective-permute-done.5.refs_3_ = bf16[1040,128]{1,0:T(8,128)(2,1)S(1)} collective-permute-done((bf16[1040,128]{1,0:T(8,128)(2,1)S(1)}, bf16[1040,128]{1,0:T(8,128)(2,1)S(1)}, u32[]{:S(2)}, u32[]{:S(2)}) %collective-permute-start.5) | collective-permute-done | bytes 266272 | tf_op jit(solution)/shard_map/ppermute | solution.py:405
  68.8 1.0 %collective-permute-done.6.refs_4_ = bf16[1040,128]{1,0:T(8,128)(2,1)S(1)} collective-permute-done((bf16[1040,128]{1,0:T(8,128)(2,1)S(1)}, bf16[1040,128]{1,0:T(8,128)(2,1)S(1)}, u32[]{:S(2)}, u32[]{:S(2)}) %collective-permute-start.6) | collective-permute-done | bytes 266272 | tf_op jit(solution)/shard_map/ppermute | solution.py:405
  69.7 5.2 %collective-permute-done.8.refs_5_ = bf16[1040,128]{1,0:T(8,128)(2,1)S(1)} collective-permute-done((bf16[1040,128]{1,0:T(8,128)(2,1)S(1)}, bf16[1040,128]{1,0:T(8,128)(2,1)S(1)}, u32[]{:S(2)}, u32[]{:S(2)}) %collective-permute-start.8) | collective-permute-done | bytes 266272 | tf_op jit(solution)/shard_map/ppermute | solution.py:405
  74.9 0.9 %shard_map.73 = (bf16[128,1024]{1,0:T(8,128)(2,1)}, f32[2,64]{1,0:T(2,128)}) custom-call(f32[128,1024]{1,0:T(8,128)S(1)} %get-tuple-element.27.refs_0_, f32[8,128]{1,0:T(8,128)S(1)} %get-tuple-element.28.refs_1_, bf16[128,1024]{1,0:T(8,128)(2,1)S(1)} %bitcast.10, bf16[1040,128]{1,0:T(8,128)(2,1)S(1)} %collective-permute-done.5.refs_3_, ...), custom_call_target="tpu_custom_call" | custom-call | tf_op jit(solution)/shard_map/pallas_call | solution.py:384
  (7 shorter events, 0.0 us)
Async XLA Ops:
  0.6 25.9 %collective-permute-start = (bf16[1536,1024]{1,0:T(8,128)(2,1)}, bf16[1536,1024]{1,0:T(8,128)(2,1)S(1)}, u32[]{:S(2)}, u32[]{:S(2)}) collective-permute-start(bf16[1536,1024]{1,0:T(8,128)(2,1)} %refs_3_.1), channel_id=1, source_target_pairs={{0,4},{4,0},{1,5},{5,1},{2,6},{6,2},{3,7},{7,3},{8,12},{12,8},{9,1... | collective-permute-start | bytes 9437192 | tf_op jit(solution)/shard_map/ppermute | solution.py:423
  9.4 12.9 %collective-permute-start.1 = (bf16[128,1024]{1,0:T(8,128)(2,1)}, bf16[128,1024]{1,0:T(8,128)(2,1)S(1)}, u32[]{:S(2)}, u32[]{:S(2)}) collective-permute-start(bf16[128,1024]{1,0:T(8,128)(2,1)} %bitcast.6), channel_id=1, source_target_pairs={{0,16},{8,24},{16,0},{24,8},{32,48},{40,56},{48,32},{56,40},{64,80... | collective-permute-start | bytes 786440 | tf_op jit(solution)/shard_map/ppermute | solution.py:405
  11.4 18.9 %collective-permute-start.2 = (bf16[128,1024]{1,0:T(8,128)(2,1)}, bf16[128,1024]{1,0:T(8,128)(2,1)}, u32[]{:S(2)}, u32[]{:S(2)}) collective-permute-start(bf16[128,1024]{1,0:T(8,128)(2,1)} %bitcast.7), channel_id=1, source_target_pairs={{0,504},{8,0},{16,8},{24,16},{32,24},{40,32},{48,40},{56,48},{64,5... | collective-permute-start | bytes 786440 | tf_op jit(solution)/shard_map/ppermute | solution.py:405
  20.4 12.8 %collective-permute-start.3 = (bf16[128,1024]{1,0:T(8,128)(2,1)}, bf16[128,1024]{1,0:T(8,128)(2,1)}, u32[]{:S(2)}, u32[]{:S(2)}) collective-permute-start(bf16[128,1024]{1,0:T(8,128)(2,1)} %bitcast.8), channel_id=1, source_target_pairs={{0,8},{8,16},{16,24},{24,32},{32,40},{40,48},{48,56},{56,64},{64,7... | collective-permute-start | bytes 786440 | tf_op jit(solution)/shard_map/ppermute | solution.py:405
  22.4 10.9 %collective-permute-start.4 = (bf16[128,1024]{1,0:T(8,128)(2,1)S(1)}, bf16[128,1024]{1,0:T(8,128)(2,1)}, u32[]{:S(2)}, u32[]{:S(2)}) collective-permute-start(bf16[128,1024]{1,0:T(8,128)(2,1)S(1)} %collective-permute-done.1.refs_5_), channel_id=1, source_target_pairs={{0,32},{8,40},{16,496},{24,504},{32,64},{40,72},{48,16},{56,24},{6... | collective-permute-start | bytes 786440 | tf_op jit(solution)/shard_map/ppermute | solution.py:405
  26.5 6.7 %copy-start.1 = (s32[6]{0:T(128)S(1)}, s32[6]{0:T(128)}, u32[]{:S(2)}) copy-start(s32[6]{0:T(128)} %refs_10_.1) | copy-start | bytes 76
  50.4 14.3 %collective-permute-start.7 = (bf16[1040,128]{1,0:T(8,128)(2,1)S(1)}, bf16[1040,128]{1,0:T(8,128)(2,1)S(1)}, u32[]{:S(2)}, u32[]{:S(2)}) collective-permute-start(bf16[1040,128]{1,0:T(8,128)(2,1)S(1)} %get-tuple-element.33), channel_id=1, source_target_pairs={{0,480},{8,488},{16,48},{24,56},{32,0},{40,8},{48,80},{56,88},{64,... | collective-permute-start | bytes 798728 | tf_op jit(solution)/shard_map/ppermute | solution.py:405
  56.0 12.8 %collective-permute-start.5 = (bf16[1040,128]{1,0:T(8,128)(2,1)S(1)}, bf16[1040,128]{1,0:T(8,128)(2,1)S(1)}, u32[]{:S(2)}, u32[]{:S(2)}) collective-permute-start(bf16[1040,128]{1,0:T(8,128)(2,1)S(1)} %get-tuple-element.29), channel_id=1, source_target_pairs={{0,8},{8,16},{16,24},{24,32},{32,40},{40,48},{48,56},{56,64},{64,7... | collective-permute-start | bytes 798728 | tf_op jit(solution)/shard_map/ppermute | solution.py:405
  59.2 10.5 %collective-permute-start.6 = (bf16[1040,128]{1,0:T(8,128)(2,1)S(1)}, bf16[1040,128]{1,0:T(8,128)(2,1)S(1)}, u32[]{:S(2)}, u32[]{:S(2)}) collective-permute-start(bf16[1040,128]{1,0:T(8,128)(2,1)S(1)} %get-tuple-element.30), channel_id=1, source_target_pairs={{0,504},{8,0},{16,8},{24,16},{32,24},{40,32},{48,40},{56,48},{64,5... | collective-permute-start | bytes 798728 | tf_op jit(solution)/shard_map/ppermute | solution.py:405
  64.7 10.2 %copy-start = (bf16[2,64,1024]{2,1,0:T(8,128)(2,1)S(1)}, bf16[2,64,1024]{2,1,0:T(8,128)(2,1)}, u32[]{:S(2)}) copy-start(bf16[2,64,1024]{2,1,0:T(8,128)(2,1)} %param.7) | copy-start | bytes 786436
  64.7 10.2 %collective-permute-start.8 = (bf16[1040,128]{1,0:T(8,128)(2,1)S(1)}, bf16[1040,128]{1,0:T(8,128)(2,1)S(1)}, u32[]{:S(2)}, u32[]{:S(2)}) collective-permute-start(bf16[1040,128]{1,0:T(8,128)(2,1)S(1)} %shard_map.72), channel_id=1, source_target_pairs={{0,16},{8,24},{16,0},{24,8},{32,48},{40,56},{48,32},{56,40},{64,80... | collective-permute-start | bytes 798728 | tf_op jit(solution)/shard_map/ppermute | solution.py:405

commit v6 on v5

--- a/solution.py
+++ b/solution.py
@@ -424,7 +424,7 @@
 
     centre = centroids.reshape(size, D)
     row = moved(centre, across)
-    near = [moved(centre, back), moved(centre, ahead)]
+    near = [moved(centre, ahead), moved(centre, back)]
     beyond = moved(row, outward)
     other = swapped(points)
     candidates = lax.all_gather(candidates, "core")
@@ -441,7 +441,7 @@
     )
     points = [kept, other]
     last_power, last_max, message = score(
-        ("after", "before", "beyond"),
+        ("before", "after", "beyond"),
         chips,
         chip,
         core,
@@ -457,7 +457,7 @@
         core, everyone, points, tops, powers, ((1, 2 * size),), size, (0,), None, True
     )
     beyond = moved(beyond, inward)
-    after, before, row, row_mass = moments(
+    before, after, row, row_mass = moments(
         core, everyone, points, tops, powers, ((1, 0), (1, size), (0, 0)), size, (0, 1), 2, False
     )
     arrived = [moved(after, ahead), moved(before, back)]

time: 76.8 us -> 76.9 us (level)
  no operation moved by 1% of the time
where the time goes in v6:
time: 76.9 us; the launch traced here: 76.4 us
  starting transfers between devices  37.6 us (49%)
  Pallas kernels  15 us (20%)
  blocking collectives  13.2 us (17%)
  waiting for transfers between devices  9.73 us (13%)
  between operations  0.78 us (1%)
    ppermute x8, starting transfers between devices, moved(): lax.ppermute(value, 'chip', [(c, step(c) % chips) for c in range(chips)])  28.8 us
    all_to_all x1, blocking collectives, local(): everyone = lax.all_to_all(message, ('core', 'cen'), 0, 0)  11 us
    ppermute x8, waiting for transfers between devices, moved(): lax.ppermute(value, 'chip', [(c, step(c) % chips) for c in range(chips)])  9.73 us
    ppermute x1, starting transfers between devices, swapped(): return lax.ppermute(value, 'core', [(0, 1), (1, 0)])  8.79 us
    pallas_call x2, Pallas kernels, score(): pl.pallas_call(kernel, in_specs=in_specs, out_specs=[VMEM] * len(out_shap...  8.39 us
    pallas_call x3, Pallas kernels, moments(): pl.pallas_call(kernel, in_specs=[SMEM] + [VMEM] * 7, out_specs=[VMEM] * l...  5.65 us
    all_gather x1, blocking collectives, local(): candidates = lax.all_gather(candidates, 'core')  2.2 us
  transfers between devices with their start and end apart: 9, of which 4 were waited for; matrix products, arithmetic and copies ran while one was open for 0% of the time, Pallas kernels for 10%

profile of v6, /device:TPU:1, one launch (start us, length us, event | category | flops | bytes accessed | tf_op | source)
XLA Modules:
  0.0 76.4 jit_solution(12611939369289922537)
XLA Ops:
  0.6 8.8 %collective-permute-start = (bf16[1536,1024]{1,0:T(8,128)(2,1)}, bf16[1536,1024]{1,0:T(8,128)(2,1)S(1)}, u32[]{:S(2)}, u32[]{:S(2)}) collective-permute-start(bf16[1536,1024]{1,0:T(8,128)(2,1)} %refs_3_.1), channel_id=1, source_target_pairs={{0,4},{4,0},{1,5},{5,1},{2,6},{6,2},{3,7},{7,3},{8,12},{12,8},{9,1... | collective-permute-start | bytes 9437192 | tf_op jit(solution)/shard_map/ppermute | solution.py:423
  9.4 1.9 %collective-permute-start.1 = (bf16[128,1024]{1,0:T(8,128)(2,1)}, bf16[128,1024]{1,0:T(8,128)(2,1)S(1)}, u32[]{:S(2)}, u32[]{:S(2)}) collective-permute-start(bf16[128,1024]{1,0:T(8,128)(2,1)} %bitcast.6), channel_id=1, source_target_pairs={{0,16},{8,24},{16,0},{24,8},{32,48},{40,56},{48,32},{56,40},{64,80... | collective-permute-start | bytes 786440 | tf_op jit(solution)/shard_map/ppermute | solution.py:405
  11.4 1.9 %collective-permute-start.2 = (bf16[128,1024]{1,0:T(8,128)(2,1)}, bf16[128,1024]{1,0:T(8,128)(2,1)}, u32[]{:S(2)}, u32[]{:S(2)}) collective-permute-start(bf16[128,1024]{1,0:T(8,128)(2,1)} %bitcast.7), channel_id=1, source_target_pairs={{0,8},{8,16},{16,24},{24,32},{32,40},{40,48},{48,56},{56,64},{64,7... | collective-permute-start | bytes 786440 | tf_op jit(solution)/shard_map/ppermute | solution.py:405
  13.3 9.1 %collective-permute-start.3 = (bf16[128,1024]{1,0:T(8,128)(2,1)}, bf16[128,1024]{1,0:T(8,128)(2,1)}, u32[]{:S(2)}, u32[]{:S(2)}) collective-permute-start(bf16[128,1024]{1,0:T(8,128)(2,1)} %bitcast.8), channel_id=1, source_target_pairs={{0,504},{8,0},{16,8},{24,16},{32,24},{40,32},{48,40},{56,48},{64,5... | collective-permute-start | bytes 786440 | tf_op jit(solution)/shard_map/ppermute | solution.py:405
  22.4 0.0 collective-permute-done.1.refs_5_
  22.4 1.9 %collective-permute-start.4 = (bf16[128,1024]{1,0:T(8,128)(2,1)S(1)}, bf16[128,1024]{1,0:T(8,128)(2,1)}, u32[]{:S(2)}, u32[]{:S(2)}) collective-permute-start(bf16[128,1024]{1,0:T(8,128)(2,1)S(1)} %collective-permute-done.1.refs_5_), channel_id=1, source_target_pairs={{0,32},{8,40},{16,496},{24,504},{32,64},{40,72},{48,16},{56,24},{6... | collective-permute-start | bytes 786440 | tf_op jit(solution)/shard_map/ppermute | solution.py:405
  24.3 2.2 %all-gather.1.refs_2_ = s32[2,6,16]{2,1,0:T(8,128)S(1)} all-gather(s32[1,6,16]{2,1,0:T(8,128)} %bitcast.11), channel_id=2, replica_groups=mesh['chip'=64,'core'=2,'cen'=4] {'core'}, dimensions={0}, use_global_device_ids=true | all-gather | bytes 1152 | tf_op jit(solution)/shard_map/all_gather | solution.py:430
  26.5 3.8 %shard_map.67 = (bf16[256,3072]{1,0:T(8,128)(2,1)S(1)}, f32[24,128]{1,0:T(8,128)S(1)}, f32[24,128]{1,0:T(8,128)S(1)}, bf16[1536,1024]{1,0:T(8,128)(2,1)S(1)}) custom-call(s32[1]{0:T(128)} %bitcast.1.refs_0_, s32[1]{0:T(128)} %bitcast.refs_1_.refs_0_, s32[2,6,16]{2,1,0:T(8,128)S(1)} %all-gather.1.refs_2_, bf16[1536,1024]{1,0:T(8,128)(2,1)} %refs_3_.1, ...), custom_call_target="tpu_custom_call" | custom-call | flops 1610612736 | bytes 7864320 | tf_op jit(solution)/shard_map/pallas_call | solution.py:197
  30.3 2.7 %collective-permute-done.4.refs_7_ = bf16[128,1024]{1,0:T(8,128)(2,1)} collective-permute-done((bf16[128,1024]{1,0:T(8,128)(2,1)S(1)}, bf16[128,1024]{1,0:T(8,128)(2,1)}, u32[]{:S(2)}, u32[]{:S(2)}) %collective-permute-start.4) | collective-permute-done | bytes 262176 | tf_op jit(solution)/shard_map/ppermute | solution.py:405
  33.0 4.6 %shard_map.68 = (bf16[384,3072]{1,0:T(8,128)(2,1)S(1)}, f32[24,128]{1,0:T(8,128)S(1)}, f32[8,32,128]{2,1,0:T(8,128)S(1)}) custom-call(s32[1]{0:T(128)} %bitcast.1.refs_0_, s32[1]{0:T(128)} %bitcast.refs_1_.refs_0_, s32[2,6,16]{2,1,0:T(8,128)S(1)} %all-gather.1.refs_2_, bf16[1536,1024]{1,0:T(8,128)(2,1)S(1)} %get-tuple-element.20.refs_3_.refs_2_, ...), custom_call_target="tpu_custom_call" | custom-call | flops 2415919104 | bytes 8650752 | tf_op jit(solution)/shard_map/pallas_call | solution.py:197
  37.7 11.0 %all_to_all.5.refs_1_ = f32[8,32,128]{2,1,0:T(8,128)S(1)} all-to-all(f32[8,32,128]{2,1,0:T(8,128)S(1)} %get-tuple-element.23), channel_id=1, replica_groups=mesh['chip'=64,'core'=2,'cen'=4] {'core','cen'}, dimensions={0} | all-to-all | bytes 262144 | tf_op jit(solution)/shard_map/all_to_all | solution.py:454
  48.7 1.6 %shard_map.71 = (bf16[1040,128]{1,0:T(8,128)(2,1)S(1)}, f32[12,128]{1,0:T(8,128)}) custom-call(s32[1]{0:T(128)} %bitcast.refs_1_.refs_0_, f32[8,32,128]{2,1,0:T(8,128)S(1)} %all_to_all.5.refs_1_, bf16[1536,1024]{1,0:T(8,128)(2,1)S(1)} %get-tuple-element.20.refs_3_.refs_2_, bf16[1536,1024]{1,0:T(8,128)(2,1)S(1)} %collective-permute-done.refs_4_.refs_3_, ...), custom_call_target="tpu_custom_call" | custom-call | flops 805306368 | bytes 7077888 | tf_op jit(solution)/shard_map/pallas_call | solution.py:339
  50.3 3.4 %collective-permute-start.7 = (bf16[1040,128]{1,0:T(8,128)(2,1)S(1)}, bf16[1040,128]{1,0:T(8,128)(2,1)S(1)}, u32[]{:S(2)}, u32[]{:S(2)}) collective-permute-start(bf16[1040,128]{1,0:T(8,128)(2,1)S(1)} %get-tuple-element.33), channel_id=1, source_target_pairs={{0,480},{8,488},{16,48},{24,56},{32,0},{40,8},{48,80},{56,88},{64,... | collective-permute-start | bytes 798728 | tf_op jit(solution)/shard_map/ppermute | solution.py:405
  53.6 2.9 %shard_map.70 = (bf16[1040,128]{1,0:T(8,128)(2,1)S(1)}, bf16[1040,128]{1,0:T(8,128)(2,1)S(1)}, f32[128,1024]{1,0:T(8,128)S(1)}, f32[8,128]{1,0:T(8,128)S(1)}) custom-call(s32[1]{0:T(128)} %bitcast.refs_1_.refs_0_, f32[8,32,128]{2,1,0:T(8,128)S(1)} %all_to_all.5.refs_1_, bf16[1536,1024]{1,0:T(8,128)(2,1)S(1)} %get-tuple-element.20.refs_3_.refs_2_, ...), custom_call_target="tpu_custom_call" | custom-call | flops 2415919104 | bytes 8650752 | tf_op jit(solution)/shard_map/pallas_call | solution.py:339
  56.6 2.6 %collective-permute-start.5 = (bf16[1040,128]{1,0:T(8,128)(2,1)S(1)}, bf16[1040,128]{1,0:T(8,128)(2,1)S(1)}, u32[]{:S(2)}, u32[]{:S(2)}) collective-permute-start(bf16[1040,128]{1,0:T(8,128)(2,1)S(1)} %get-tuple-element.29), channel_id=1, source_target_pairs={{0,8},{8,16},{16,24},{24,32},{32,40},{40,48},{48,56},{56,64},{64,7... | collective-permute-start | bytes 798728 | tf_op jit(solution)/shard_map/ppermute | solution.py:405
  59.1 6.0 %collective-permute-start.6 = (bf16[1040,128]{1,0:T(8,128)(2,1)S(1)}, bf16[1040,128]{1,0:T(8,128)(2,1)S(1)}, u32[]{:S(2)}, u32[]{:S(2)}) collective-permute-start(bf16[1040,128]{1,0:T(8,128)(2,1)S(1)} %get-tuple-element.30), channel_id=1, source_target_pairs={{0,504},{8,0},{16,8},{24,16},{32,24},{40,32},{48,40},{56,48},{64,5... | collective-permute-start | bytes 798728 | tf_op jit(solution)/shard_map/ppermute | solution.py:405
  65.2 0.1 shard_map.72
  65.3 0.0 copy-start
  65.3 2.1 %collective-permute-start.8 = (bf16[1040,128]{1,0:T(8,128)(2,1)S(1)}, bf16[1040,128]{1,0:T(8,128)(2,1)S(1)}, u32[]{:S(2)}, u32[]{:S(2)}) collective-permute-start(bf16[1040,128]{1,0:T(8,128)(2,1)S(1)} %shard_map.72), channel_id=1, source_target_pairs={{0,16},{8,24},{16,0},{24,8},{32,48},{40,56},{48,32},{56,40},{64,80... | collective-permute-start | bytes 798728 | tf_op jit(solution)/shard_map/ppermute | solution.py:405
  67.4 1.1 %shard_map.69 = (f32[128,1024]{1,0:T(8,128)S(1)}, f32[8,128]{1,0:T(8,128)S(1)}) custom-call(s32[1]{0:T(128)} %bitcast.refs_1_.refs_0_, f32[8,32,128]{2,1,0:T(8,128)S(1)} %all_to_all.5.refs_1_, bf16[1536,1024]{1,0:T(8,128)(2,1)S(1)} %get-tuple-element.20.refs_3_.refs_2_, bf16[1536,1024]{1,0:T(8,128)(2,1)S(1)} %collective-permute-done.refs_4_.refs_3_, ...), custom_call_target="tpu_custom_call" | custom-call | flops 805306368 | bytes 7077888 | tf_op jit(solution)/shard_map/pallas_call | solution.py:339
  68.5 0.6 collective-permute-done.5.refs_3_
  69.1 1.6 %collective-permute-done.6.refs_4_ = bf16[1040,128]{1,0:T(8,128)(2,1)S(1)} collective-permute-done((bf16[1040,128]{1,0:T(8,128)(2,1)S(1)}, bf16[1040,128]{1,0:T(8,128)(2,1)S(1)}, u32[]{:S(2)}, u32[]{:S(2)}) %collective-permute-start.6) | collective-permute-done | bytes 266272 | tf_op jit(solution)/shard_map/ppermute | solution.py:405
  70.7 4.8 %collective-permute-done.8.refs_5_ = bf16[1040,128]{1,0:T(8,128)(2,1)S(1)} collective-permute-done((bf16[1040,128]{1,0:T(8,128)(2,1)S(1)}, bf16[1040,128]{1,0:T(8,128)(2,1)S(1)}, u32[]{:S(2)}, u32[]{:S(2)}) %collective-permute-start.8) | collective-permute-done | bytes 266272 | tf_op jit(solution)/shard_map/ppermute | solution.py:405
  75.5 0.9 %shard_map.73 = (bf16[128,1024]{1,0:T(8,128)(2,1)}, f32[2,64]{1,0:T(2,128)}) custom-call(f32[128,1024]{1,0:T(8,128)S(1)} %get-tuple-element.27.refs_0_, f32[8,128]{1,0:T(8,128)S(1)} %get-tuple-element.28.refs_1_, bf16[128,1024]{1,0:T(8,128)(2,1)S(1)} %bitcast.10, bf16[1040,128]{1,0:T(8,128)(2,1)S(1)} %collective-permute-done.5.refs_3_, ...), custom_call_target="tpu_custom_call" | custom-call | tf_op jit(solution)/shard_map/pallas_call | solution.py:384
  (7 shorter events, 0.0 us)
Async XLA Ops:
  0.6 25.9 %collective-permute-start = (bf16[1536,1024]{1,0:T(8,128)(2,1)}, bf16[1536,1024]{1,0:T(8,128)(2,1)S(1)}, u32[]{:S(2)}, u32[]{:S(2)}) collective-permute-start(bf16[1536,1024]{1,0:T(8,128)(2,1)} %refs_3_.1), channel_id=1, source_target_pairs={{0,4},{4,0},{1,5},{5,1},{2,6},{6,2},{3,7},{7,3},{8,12},{12,8},{9,1... | collective-permute-start | bytes 9437192 | tf_op jit(solution)/shard_map/ppermute | solution.py:423
  9.4 12.9 %collective-permute-start.1 = (bf16[128,1024]{1,0:T(8,128)(2,1)}, bf16[128,1024]{1,0:T(8,128)(2,1)S(1)}, u32[]{:S(2)}, u32[]{:S(2)}) collective-permute-start(bf16[128,1024]{1,0:T(8,128)(2,1)} %bitcast.6), channel_id=1, source_target_pairs={{0,16},{8,24},{16,0},{24,8},{32,48},{40,56},{48,32},{56,40},{64,80... | collective-permute-start | bytes 786440 | tf_op jit(solution)/shard_map/ppermute | solution.py:405
  11.4 18.9 %collective-permute-start.2 = (bf16[128,1024]{1,0:T(8,128)(2,1)}, bf16[128,1024]{1,0:T(8,128)(2,1)}, u32[]{:S(2)}, u32[]{:S(2)}) collective-permute-start(bf16[128,1024]{1,0:T(8,128)(2,1)} %bitcast.7), channel_id=1, source_target_pairs={{0,8},{8,16},{16,24},{24,32},{32,40},{40,48},{48,56},{56,64},{64,7... | collective-permute-start | bytes 786440 | tf_op jit(solution)/shard_map/ppermute | solution.py:405
  13.3 17.0 %collective-permute-start.3 = (bf16[128,1024]{1,0:T(8,128)(2,1)}, bf16[128,1024]{1,0:T(8,128)(2,1)}, u32[]{:S(2)}, u32[]{:S(2)}) collective-permute-start(bf16[128,1024]{1,0:T(8,128)(2,1)} %bitcast.8), channel_id=1, source_target_pairs={{0,504},{8,0},{16,8},{24,16},{32,24},{40,32},{48,40},{56,48},{64,5... | collective-permute-start | bytes 786440 | tf_op jit(solution)/shard_map/ppermute | solution.py:405
  22.4 10.7 %collective-permute-start.4 = (bf16[128,1024]{1,0:T(8,128)(2,1)S(1)}, bf16[128,1024]{1,0:T(8,128)(2,1)}, u32[]{:S(2)}, u32[]{:S(2)}) collective-permute-start(bf16[128,1024]{1,0:T(8,128)(2,1)S(1)} %collective-permute-done.1.refs_5_), channel_id=1, source_target_pairs={{0,32},{8,40},{16,496},{24,504},{32,64},{40,72},{48,16},{56,24},{6... | collective-permute-start | bytes 786440 | tf_op jit(solution)/shard_map/ppermute | solution.py:405
  26.5 6.5 %copy-start.1 = (s32[6]{0:T(128)S(1)}, s32[6]{0:T(128)}, u32[]{:S(2)}) copy-start(s32[6]{0:T(128)} %refs_10_.1) | copy-start | bytes 76
  50.3 14.9 %collective-permute-start.7 = (bf16[1040,128]{1,0:T(8,128)(2,1)S(1)}, bf16[1040,128]{1,0:T(8,128)(2,1)S(1)}, u32[]{:S(2)}, u32[]{:S(2)}) collective-permute-start(bf16[1040,128]{1,0:T(8,128)(2,1)S(1)} %get-tuple-element.33), channel_id=1, source_target_pairs={{0,480},{8,488},{16,48},{24,56},{32,0},{40,8},{48,80},{56,88},{64,... | collective-permute-start | bytes 798728 | tf_op jit(solution)/shard_map/ppermute | solution.py:405
  56.6 12.5 %collective-permute-start.5 = (bf16[1040,128]{1,0:T(8,128)(2,1)S(1)}, bf16[1040,128]{1,0:T(8,128)(2,1)S(1)}, u32[]{:S(2)}, u32[]{:S(2)}) collective-permute-start(bf16[1040,128]{1,0:T(8,128)(2,1)S(1)} %get-tuple-element.29), channel_id=1, source_target_pairs={{0,8},{8,16},{16,24},{24,32},{32,40},{40,48},{48,56},{56,64},{64,7... | collective-permute-start | bytes 798728 | tf_op jit(solution)/shard_map/ppermute | solution.py:405
  59.1 11.5 %collective-permute-start.6 = (bf16[1040,128]{1,0:T(8,128)(2,1)S(1)}, bf16[1040,128]{1,0:T(8,128)(2,1)S(1)}, u32[]{:S(2)}, u32[]{:S(2)}) collective-permute-start(bf16[1040,128]{1,0:T(8,128)(2,1)S(1)} %get-tuple-element.30), channel_id=1, source_target_pairs={{0,504},{8,0},{16,8},{24,16},{32,24},{40,32},{48,40},{56,48},{64,5... | collective-permute-start | bytes 798728 | tf_op jit(solution)/shard_map/ppermute | solution.py:405
  65.3 10.2 %copy-start = (bf16[2,64,1024]{2,1,0:T(8,128)(2,1)S(1)}, bf16[2,64,1024]{2,1,0:T(8,128)(2,1)}, u32[]{:S(2)}) copy-start(bf16[2,64,1024]{2,1,0:T(8,128)(2,1)} %param.7) | copy-start | bytes 786436
  65.3 10.2 %collective-permute-start.8 = (bf16[1040,128]{1,0:T(8,128)(2,1)S(1)}, bf16[1040,128]{1,0:T(8,128)(2,1)S(1)}, u32[]{:S(2)}, u32[]{:S(2)}) collective-permute-start(bf16[1040,128]{1,0:T(8,128)(2,1)S(1)} %shard_map.72), channel_id=1, source_target_pairs={{0,16},{8,24},{16,0},{24,8},{32,48},{40,56},{48,32},{56,40},{64,80... | collective-permute-start | bytes 798728 | tf_op jit(solution)/shard_map/ppermute | solution.py:405
